TPU v7x, 512 devices: a whole 4x4x16 slice. The times are simulated.
512 devices in a mesh: dp: 4 (over x), seq: 128 (over z, y, core).
Axes of the slice: x: 4, y: 4, z: 16, core: 2. Of those that a mesh axis runs over, the one named last changes fastest.
Arguments:
- spatial_query: bfloat16 [4, 128, 128, 576], P('dp', 'seq'), may hold values from -6 to 6
- spatial_key: bfloat16 [4, 128, 128, 576], P('dp', 'seq'), may hold values from -6 to 6
- spatial_value: bfloat16 [4, 128, 128, 576], P('dp', 'seq'), may hold values from -6 to 6
- temporal_query: bfloat16 [4, 128, 128, 576], P('dp', 'seq'), may hold values from -6 to 6
- temporal_key: bfloat16 [4, 128, 128, 576], P('dp', 'seq'), may hold values from -6 to 6
- temporal_value_in: bfloat16 [4, 128, 128, 576], P('dp', 'seq'), may hold values from -6 to 6
- out_grad: bfloat16 [4, 128, 128, 576], P('dp', 'seq'), may hold values from -6 to 6
- video_ids: int32 [4, 128], P('dp'), may hold values from 0 to 5, never falling along the last dimension, each value on 1 to 51 neighbouring positions
- spatial_query_gain: float32 [72], replicated, may hold values from 0.5 to 2
- spatial_key_gain: float32 [72], replicated, may hold values from 0.5 to 2
- temporal_query_gain: float32 [72], replicated, may hold values from 0.5 to 2
- temporal_key_gain: float32 [72], replicated, may hold values from 0.5 to 2
Outputs:
- temporal_out: bfloat16 [4, 128, 128, 576], P('dp', 'seq')
- grad_spatial_query: bfloat16 [4, 128, 128, 576], P('dp', 'seq')
- grad_spatial_key: bfloat16 [4, 128, 128, 576], P('dp', 'seq')
- grad_spatial_value: bfloat16 [4, 128, 128, 576], P('dp', 'seq')
- grad_temporal_query: bfloat16 [4, 128, 128, 576], P('dp', 'seq')
- grad_temporal_key: bfloat16 [4, 128, 128, 576], P('dp', 'seq')
- grad_temporal_value_in: bfloat16 [4, 128, 128, 576], P('dp', 'seq')
- grad_spatial_query_gain: float32 [72], replicated
- grad_spatial_key_gain: float32 [72], replicated
- grad_temporal_query_gain: float32 [72], replicated
- grad_temporal_key_gain: float32 [72], replicated
Inputs may be any that keep to these rules, and one draw needn't show every extreme that they name: `video_ids`: ids never fall along the frames; each video has 1 to 51 frames.
All inputs are finite; a program needn't handle non-finite values.
Results may differ from a plain program's by a relative error of at most 0.02.
Values may be sent and summed in bfloat16 or wider, within the bound.
No kernel may reach another device: no remote copies, remote signals or barrier semaphores. Data moves between devices by JAX's collectives and lax.ppermute only.
A program may use at most 64 MiB of HBM per device.

v0:
```python
import jax
import jax.numpy as jnp
from jax import lax
from jax.sharding import PartitionSpec as P

HEADS = 8
HEAD_DIM = 72


def normed(values, gain):
    floats = values.astype(jnp.float32)
    square = jnp.mean(floats * floats, axis=-1, keepdims=True)
    return (floats * lax.rsqrt(square + 1e-06) * gain).astype(jnp.bfloat16)


def attend(query, key_in, value, query_gain, key_gain, penalty, score_form, mix_form):
    shape = query.shape
    split = shape[:-1] + (HEADS, HEAD_DIM)
    query_h = normed(query.reshape(split), query_gain)
    key_h = normed(key_in.reshape(split), key_gain)
    value_h = value.reshape(split)
    scores = (
        jnp.einsum(score_form, query_h, key_h, preferred_element_type=jnp.float32)
        * HEAD_DIM ** (-0.5)
        + penalty
    )
    probs = jax.nn.softmax(scores, axis=-1).astype(jnp.bfloat16)
    mixed = jnp.einsum(mix_form, probs, value_h, preferred_element_type=jnp.float32)
    return mixed.astype(jnp.bfloat16).reshape(shape)


def spatial_attend(query, key_in, value, query_gain, key_gain):
    return attend(
        query,
        key_in,
        value,
        query_gain,
        key_gain,
        jnp.float32(0.0),
        "fqhe,fkhe->fhqk",
        "fhqk,fkhe->fqhe",
    )


def shards(
    spatial_query,
    spatial_key,
    spatial_value,
    temporal_query,
    temporal_key,
    temporal_value_in,
    out_grad,
    video_ids,
    spatial_query_gain,
    spatial_key_gain,
    temporal_query_gain,
    temporal_key_gain,
):
    ids = video_ids[0]
    penalty = jnp.where(ids[:, None] == ids[None, :], 0.0, -1000000000.0).astype(jnp.float32)

    def temporal_attend(query, key_in, value, query_gain, key_gain):
        return attend(
            query,
            key_in,
            value,
            query_gain,
            key_gain,
            penalty,
            "qphe,kphe->phqk",
            "phqk,kphe->qphe",
        )

    cotan_pos = None
    spatial_out, spatial_pull = jax.vjp(
        spatial_attend,
        spatial_query[0],
        spatial_key[0],
        spatial_value[0],
        spatial_query_gain,
        spatial_key_gain,
    )
    temporal_value = (
        temporal_value_in[0].astype(jnp.float32) + spatial_out.astype(jnp.float32)
    ).astype(jnp.bfloat16)
    query_pos, key_pos, value_pos = (
        lax.all_to_all(temporal_query[0], "seq", split_axis=1, concat_axis=0, tiled=True),
        lax.all_to_all(temporal_key[0], "seq", split_axis=1, concat_axis=0, tiled=True),
        lax.all_to_all(temporal_value, "seq", split_axis=1, concat_axis=0, tiled=True),
    )
    temporal_pos, temporal_pull = jax.vjp(
        temporal_attend, query_pos, key_pos, value_pos, temporal_query_gain, temporal_key_gain
    )
    temporal_out = None
    temporal_out = lax.all_to_all(temporal_pos, "seq", split_axis=0, concat_axis=1, tiled=True)
    cotan_pos = lax.all_to_all(out_grad[0], "seq", split_axis=1, concat_axis=0, tiled=True)
    grad_query_pos, grad_key_pos, grad_value_pos, grad_tq_gain, grad_tk_gain = temporal_pull(
        cotan_pos
    )
    grad_query, grad_key, grad_value = (
        lax.all_to_all(grad_query_pos, "seq", split_axis=0, concat_axis=1, tiled=True),
        lax.all_to_all(grad_key_pos, "seq", split_axis=0, concat_axis=1, tiled=True),
        lax.all_to_all(grad_value_pos, "seq", split_axis=0, concat_axis=1, tiled=True),
    )
    grad_sq, grad_sk, grad_sv, grad_sq_gain, grad_sk_gain = spatial_pull(grad_value)
    gain_totals = lax.psum((grad_sq_gain, grad_sk_gain, grad_tq_gain, grad_tk_gain), ("dp", "seq"))
    return (
        temporal_out[None],
        grad_sq[None],
        grad_sk[None],
        grad_sv[None],
        grad_query[None],
        grad_key[None],
        grad_value[None],
        gain_totals[0],
        gain_totals[1],
        gain_totals[2],
        gain_totals[3],
    )


def solution(mesh):
    placed = (
        P("dp", "seq", None, None),
        P("dp", "seq", None, None),
        P("dp", "seq", None, None),
        P("dp", "seq", None, None),
        P("dp", "seq", None, None),
        P("dp", "seq", None, None),
        P("dp", "seq", None, None),
        P("dp", None),
        P(),
        P(),
        P(),
        P(),
    )
    return jax.shard_map(
        shards,
        mesh=mesh,
        in_specs=placed,
        out_specs=(
            P("dp", "seq", None, None),
            P("dp", "seq", None, None),
            P("dp", "seq", None, None),
            P("dp", "seq", None, None),
            P("dp", "seq", None, None),
            P("dp", "seq", None, None),
            P("dp", "seq", None, None),
            P(),
            P(),
            P(),
            P(),
        ),
        check_vma=False,
    )
```

profile of v0, /device:TPU:1, one launch (start us, length us, event | category | flops | bytes accessed | tf_op | source)
XLA Modules:
  0.0 336.7 jit_solution(15822238368342739282)
XLA Ops:
  0.7 1.2 copy.63
  2.4 1.6 reduce.26
  4.9 20.7 %all-to-all-start.1 = ((bf16[128,2,288]{2,1,0:T(2,128)(2,1)}), bf16[128,2,288]{2,1,0:T(2,128)(2,1)S(1)}, u32[]{:S(2)}, u32[]{:S(2)}) async-start(bf16[128,2,288]{2,1,0:T(2,128)(2,1)} %reshape.685), calls=%async_computation.1 | async-start | bytes 393216 | tf_op jit(solution)/shard_map/all_to_all | solution.py:87
  29.0 1.7 reduce.25
  33.7 10.0 %all-to-all-done.1 = bf16[128,2,288]{2,1,0:T(2,128)(2,1)S(1)} async-done(((bf16[128,2,288]{2,1,0:T(2,128)(2,1)}), bf16[128,2,288]{2,1,0:T(2,128)(2,1)S(1)}, u32[]{:S(2)}, u32[]{:S(2)}) %all-to-all-start.1) | async-done | bytes 147488 | tf_op jit(solution)/shard_map/all_to_all | solution.py:87
  43.6 8.0 %all-to-all-start.2 = ((bf16[128,2,288]{2,1,0:T(2,128)(2,1)}), bf16[128,2,288]{2,1,0:T(2,128)(2,1)S(1)}, u32[]{:S(2)}, u32[]{:S(2)}) async-start(bf16[128,2,288]{2,1,0:T(2,128)(2,1)} %reshape.687), calls=%async_computation.2 | async-start | bytes 393216 | tf_op jit(solution)/shard_map/all_to_all | solution.py:88
  52.1 1.7 reduce.24
  53.8 0.9 reshape.683
  55.0 1.7 reduce.28
  60.0 9.6 %all-to-all-done.2 = bf16[128,2,288]{2,1,0:T(2,128)(2,1)S(1)} async-done(((bf16[128,2,288]{2,1,0:T(2,128)(2,1)}), bf16[128,2,288]{2,1,0:T(2,128)(2,1)S(1)}, u32[]{:S(2)}, u32[]{:S(2)}) %all-to-all-start.2) | async-done | bytes 147488 | tf_op jit(solution)/shard_map/all_to_all | solution.py:88
  69.6 8.1 %all-to-all-start = ((bf16[128,2,288]{2,1,0:T(2,128)(2,1)}), bf16[128,2,288]{2,1,0:T(2,128)(2,1)S(1)}, u32[]{:S(2)}, u32[]{:S(2)}) async-start(bf16[128,2,288]{2,1,0:T(2,128)(2,1)} %reshape.683), calls=%async_computation | async-start | bytes 393216 | tf_op jit(solution)/shard_map/all_to_all | solution.py:89
  79.0 16.8 %all-to-all-done = bf16[128,2,288]{2,1,0:T(2,128)(2,1)S(1)} async-done(((bf16[128,2,288]{2,1,0:T(2,128)(2,1)}), bf16[128,2,288]{2,1,0:T(2,128)(2,1)S(1)}, u32[]{:S(2)}, u32[]{:S(2)}) %all-to-all-start) | async-done | bytes 147488 | tf_op jit(solution)/shard_map/all_to_all | solution.py:89
  95.7 8.1 %all-to-all-start.4 = ((bf16[128,2,288]{2,1,0:T(2,128)(2,1)}), bf16[128,2,288]{2,1,0:T(2,128)(2,1)S(1)}, u32[]{:S(2)}, u32[]{:S(2)}) async-start(bf16[128,2,288]{2,1,0:T(2,128)(2,1)} %reshape.691), calls=%async_computation.4 | async-start | bytes 393216 | tf_op jit(solution)/shard_map/all_to_all | solution.py:96
  106.5 1.2 fusion.40
  108.3 13.6 %all-to-all-done.4 = bf16[128,2,288]{2,1,0:T(2,128)(2,1)S(1)} async-done(((bf16[128,2,288]{2,1,0:T(2,128)(2,1)}), bf16[128,2,288]{2,1,0:T(2,128)(2,1)S(1)}, u32[]{:S(2)}, u32[]{:S(2)}) %all-to-all-start.4) | async-done | bytes 147488 | tf_op jit(solution)/shard_map/all_to_all | solution.py:96
  123.1 1.5 convolution_convert_fusion.7
  125.7 0.9 reshape.693
  126.6 8.2 %all-to-all-start.5 = ((bf16[128,2,288]{2,1,0:T(2,128)(2,1)}), bf16[128,2,288]{2,1,0:T(2,128)(2,1)S(1)}, u32[]{:S(2)}, u32[]{:S(2)}) async-start(bf16[128,2,288]{2,1,0:T(2,128)(2,1)} %reshape.693), calls=%async_computation.5 | async-start | bytes 393216 | tf_op jit(solution)/shard_map/all_to_all | solution.py:103
  135.4 1.5 multiply_reduce_fusion.1
  138.0 0.9 reshape.697
  138.9 1.5 multiply_reduce_fusion.2
  140.4 12.4 %all-to-all-done.5 = bf16[128,2,288]{2,1,0:T(2,128)(2,1)S(1)} async-done(((bf16[128,2,288]{2,1,0:T(2,128)(2,1)}), bf16[128,2,288]{2,1,0:T(2,128)(2,1)S(1)}, u32[]{:S(2)}, u32[]{:S(2)}) %all-to-all-start.5) | async-done | bytes 147488 | tf_op jit(solution)/shard_map/all_to_all | solution.py:103
  152.8 8.2 %all-to-all-start.7 = ((bf16[128,2,288]{2,1,0:T(2,128)(2,1)}), bf16[128,2,288]{2,1,0:T(2,128)(2,1)S(1)}, u32[]{:S(2)}, u32[]{:S(2)}) async-start(bf16[128,2,288]{2,1,0:T(2,128)(2,1)} %reshape.697), calls=%async_computation.7 | async-start | bytes 393216 | tf_op jit(solution)/shard_map/all_to_all | solution.py:102
  162.9 1.3 convolution_convert_fusion.8
  165.1 0.9 reshape.689
  166.5 12.5 %all-to-all-done.7 = bf16[128,2,288]{2,1,0:T(2,128)(2,1)S(1)} async-done(((bf16[128,2,288]{2,1,0:T(2,128)(2,1)}), bf16[128,2,288]{2,1,0:T(2,128)(2,1)S(1)}, u32[]{:S(2)}, u32[]{:S(2)}) %all-to-all-start.7) | async-done | bytes 147488 | tf_op jit(solution)/shard_map/all_to_all | solution.py:102
  179.0 8.2 %all-to-all-start.6 = ((bf16[128,2,288]{2,1,0:T(2,128)(2,1)}), bf16[128,2,288]{2,1,0:T(2,128)(2,1)S(1)}, u32[]{:S(2)}, u32[]{:S(2)}) async-start(bf16[128,2,288]{2,1,0:T(2,128)(2,1)} %reshape.695), calls=%async_computation.6 | async-start | bytes 393216 | tf_op jit(solution)/shard_map/all_to_all | solution.py:101
  190.8 14.4 %all-to-all-done.6 = bf16[128,2,288]{2,1,0:T(2,128)(2,1)S(1)} async-done(((bf16[128,2,288]{2,1,0:T(2,128)(2,1)}), bf16[128,2,288]{2,1,0:T(2,128)(2,1)S(1)}, u32[]{:S(2)}, u32[]{:S(2)}) %all-to-all-start.6) | async-done | bytes 147488 | tf_op jit(solution)/shard_map/all_to_all | solution.py:101
  205.2 8.1 %all-to-all-start.3 = ((bf16[128,2,288]{2,1,0:T(2,128)(2,1)}), bf16[128,2,288]{2,1,0:T(2,128)(2,1)S(1)}, u32[]{:S(2)}, u32[]{:S(2)}) async-start(bf16[128,2,288]{2,1,0:T(2,128)(2,1)} %reshape.689), calls=%async_computation.3 | async-start | bytes 393216 | tf_op jit(solution)/shard_map/all_to_all | solution.py:95
  215.1 1.2 convolution_convert_fusion.4
  216.4 14.9 %all-to-all-done.3 = bf16[128,2,288]{2,1,0:T(2,128)(2,1)S(1)} async-done(((bf16[128,2,288]{2,1,0:T(2,128)(2,1)}), bf16[128,2,288]{2,1,0:T(2,128)(2,1)S(1)}, u32[]{:S(2)}, u32[]{:S(2)}) %all-to-all-start.3) | async-done | bytes 147488 | tf_op jit(solution)/shard_map/all_to_all | solution.py:95
  234.0 102.7 %all-reduce = (f32[72]{0:T(128)}, f32[72]{0:T(128)}, f32[72]{0:T(128)}, f32[72]{0:T(128)}) all-reduce(f32[72]{0:T(128)S(1)} %get-tuple-element.28, f32[72]{0:T(128)S(1)} %get-tuple-element.26, f32[72]{0:T(128)S(1)} %get-tuple-element.24, f32[72]{0:T(128)S(1)} %get-tuple-element.22), channel_id=1, replica_groups=mesh['dp'=4,'seq'=128] {'dp','seq'}, use_global_device_ids=true, to_apply=%region_15.16 | all-reduce | flops 288 | bytes 2304 | tf_op jit(solution)/shard_map/psum | solution.py:106
  (145 shorter events, 31.3 us)
Async XLA Ops:
  0.6 31.3 %copy-start = (bf16[1,1,128,576]{2,3,1,0:T(8,128)(2,1)S(1)}, bf16[1,1,128,576]{2,3,1,0:T(8,128)(2,1)}, u32[]{:S(2)}) copy-start(bf16[1,1,128,576]{2,3,1,0:T(8,128)(2,1)} %param.14) | copy-start | bytes 442372
  4.9 20.7 %copy-start.2 = (bf16[1,1,128,576]{2,3,1,0:T(8,128)(2,1)S(1)}, bf16[1,1,128,576]{2,3,1,0:T(8,128)(2,1)}, u32[]{:S(2)}) copy-start(bf16[1,1,128,576]{2,3,1,0:T(8,128)(2,1)} %param.12) | copy-start | bytes 442372
  4.9 38.7 %all-to-all-start.1 = ((bf16[128,2,288]{2,1,0:T(2,128)(2,1)}), bf16[128,2,288]{2,1,0:T(2,128)(2,1)S(1)}, u32[]{:S(2)}, u32[]{:S(2)}) async-start(bf16[128,2,288]{2,1,0:T(2,128)(2,1)} %reshape.685), calls=%async_computation.1 | async-start | bytes 393216 | tf_op jit(solution)/shard_map/all_to_all | solution.py:87
  25.6 0.9 copy-start.3
  27.9 0.9 copy-start.4
  28.0 4.0 %copy-start.7 = (bf16[128,8,72]{0,2,1:T(8,128)(2,1)}, bf16[128,8,72]{0,2,1:T(8,128)(2,1)S(1)}, u32[]{:S(2)}) copy-start(bf16[128,8,72]{0,2,1:T(8,128)(2,1)S(1)} %get-tuple-element.47) | copy-start | bytes 442372
  32.0 25.6 %copy-start.25 = (f32[8,128]{1,0:T(8,128)}, f32[8,128]{1,0:T(8,128)S(1)}, u32[]{:S(2)}) copy-start(f32[8,128]{1,0:T(8,128)S(1)} %get-tuple-element.34) | copy-start | bytes 12292
  32.5 0.9 copy-start.5
  43.6 26.0 %all-to-all-start.2 = ((bf16[128,2,288]{2,1,0:T(2,128)(2,1)}), bf16[128,2,288]{2,1,0:T(2,128)(2,1)S(1)}, u32[]{:S(2)}, u32[]{:S(2)}) async-start(bf16[128,2,288]{2,1,0:T(2,128)(2,1)} %reshape.687), calls=%async_computation.2 | async-start | bytes 393216 | tf_op jit(solution)/shard_map/all_to_all | solution.py:88
  53.8 0.9 copy-start.6
  69.6 26.1 %all-to-all-start = ((bf16[128,2,288]{2,1,0:T(2,128)(2,1)}), bf16[128,2,288]{2,1,0:T(2,128)(2,1)S(1)}, u32[]{:S(2)}, u32[]{:S(2)}) async-start(bf16[128,2,288]{2,1,0:T(2,128)(2,1)} %reshape.683), calls=%async_computation | async-start | bytes 393216 | tf_op jit(solution)/shard_map/all_to_all | solution.py:89
  95.7 26.1 %all-to-all-start.4 = ((bf16[128,2,288]{2,1,0:T(2,128)(2,1)}), bf16[128,2,288]{2,1,0:T(2,128)(2,1)S(1)}, u32[]{:S(2)}, u32[]{:S(2)}) async-start(bf16[128,2,288]{2,1,0:T(2,128)(2,1)} %reshape.691), calls=%async_computation.4 | async-start | bytes 393216 | tf_op jit(solution)/shard_map/all_to_all | solution.py:96
  105.5 0.9 copy-start.12
  122.2 0.9 copy-start.10
  122.2 0.9 copy-start.28
  123.1 1.5 copy-start.24
  126.6 8.2 %copy-start.11 = (bf16[128,8,72]{0,2,1:T(8,128)(2,1)S(1)}, bf16[128,8,72]{0,2,1:T(8,128)(2,1)}, u32[]{:S(2)}) copy-start(bf16[128,8,72]{0,2,1:T(8,128)(2,1)} %copy-done.9) | copy-start | bytes 442372
  126.6 8.2 %copy-start.13 = (bf16[128,8,72]{0,2,1:T(8,128)(2,1)S(1)}, bf16[128,8,72]{0,2,1:T(8,128)(2,1)}, u32[]{:S(2)}) copy-start(bf16[128,8,72]{0,2,1:T(8,128)(2,1)} %get-tuple-element.49) | copy-start | bytes 442372
  126.6 8.2 %copy-start.29 = (f32[8,128]{1,0:T(8,128)S(1)}, f32[8,128]{1,0:T(8,128)}, u32[]{:S(2)}) copy-start(f32[8,128]{1,0:T(8,128)} %copy-done.27) | copy-start | bytes 12292
  126.6 26.2 %all-to-all-start.5 = ((bf16[128,2,288]{2,1,0:T(2,128)(2,1)}), bf16[128,2,288]{2,1,0:T(2,128)(2,1)S(1)}, u32[]{:S(2)}, u32[]{:S(2)}) async-start(bf16[128,2,288]{2,1,0:T(2,128)(2,1)} %reshape.693), calls=%async_computation.5 | async-start | bytes 393216 | tf_op jit(solution)/shard_map/all_to_all | solution.py:103
  135.4 1.6 copy-start.22
  138.0 0.9 copy-start.14
  138.0 0.9 copy-start.34
  152.8 8.2 %copy-start.20 = (f32[128,8]{0,1:T(8,128)S(1)}, f32[128,8]{0,1:T(8,128)}, u32[]{:S(2)}) copy-start(f32[128,8]{0,1:T(8,128)} %copy-done.19) | copy-start | bytes 12292
  152.8 26.1 %all-to-all-start.7 = ((bf16[128,2,288]{2,1,0:T(2,128)(2,1)}), bf16[128,2,288]{2,1,0:T(2,128)(2,1)S(1)}, u32[]{:S(2)}, u32[]{:S(2)}) async-start(bf16[128,2,288]{2,1,0:T(2,128)(2,1)} %reshape.697), calls=%async_computation.7 | async-start | bytes 393216 | tf_op jit(solution)/shard_map/all_to_all | solution.py:102
  166.5 48.7 %copy-start.1 = (bf16[128,1,576]{0,2,1:T(8,128)(2,1)}, bf16[128,1,576]{0,2,1:T(8,128)(2,1)S(1)}, u32[]{:S(2)}) copy-start(bf16[128,1,576]{0,2,1:T(8,128)(2,1)S(1)} %copy.74) | copy-start | bytes 442372
  179.0 8.2 %copy-start.23 = (f32[8,128]{1,0:T(8,128)S(1)}, f32[8,128]{1,0:T(8,128)}, u32[]{:S(2)}) copy-start(f32[8,128]{1,0:T(8,128)} %multiply_divide_fusion.1) | copy-start | bytes 12292
  179.0 26.2 %all-to-all-start.6 = ((bf16[128,2,288]{2,1,0:T(2,128)(2,1)}), bf16[128,2,288]{2,1,0:T(2,128)(2,1)S(1)}, u32[]{:S(2)}, u32[]{:S(2)}) async-start(bf16[128,2,288]{2,1,0:T(2,128)(2,1)} %reshape.695), calls=%async_computation.6 | async-start | bytes 393216 | tf_op jit(solution)/shard_map/all_to_all | solution.py:101
  187.8 0.9 copy-start.8
  187.8 0.9 copy-start.26
  205.2 26.2 %all-to-all-start.3 = ((bf16[128,2,288]{2,1,0:T(2,128)(2,1)}), bf16[128,2,288]{2,1,0:T(2,128)(2,1)S(1)}, u32[]{:S(2)}, u32[]{:S(2)}) async-start(bf16[128,2,288]{2,1,0:T(2,128)(2,1)} %reshape.689), calls=%async_computation.3 | async-start | bytes 393216 | tf_op jit(solution)/shard_map/all_to_all | solution.py:95
  213.3 1.2 copy-start.18
  (15 other events, 9.7 us)
where the time goes:
time: 338 us; the launch traced here: 337 us
  waiting for transfers between devices  104 us (31%)
  blocking collectives  103 us (30%)
  starting transfers between devices  77.6 us (23%)
  local copies, waits for them, and re-layouts  25 us (7%)
  other arithmetic  14.7 us (4%)
  matrix products  11.2 us (3%)
    psum x1, blocking collectives, shards(): lax.psum((grad_sq_gain, grad_sk_gain, grad_tq_gain, grad_tk_gain), ('dp',...  103 us
    all_to_all x1, starting transfers between devices, shards(): lax.all_to_all(temporal_query[0], 'seq', split_axis=1, concat_axis=0, til...  20.7 us
    unnamed x100, local copies, waits for them, and re-layouts  19.5 us
    all_to_all x1, waiting for transfers between devices, shards(): lax.all_to_all(temporal_value, 'seq', split_axis=1, concat_axis=0, tiled=...  16.8 us
    all_to_all x1, waiting for transfers between devices, shards(): lax.all_to_all(temporal_pos, 'seq', split_axis=0, concat_axis=1, tiled=True)  14.9 us
    all_to_all x1, waiting for transfers between devices, shards(): lax.all_to_all(grad_query_pos, 'seq', split_axis=0, concat_axis=1, tiled=...  14.4 us
    all_to_all x1, waiting for transfers between devices, shards(): lax.all_to_all(out_grad[0], 'seq', split_axis=1, concat_axis=0, tiled=True)  13.6 us
    all_to_all x1, waiting for transfers between devices, shards(): lax.all_to_all(grad_key_pos, 'seq', split_axis=0, concat_axis=1, tiled=True)  12.5 us
  transfers between devices with their start and end apart: 8, of which 8 were waited for; matrix products, arithmetic and copies ran while one was open for 9% of the time, Pallas kernels for 0%

commit v1 on v0

v1 whole, which is shorter than its diff:
```python
import jax
import jax.numpy as jnp
from jax import lax
from jax.experimental import pallas as pl
from jax.experimental.pallas import tpu as pltpu
from jax.sharding import Mesh
from jax.sharding import PartitionSpec as P

HEADS = 8
HEAD_DIM = 72
INNER = 576
TOKENS = 128
SCALE = HEAD_DIM ** (-0.5)
EPS = 1e-06
BF = jnp.bfloat16
F32 = jnp.float32
PARAMS = pltpu.CompilerParams(vmem_limit_bytes=48 * 1024 * 1024)


def dot(left, right, left_dim, right_dim):
    return lax.dot_general(
        left, right, (((left_dim,), (right_dim,)), ((), ())), preferred_element_type=F32
    )


def pack(features, tiles, out_ref):
    size = 16 * tiles
    row = lax.broadcasted_iota(jnp.int32, (size, size), 0)
    col = lax.broadcasted_iota(jnp.int32, (size, size), 1)
    order = (row == (col & 15) * tiles + (col >> 4)).astype(F32).astype(BF)
    stacked = []
    for tile in range(tiles):
        turned = features[128 * tile : 128 * tile + 128, :].T
        stacked.append(
            jnp.concatenate([turned[16 * b : 16 * b + 16, :] for b in range(8)], axis=1)
        )
    mixed = dot(order, jnp.concatenate(stacked, axis=0), 1, 0).astype(BF)
    for b in range(8):
        out_ref[size * b : size * b + size, :] = mixed[:, 128 * b : 128 * b + 128]


def unpack(in_ref, tiles):
    size = 16 * tiles
    row = lax.broadcasted_iota(jnp.int32, (size, size), 0)
    col = lax.broadcasted_iota(jnp.int32, (size, size), 1)
    order = (col == (row & 15) * tiles + (row >> 4)).astype(F32).astype(BF)
    blocks = jnp.concatenate(
        [in_ref[size * b : size * b + size, :] for b in range(8)], axis=1
    )
    mixed = dot(order, blocks, 1, 0).astype(BF)
    turned = []
    for tile in range(tiles):
        rows = mixed[16 * tile : 16 * tile + 16, :]
        turned.append(
            jnp.concatenate([rows[:, 128 * b : 128 * b + 128] for b in range(8)], axis=0).T
        )
    return jnp.concatenate(turned, axis=0)


def column(gain_ref):
    row = lax.broadcasted_iota(jnp.int32, (HEAD_DIM, HEAD_DIM), 0)
    col = lax.broadcasted_iota(jnp.int32, (HEAD_DIM, HEAD_DIM), 1)
    spread = jnp.where(row == col, gain_ref[...], 0.0)
    return jnp.sum(spread, axis=1, keepdims=True)


def normed(values, gain):
    floats = values.astype(F32).reshape(HEADS, HEAD_DIM, TOKENS)
    inverse = lax.rsqrt(jnp.mean(floats * floats, axis=1, keepdims=True) + EPS)
    unit = floats * inverse
    return unit, inverse, (unit * gain[None]).astype(BF)


def normed_back(cotangent, unit, inverse, gain):
    scaled = cotangent * gain[None]
    along = jnp.mean(scaled * unit, axis=1, keepdims=True)
    grad = inverse * (scaled - unit * along)
    return grad.reshape(INNER, TOKENS).astype(BF), jnp.sum(cotangent * unit, axis=0)


def probabilities(query, key_in, same):
    weights = jnp.exp(dot(key_in, query, 0, 0) * SCALE)
    if same is not None:
        weights = weights * same
    return weights * (1.0 / jnp.sum(weights, axis=0, keepdims=True))


def attention_back(probs, query, key_in, value, cotangent):
    rounded = probs.astype(BF)
    grad_value = dot(cotangent, rounded, 1, 1)
    grad_probs = dot(value, cotangent, 0, 0)
    along = jnp.sum(probs * grad_probs, axis=0, keepdims=True)
    grad_scores = (probs * (grad_probs - along) * SCALE).astype(BF)
    grad_query = dot(key_in, grad_scores, 1, 0)
    grad_key = dot(query, grad_scores, 1, 1)
    return grad_query, grad_key, grad_value


def head(values, index):
    return values[HEAD_DIM * index : HEAD_DIM * (index + 1), :]


def by_head(parts):
    return jnp.stack([part.astype(BF).astype(F32) for part in parts])


def gain_row(terms):
    return jnp.sum(terms.T, axis=0, keepdims=True)


def send_kernel(sq, sk, sv, tq, tk, tv_in, og, gain_q, gain_k, out_ref):
    _, _, query = normed(sq[...], column(gain_q))
    _, _, key_in = normed(sk[...], column(gain_k))
    value = sv[...]
    mixed = []
    for h in range(HEADS):
        probs = probabilities(query[h], key_in[h], None).astype(BF)
        mixed.append(dot(head(value, h), probs, 1, 0))
    spatial = jnp.concatenate(mixed, axis=0).astype(BF)
    total = (tv_in[...].astype(F32) + spatial.astype(F32)).astype(BF)
    pack(jnp.concatenate([tq[...], tk[...], og[...], total], axis=0), 18, out_ref)


def temporal_kernel(in_ref, ids_ref, gain_q, gain_k, out_ref, gains_ref):
    arrays = unpack(in_ref, 18)
    tq, tk, og, tv = (arrays[INNER * i : INNER * (i + 1), :] for i in range(4))
    column_q, column_k = column(gain_q), column(gain_k)
    unit_q, inverse_q, query = normed(tq, column_q)
    unit_k, inverse_k, key_in = normed(tk, column_k)
    ids = jnp.broadcast_to(ids_ref[...].astype(F32), (TOKENS, TOKENS))
    same = (ids == ids.T).astype(F32)
    mixed, grads_q, grads_k, grads_v = [], [], [], []
    for h in range(HEADS):
        probs = probabilities(query[h], key_in[h], same)
        value, cotangent = head(tv, h), head(og, h)
        mixed.append(dot(value, probs.astype(BF), 1, 0))
        grad_q, grad_k, grad_v = attention_back(probs, query[h], key_in[h], value, cotangent)
        grads_q.append(grad_q)
        grads_k.append(grad_k)
        grads_v.append(grad_v)
    out = jnp.concatenate(mixed, axis=0).astype(BF)
    grad_v = jnp.concatenate(grads_v, axis=0).astype(BF)
    grad_q, terms_q = normed_back(by_head(grads_q), unit_q, inverse_q, column_q)
    grad_k, terms_k = normed_back(by_head(grads_k), unit_k, inverse_k, column_k)
    gains_ref[0:1, :] = gain_row(terms_q)
    gains_ref[1:2, :] = gain_row(terms_k)
    pack(jnp.concatenate([out, grad_q, grad_k, grad_v], axis=0), 18, out_ref)


def spatial_back_kernel(
    in_ref, sq, sk, sv, gain_q, gain_k, gains_in, out, grad_tq, grad_tk, grad_tv, grad_sq, grad_sk, grad_sv, gains_ref
):
    arrays = unpack(in_ref, 18)
    out[...], grad_tq[...], grad_tk[...], grad_tv[...] = (
        arrays[INNER * i : INNER * (i + 1), :] for i in range(4)
    )
    given = arrays[INNER * 3 :, :]
    column_q, column_k = column(gain_q), column(gain_k)
    unit_q, inverse_q, query = normed(sq[...], column_q)
    unit_k, inverse_k, key_in = normed(sk[...], column_k)
    value_all = sv[...]
    grads_q, grads_k, grads_v = [], [], []
    for h in range(HEADS):
        probs = probabilities(query[h], key_in[h], None)
        grad_q, grad_k, grad_v = attention_back(
            probs, query[h], key_in[h], head(value_all, h), head(given, h)
        )
        grads_q.append(grad_q)
        grads_k.append(grad_k)
        grads_v.append(grad_v)
    grad_sv[...] = jnp.concatenate(grads_v, axis=0).astype(BF)
    grad_sq[...], terms_q = normed_back(by_head(grads_q), unit_q, inverse_q, column_q)
    grad_sk[...], terms_k = normed_back(by_head(grads_k), unit_k, inverse_k, column_k)
    rows = jnp.concatenate([gain_row(terms_q), gain_row(terms_k), gains_in[...]], axis=0)
    rows = jnp.concatenate([rows, jnp.zeros((4, 128 - HEAD_DIM), F32)], axis=1)
    gains_ref[...] = jnp.broadcast_to(rows[None], gains_ref.shape)


def gain_middle_kernel(in_ref, out_ref):
    out_ref[...] = jnp.broadcast_to(jnp.sum(in_ref[...], axis=0, keepdims=True), out_ref.shape)


def gain_last_kernel(in_ref, *outs):
    total = jnp.sum(in_ref[...], axis=0)
    for i, out in enumerate(outs):
        out[...] = total[i : i + 1, :HEAD_DIM]


def shape(*extent, dtype=BF):
    return jax.ShapeDtypeStruct(extent, dtype)


def exchange(message, axes, tiles):
    parts = message.reshape(TOKENS, tiles // 2, 2, 128)
    parts = lax.all_to_all(parts, axes, split_axis=0, concat_axis=0, tiled=True)
    return parts.reshape(TOKENS * tiles, 128)


def shards(
    spatial_query,
    spatial_key,
    spatial_value,
    temporal_query,
    temporal_key,
    temporal_value_in,
    out_grad,
    video_ids,
    spatial_query_gain,
    spatial_key_gain,
    temporal_query_gain,
    temporal_key_gain,
):
    sq, sk, sv, tq, tk, tv_in, og = (
        a.reshape(TOKENS, INNER).T
        for a in (
            spatial_query,
            spatial_key,
            spatial_value,
            temporal_query,
            temporal_key,
            temporal_value_in,
            out_grad,
        )
    )
    sq_gain, sk_gain, tq_gain, tk_gain = (
        g.reshape(1, HEAD_DIM)
        for g in (spatial_query_gain, spatial_key_gain, temporal_query_gain, temporal_key_gain)
    )
    seq = ("z", "y", "core")
    sent = pl.pallas_call(send_kernel, out_shape=shape(2304, 128), compiler_params=PARAMS)(
        sq, sk, sv, tq, tk, tv_in, og, sq_gain, sk_gain
    )
    arrived = exchange(sent, seq, 18)
    sent, temporal_gains = pl.pallas_call(
        temporal_kernel,
        out_shape=(shape(2304, 128), shape(2, HEAD_DIM, dtype=F32)),
        compiler_params=PARAMS,
    )(arrived, video_ids, tq_gain, tk_gain)
    arrived = exchange(sent, seq, 18)
    results = pl.pallas_call(
        spatial_back_kernel,
        out_shape=(shape(INNER, TOKENS),) * 7 + (shape(16, 4, 128, dtype=F32),),
        compiler_params=PARAMS,
    )(arrived, sq, sk, sv, sq_gain, sk_gain, temporal_gains)
    out, grad_tq, grad_tk, grad_tv, grad_sq, grad_sk, grad_sv, gains = results
    gains = lax.all_to_all(gains, "z", split_axis=0, concat_axis=0, tiled=True)
    gains = pl.pallas_call(
        gain_middle_kernel, out_shape=shape(32, 4, 128, dtype=F32), compiler_params=PARAMS
    )(gains)
    gains = lax.all_to_all(gains, ("dp", "y", "core"), split_axis=0, concat_axis=0, tiled=True)
    gains = pl.pallas_call(
        gain_last_kernel, out_shape=(shape(1, HEAD_DIM, dtype=F32),) * 4, compiler_params=PARAMS
    )(gains)
    arrays = (out, grad_sq, grad_sk, grad_sv, grad_tq, grad_tk, grad_tv)
    return tuple(a.T.reshape(1, 1, TOKENS, INNER) for a in arrays) + tuple(
        g.reshape(HEAD_DIM) for g in gains
    )


def solution(mesh):
    fine = Mesh(mesh.devices.reshape(4, 16, 4, 2), ("dp", "z", "y", "core"))
    tokens = P("dp", ("z", "y", "core"), None, None)
    return jax.shard_map(
        shards,
        mesh=fine,
        in_specs=(tokens,) * 7 + (P("dp", None),) + (P(),) * 4,
        out_specs=(tokens,) * 7 + (P(),) * 4,
        check_vma=False,
    )
```

time: 338 us -> 147 us (0.43)
  waiting for transfers between devices: 104 us -> 0 us
  starting transfers between devices: 77.6 us -> 0 us
  blocking collectives: 103 us -> 128 us
  local copies, waits for them, and re-layouts: 25 us -> 7.73 us
  other arithmetic: 14.7 us -> 0 us
  matrix products: 11.2 us -> 0 us
  Pallas kernels: 0 us -> 9.62 us
    all_to_all x0 -> x4, blocking collectives: none -> 128 us  [the longest x2 96.7 us: exchange(): parts = lax.all_to_all(parts, axes, split_axis=0, concat_axis=0, tiled=True)]
    all_to_all x8 -> x0, waiting for transfers between devices: 104 us -> none  [the longest x1 16.8 us: shards(): lax.all_to_all(temporal_value, 'seq', split_axis=1, concat_axis=0, tiled=...]
    psum x1 -> x0, blocking collectives: 103 us -> none  [shards(): lax.psum((grad_sq_gain, grad_sk_gain, grad_tq_gain, grad_tk_gain), ('dp',...]
    all_to_all x8 -> x0, starting transfers between devices: 77.6 us -> none  [the longest x1 20.7 us: shards(): lax.all_to_all(temporal_query[0], 'seq', split_axis=1, concat_axis=0, til...]
    unnamed x100 -> x30, local copies, waits for them, and re-layouts: 19.5 us -> 7.73 us
    dot_general x10 -> x0, matrix products: 9.63 us -> none  [the longest x6 5.18 us: attend(): jnp.einsum(mix_form, probs, value_h, preferred_element_type=jnp.float32)]
    pallas_call x0 -> x5, Pallas kernels: none -> 9.62 us  [the longest x1 4.34 us: shards(): pl.pallas_call(temporal_kernel, out_shape=(shape(2304, 128), shape(2, HEA...]
    unnamed x5 -> x0, other arithmetic: 7.06 us -> none
  transfers between devices with their start and end apart: 8 -> 0, of which waited for: 8 -> 0; matrix products, arithmetic and copies ran while one was open for 9% -> 0% of each run, Pallas kernels for 0% -> 0%
where the time goes in v1:
time: 147 us; the launch traced here: 146 us
  blocking collectives  128 us (87%)
  Pallas kernels  9.62 us (7%)
  local copies, waits for them, and re-layouts  7.73 us (5%)
    all_to_all x2, blocking collectives, exchange(): parts = lax.all_to_all(parts, axes, split_axis=0, concat_axis=0, tiled=True)  96.7 us
    all_to_all x1, blocking collectives, shards(): gains = lax.all_to_all(gains, 'z', split_axis=0, concat_axis=0, tiled=True)  17.4 us
    all_to_all x1, blocking collectives, shards(): lax.all_to_all(gains, ('dp', 'y', 'core'), split_axis=0, concat_axis=0, t...  14.3 us
    unnamed x30, local copies, waits for them, and re-layouts  7.73 us
    pallas_call x1, Pallas kernels, shards(): pl.pallas_call(temporal_kernel, out_shape=(shape(2304, 128), shape(2, HEA...  4.34 us
    pallas_call x1, Pallas kernels, shards(): pl.pallas_call(spatial_back_kernel, out_shape=(shape(INNER, TOKENS),) * 7...  3.35 us

profile of v1, /device:TPU:1, one launch (start us, length us, event | category | flops | bytes accessed | tf_op | source)
XLA Modules:
  0.0 146.5 jit_solution(14305825571531996601)
XLA Ops:
  0.6 0.0 copy-start.10
  0.7 0.0 copy-start.11
  0.7 0.6 copy-done.10
  1.3 0.0 copy-done.11
  1.3 0.0 copy-start
  1.3 0.9 copy-done
  2.2 0.0 copy-start.2
  2.2 0.9 copy-done.2
  3.1 0.0 copy-start.4
  3.1 0.9 copy-done.4
  4.0 0.0 copy-start.6
  4.1 0.9 copy-done.6
  5.0 0.9 copy-done.7
  5.9 0.9 copy-done.8
  6.8 0.9 copy-done.9
  7.7 1.4 shard_map.203
  9.1 54.1 %all_to_all.20 = bf16[128,9,2,128]{3,2,1,0:T(2,128)(2,1)S(1)} all-to-all(bf16[128,9,2,128]{3,2,1,0:T(2,128)(2,1)S(1)} %bitcast.56), channel_id=1, replica_groups=mesh['dp'=4,'z'=16,'y'=4,'core'=2] {'z','y','core'}, dimensions={0} | all-to-all | bytes 1179648 | tf_op jit(solution)/shard_map/all_to_all | solution.py:195
  63.1 0.6 copy-done.12
  63.8 0.0 copy-done.13
  63.8 0.0 copy-done.14
  63.8 4.3 %shard_map.204 = (bf16[2304,128]{1,0:T(8,128)(2,1)S(1)}, f32[2,72]{1,0:T(2,128)S(1)}) custom-call(bf16[2304,128]{1,0:T(8,128)(2,1)S(1)} %bitcast.55, s32[1,128]{1,0:T(1,128)S(1)} %copy-done.12, f32[1,72]{1,0:T(1,128)S(1)} %bitcast.72, f32[1,72]{1,0:T(1,128)S(1)} %bitcast.73), custom_call_target="tpu_custom_call" | custom-call | tf_op jit(solution)/shard_map/pallas_call | solution.py:234
  68.1 0.0 copy-start.1
  68.2 0.0 copy-start.3
  68.2 0.0 copy-start.5
  68.2 42.6 %all_to_all.21 = bf16[128,9,2,128]{3,2,1,0:T(2,128)(2,1)S(1)} all-to-all(bf16[128,9,2,128]{3,2,1,0:T(2,128)(2,1)S(1)} %bitcast.57), channel_id=1, replica_groups=mesh['dp'=4,'z'=16,'y'=4,'core'=2] {'z','y','core'}, dimensions={0} | all-to-all | bytes 1179648 | tf_op jit(solution)/shard_map/all_to_all | solution.py:195
  110.8 0.0 copy-done.1
  110.8 0.0 copy-done.3
  110.8 0.0 copy-done.5
  110.8 3.3 %shard_map.205 = (bf16[576,128]{1,0:T(8,128)(2,1)}, bf16[576,128]{1,0:T(8,128)(2,1)}, bf16[576,128]{1,0:T(8,128)(2,1)}, bf16[576,128]{1,0:T(8,128)(2,1)}, bf16[5...) custom-call(bf16[2304,128]{1,0:T(8,128)(2,1)S(1)} %bitcast.54, ...), custom_call_target="tpu_custom_call" | custom-call | tf_op jit(solution)/shard_map/pallas_call | solution.py:240
  114.2 17.4 %all_to_all.22.in_ref = f32[16,4,128]{2,1,0:T(4,128)S(1)} all-to-all(f32[16,4,128]{2,1,0:T(4,128)S(1)} %get-tuple-element.34), channel_id=1, replica_groups=mesh['dp'=4,'z'=16,'y'=4,'core'=2] {'z'}, dimensions={0} | all-to-all | bytes 65536 | tf_op jit(solution)/shard_map/all_to_all | solution.py:246
  131.6 14.3 %all_to_all.23.in_ref = f32[32,4,128]{2,1,0:T(4,128)S(1)} all-to-all(f32[32,4,128]{2,1,0:T(4,128)S(1)} %shard_map.206), channel_id=1, replica_groups=mesh['dp'=4,'z'=16,'y'=4,'core'=2] {'dp','y','core'}, dimensions={0} | all-to-all | bytes 131072 | tf_op jit(solution)/shard_map/all_to_all | solution.py:250
  145.9 0.6 shard_map.207
  (7 shorter events, 0.0 us)
Async XLA Ops:
  0.6 0.7 copy-start.10
  0.7 0.7 copy-start.11
  1.3 0.9 copy-start
  2.2 0.9 copy-start.2
  3.1 0.9 copy-start.4
  4.0 0.9 copy-start.6
  5.0 0.9 copy-start.7
  5.9 0.9 copy-start.8
  6.8 0.9 copy-start.9
  63.1 0.7 copy-start.12
  63.1 0.7 copy-start.13
  63.1 0.7 copy-start.14
  68.1 42.7 %copy-start.1 = (bf16[1,1,128,576]{2,3,1,0:T(8,128)(2,1)S(1)}, bf16[1,1,128,576]{2,3,1,0:T(8,128)(2,1)}, u32[]{:S(2)}) copy-start(bf16[1,1,128,576]{2,3,1,0:T(8,128)(2,1)} %param.12) | copy-start | bytes 442372
  68.2 42.7 %copy-start.3 = (bf16[1,1,128,576]{2,3,1,0:T(8,128)(2,1)S(1)}, bf16[1,1,128,576]{2,3,1,0:T(8,128)(2,1)}, u32[]{:S(2)}) copy-start(bf16[1,1,128,576]{2,3,1,0:T(8,128)(2,1)} %param.13) | copy-start | bytes 442372
  68.2 42.6 %copy-start.5 = (bf16[1,1,128,576]{2,3,1,0:T(8,128)(2,1)S(1)}, bf16[1,1,128,576]{2,3,1,0:T(8,128)(2,1)}, u32[]{:S(2)}) copy-start(bf16[1,1,128,576]{2,3,1,0:T(8,128)(2,1)} %param.14) | copy-start | bytes 442372

commit v2 on v1

--- a/solution.py
+++ b/solution.py
@@ -14,7 +14,7 @@
 EPS = 1e-06
 BF = jnp.bfloat16
 F32 = jnp.float32
-PARAMS = pltpu.CompilerParams(vmem_limit_bytes=48 * 1024 * 1024)
+MIB = 1024 * 1024
 
 
 def dot(left, right, left_dim, right_dim):
@@ -85,15 +85,13 @@
     return weights * (1.0 / jnp.sum(weights, axis=0, keepdims=True))
 
 
-def attention_back(probs, query, key_in, value, cotangent):
-    rounded = probs.astype(BF)
-    grad_value = dot(cotangent, rounded, 1, 1)
+def scores_back(probs, query, key_in, value, cotangent):
     grad_probs = dot(value, cotangent, 0, 0)
     along = jnp.sum(probs * grad_probs, axis=0, keepdims=True)
     grad_scores = (probs * (grad_probs - along) * SCALE).astype(BF)
     grad_query = dot(key_in, grad_scores, 1, 0)
     grad_key = dot(query, grad_scores, 1, 1)
-    return grad_query, grad_key, grad_value
+    return grad_query, grad_key
 
 
 def head(values, index):
@@ -104,13 +102,26 @@
     return jnp.stack([part.astype(BF).astype(F32) for part in parts])
 
 
-def gain_row(terms):
-    return jnp.sum(terms.T, axis=0, keepdims=True)
-
-
-def send_kernel(sq, sk, sv, tq, tk, tv_in, og, gain_q, gain_k, out_ref):
+def load(sources, buffers, sems):
+    copies = [
+        pltpu.make_async_copy(source, buffer, sems.at[i])
+        for i, (source, buffer) in enumerate(zip(sources, buffers))
+    ]
+    for copy in copies:
+        copy.start()
+    return copies
+
+
+def send_kernel(*refs):
+    sources, (out_ref, *buffers, sems) = refs[:9], refs[9:]
+    copies = load(sources, buffers, sems)
+    gain_q, gain_k, sq, sk, sv, tq, tk, og, tv_in = buffers
+    for copy in copies[:4]:
+        copy.wait()
     _, _, query = normed(sq[...], column(gain_q))
     _, _, key_in = normed(sk[...], column(gain_k))
+    for copy in copies[4:]:
+        copy.wait()
     value = sv[...]
     mixed = []
     for h in range(HEADS):
@@ -121,40 +132,72 @@
     pack(jnp.concatenate([tq[...], tk[...], og[...], total], axis=0), 18, out_ref)
 
 
-def temporal_kernel(in_ref, ids_ref, gain_q, gain_k, out_ref, gains_ref):
+def same_video(ids):
+    ids = jnp.broadcast_to(ids.astype(F32), (TOKENS, TOKENS))
+    return (ids == ids.T).astype(F32)
+
+
+def temporal_first_kernel(in_ref, ids_hbm, gain_q_hbm, gain_k_hbm, out_ref, arrays_ref, ids, gain_q, gain_k, sems):
+    copies = load((ids_hbm, gain_q_hbm, gain_k_hbm), (ids, gain_q, gain_k), sems)
     arrays = unpack(in_ref, 18)
-    tq, tk, og, tv = (arrays[INNER * i : INNER * (i + 1), :] for i in range(4))
+    arrays_ref[...] = arrays
+    for copy in copies:
+        copy.wait()
+    tq, tk, og = (arrays[INNER * i : INNER * (i + 1), :] for i in range(3))
+    _, _, query = normed(tq, column(gain_q))
+    _, _, key_in = normed(tk, column(gain_k))
+    same = same_video(ids[...])
+    grads_v = []
+    for h in range(HEADS):
+        probs = probabilities(query[h], key_in[h], same).astype(BF)
+        grads_v.append(dot(head(og, h), probs, 1, 1))
+    grad_v = jnp.concatenate(grads_v, axis=0).astype(BF)
+    pack(jnp.concatenate([grad_v, jnp.zeros((192, TOKENS), BF)], axis=0), 6, out_ref)
+
+
+def temporal_second_kernel(arrays_ref, ids_ref, gain_q, gain_k, out_ref, terms_ref):
+    tq, tk, og, tv = (arrays_ref[INNER * i : INNER * (i + 1), :] for i in range(4))
     column_q, column_k = column(gain_q), column(gain_k)
     unit_q, inverse_q, query = normed(tq, column_q)
     unit_k, inverse_k, key_in = normed(tk, column_k)
-    ids = jnp.broadcast_to(ids_ref[...].astype(F32), (TOKENS, TOKENS))
-    same = (ids == ids.T).astype(F32)
-    mixed, grads_q, grads_k, grads_v = [], [], [], []
+    same = same_video(ids_ref[...])
+    mixed, grads_q, grads_k = [], [], []
     for h in range(HEADS):
         probs = probabilities(query[h], key_in[h], same)
         value, cotangent = head(tv, h), head(og, h)
         mixed.append(dot(value, probs.astype(BF), 1, 0))
-        grad_q, grad_k, grad_v = attention_back(probs, query[h], key_in[h], value, cotangent)
+        grad_q, grad_k = scores_back(probs, query[h], key_in[h], value, cotangent)
         grads_q.append(grad_q)
         grads_k.append(grad_k)
-        grads_v.append(grad_v)
     out = jnp.concatenate(mixed, axis=0).astype(BF)
-    grad_v = jnp.concatenate(grads_v, axis=0).astype(BF)
-    grad_q, terms_q = normed_back(by_head(grads_q), unit_q, inverse_q, column_q)
-    grad_k, terms_k = normed_back(by_head(grads_k), unit_k, inverse_k, column_k)
-    gains_ref[0:1, :] = gain_row(terms_q)
-    gains_ref[1:2, :] = gain_row(terms_k)
-    pack(jnp.concatenate([out, grad_q, grad_k, grad_v], axis=0), 18, out_ref)
+    grad_q, terms_ref[0] = normed_back(by_head(grads_q), unit_q, inverse_q, column_q)
+    grad_k, terms_ref[1] = normed_back(by_head(grads_k), unit_k, inverse_k, column_k)
+    spare = jnp.zeros((320, TOKENS), BF)
+    pack(jnp.concatenate([out, grad_q, grad_k, spare], axis=0), 16, out_ref)
+
+
+def gain_rows(spatial, temporal):
+    both = [jnp.sum(terms, axis=1, keepdims=True) for terms in (spatial, temporal)]
+    high = [total.astype(BF).astype(F32) for total in both]
+    low = [total - part for total, part in zip(both, high)]
+    tiles = [
+        [jnp.zeros((64, 1), F32), low[0][56:], low[1][56:], jnp.zeros((32, 1), F32)],
+        [high[0], low[0][:56]],
+        [high[1], low[1][:56]],
+    ]
+    row = lax.broadcasted_iota(jnp.int32, (16, 128), 0)
+    rows = jnp.zeros((16, 128), F32)
+    for i, parts in enumerate(tiles):
+        tile = jnp.broadcast_to(jnp.concatenate(parts, axis=0), (128, 128)).T[:16, :]
+        rows = rows + jnp.where(row == 13 + i, tile, 0.0)
+    return rows
 
 
 def spatial_back_kernel(
-    in_ref, sq, sk, sv, gain_q, gain_k, gains_in, out, grad_tq, grad_tk, grad_tv, grad_sq, grad_sk, grad_sv, gains_ref
+    in_ref, message, terms_ref, sq, sk, sv, gain_q, gain_k, out_ref, grad_tv, grad_sq, grad_sk, grad_sv
 ):
-    arrays = unpack(in_ref, 18)
-    out[...], grad_tq[...], grad_tk[...], grad_tv[...] = (
-        arrays[INNER * i : INNER * (i + 1), :] for i in range(4)
-    )
-    given = arrays[INNER * 3 :, :]
+    given = unpack(in_ref, 6)[:INNER, :]
+    grad_tv[...] = given
     column_q, column_k = column(gain_q), column(gain_k)
     unit_q, inverse_q, query = normed(sq[...], column_q)
     unit_k, inverse_k, key_in = normed(sk[...], column_k)
@@ -162,32 +205,68 @@
     grads_q, grads_k, grads_v = [], [], []
     for h in range(HEADS):
         probs = probabilities(query[h], key_in[h], None)
-        grad_q, grad_k, grad_v = attention_back(
-            probs, query[h], key_in[h], head(value_all, h), head(given, h)
-        )
+        cotangent = head(given, h)
+        grad_q, grad_k = scores_back(probs, query[h], key_in[h], head(value_all, h), cotangent)
         grads_q.append(grad_q)
         grads_k.append(grad_k)
-        grads_v.append(grad_v)
+        grads_v.append(dot(cotangent, probs.astype(BF), 1, 1))
     grad_sv[...] = jnp.concatenate(grads_v, axis=0).astype(BF)
     grad_sq[...], terms_q = normed_back(by_head(grads_q), unit_q, inverse_q, column_q)
     grad_sk[...], terms_k = normed_back(by_head(grads_k), unit_k, inverse_k, column_k)
-    rows = jnp.concatenate([gain_row(terms_q), gain_row(terms_k), gains_in[...]], axis=0)
-    rows = jnp.concatenate([rows, jnp.zeros((4, 128 - HEAD_DIM), F32)], axis=1)
-    gains_ref[...] = jnp.broadcast_to(rows[None], gains_ref.shape)
+    rows = jnp.stack([gain_rows(terms_q, terms_ref[0]), gain_rows(terms_k, terms_ref[1])])
+    filled = message[...].astype(F32).reshape(64, 2, 16, 128) + rows[None]
+    out_ref[...] = filled.astype(BF).reshape(2048, 128)
 
 
 def gain_middle_kernel(in_ref, out_ref):
-    out_ref[...] = jnp.broadcast_to(jnp.sum(in_ref[...], axis=0, keepdims=True), out_ref.shape)
+    total = jnp.sum(in_ref[...].astype(F32).reshape(128, 16, 128), axis=0)
+    rest, spatial, temporal = (total[i : i + 1, :] for i in (13, 14, 15))
+    pad = jnp.zeros((1, 128 - HEAD_DIM), F32)
+    low = [
+        jnp.concatenate([spatial[:, 72:], rest[:, 64:80], pad], axis=1),
+        jnp.concatenate([temporal[:, 72:], rest[:, 80:96], pad], axis=1),
+    ]
+    rows = jnp.concatenate([spatial + low[0], temporal + low[1]], axis=0)
+    out_ref[...] = jnp.broadcast_to(rows[None], out_ref.shape)
+
+
+def last_kernel(in_ref, out, grad_tq, grad_tk):
+    arrays = unpack(in_ref, 16)
+    out[...], grad_tq[...], grad_tk[...] = (
+        arrays[INNER * i : INNER * (i + 1), :] for i in range(3)
+    )
 
 
 def gain_last_kernel(in_ref, *outs):
-    total = jnp.sum(in_ref[...], axis=0)
+    total = jnp.sum(in_ref[...].reshape(4, 2, 2, 128), axis=0)
     for i, out in enumerate(outs):
-        out[...] = total[i : i + 1, :HEAD_DIM]
+        out[...] = total[i % 2, i // 2 : i // 2 + 1, :HEAD_DIM]
 
 
 def shape(*extent, dtype=BF):
     return jax.ShapeDtypeStruct(extent, dtype)
+
+
+def call(kernel, out_shape, *args, in_hbm=0, scratch=(), work=0, vmem=32):
+    specs = [pl.BlockSpec(memory_space=pltpu.VMEM)] * (len(args) - in_hbm)
+    specs += [pl.BlockSpec(memory_space=pltpu.HBM)] * in_hbm
+    split = len(args) - in_hbm
+    args = args[:split] + tuple(
+        pltpu.with_memory_space_constraint(a, pltpu.HBM) for a in args[split:]
+    )
+    cost = pl.CostEstimate(flops=work, bytes_accessed=0, transcendentals=0) if work else None
+    return pl.pallas_call(
+        kernel,
+        out_shape=out_shape,
+        in_specs=specs,
+        scratch_shapes=scratch,
+        compiler_params=pltpu.CompilerParams(vmem_limit_bytes=vmem * MIB),
+        cost_estimate=cost,
+    )(*args)
+
+
+def buffers(*arrays):
+    return [pltpu.VMEM(a.shape, a.dtype) for a in arrays] + [pltpu.SemaphoreType.DMA((len(arrays),))]
 
 
 def exchange(message, axes, tiles):
@@ -227,32 +306,46 @@
         for g in (spatial_query_gain, spatial_key_gain, temporal_query_gain, temporal_key_gain)
     )
     seq = ("z", "y", "core")
-    sent = pl.pallas_call(send_kernel, out_shape=shape(2304, 128), compiler_params=PARAMS)(
-        sq, sk, sv, tq, tk, tv_in, og, sq_gain, sk_gain
-    )
+    array = shape(INNER, TOKENS)
+    args = (sq_gain, sk_gain, sq, sk, sv, tq, tk, og, tv_in)
+    sent = call(send_kernel, shape(2304, 128), *args, in_hbm=9, scratch=buffers(*args))
     arrived = exchange(sent, seq, 18)
-    sent, temporal_gains = pl.pallas_call(
-        temporal_kernel,
-        out_shape=(shape(2304, 128), shape(2, HEAD_DIM, dtype=F32)),
-        compiler_params=PARAMS,
-    )(arrived, video_ids, tq_gain, tk_gain)
-    arrived = exchange(sent, seq, 18)
-    results = pl.pallas_call(
+    args = (video_ids, tq_gain, tk_gain)
+    sent, arrays = call(
+        temporal_first_kernel,
+        (shape(768, 128), shape(2304, 128)),
+        arrived,
+        *args,
+        in_hbm=3,
+        scratch=buffers(*args),
+    )
+    arrived = exchange(sent, seq, 6)
+    message, terms = call(
+        temporal_second_kernel,
+        (shape(2048, 128), shape(2, HEAD_DIM, TOKENS, dtype=F32)),
+        arrays,
+        *args,
+        work=4_000_000_000,
+    )
+    sent, grad_tv, grad_sq, grad_sk, grad_sv = call(
         spatial_back_kernel,
-        out_shape=(shape(INNER, TOKENS),) * 7 + (shape(16, 4, 128, dtype=F32),),
-        compiler_params=PARAMS,
-    )(arrived, sq, sk, sv, sq_gain, sk_gain, temporal_gains)
-    out, grad_tq, grad_tk, grad_tv, grad_sq, grad_sk, grad_sv, gains = results
-    gains = lax.all_to_all(gains, "z", split_axis=0, concat_axis=0, tiled=True)
-    gains = pl.pallas_call(
-        gain_middle_kernel, out_shape=shape(32, 4, 128, dtype=F32), compiler_params=PARAMS
-    )(gains)
-    gains = lax.all_to_all(gains, ("dp", "y", "core"), split_axis=0, concat_axis=0, tiled=True)
-    gains = pl.pallas_call(
-        gain_last_kernel, out_shape=(shape(1, HEAD_DIM, dtype=F32),) * 4, compiler_params=PARAMS
-    )(gains)
-    arrays = (out, grad_sq, grad_sk, grad_sv, grad_tq, grad_tk, grad_tv)
-    return tuple(a.T.reshape(1, 1, TOKENS, INNER) for a in arrays) + tuple(
+        (shape(2048, 128),) + (array,) * 4,
+        arrived,
+        message,
+        terms,
+        sq,
+        sk,
+        sv,
+        sq_gain,
+        sk_gain,
+    )
+    arrived = exchange(sent, seq, 16)
+    gains = call(gain_middle_kernel, shape(8, 2, 128, dtype=F32), arrived)
+    gains = lax.all_to_all(gains, ("dp", "core"), split_axis=0, concat_axis=0, tiled=True)
+    out, grad_tq, grad_tk = call(last_kernel, (array,) * 3, arrived, work=1_000_000_000)
+    gains = call(gain_last_kernel, (shape(1, HEAD_DIM, dtype=F32),) * 4, gains)
+    results = (out, grad_sq, grad_sk, grad_sv, grad_tq, grad_tk, grad_tv)
+    return tuple(a.T.reshape(1, 1, TOKENS, INNER) for a in results) + tuple(
         g.reshape(HEAD_DIM) for g in gains
     )
 

time: 147 us -> 142 us (0.966)
  blocking collectives: 128 us -> 92.8 us
  waiting for transfers between devices: 0 us -> 18.2 us
  starting transfers between devices: 0 us -> 14.5 us
  local copies, waits for them, and re-layouts: 7.73 us -> 1.33 us
  Pallas kernels: 9.62 us -> 13.8 us
    all_to_all x2 -> x0, blocking collectives: 31.7 us -> none  [the longest x1 17.4 us: shards(): gains = lax.all_to_all(gains, 'z', split_axis=0, concat_axis=0, tiled=True)]
    all_to_all x0 -> x2, waiting for transfers between devices: none -> 18.2 us  [the longest x1 14.6 us: exchange(): parts = lax.all_to_all(parts, axes, split_axis=0, concat_axis=0, tiled=True)]
    all_to_all x0 -> x2, starting transfers between devices: none -> 14.5 us  [the longest x1 9 us: exchange(): parts = lax.all_to_all(parts, axes, split_axis=0, concat_axis=0, tiled=True)]
    unnamed x30 -> x16, local copies, waits for them, and re-layouts: 7.73 us -> 1.33 us
    pallas_call x5 -> x7, Pallas kernels: 9.62 us -> 13.8 us  [call(): pl.pallas_call(kernel, out_shape=out_shape, in_specs=specs, scratch_shape...]
    all_to_all x2, blocking collectives: 96.7 us -> 92.8 us  [exchange(): parts = lax.all_to_all(parts, axes, split_axis=0, concat_axis=0, tiled=True)]
  transfers between devices with their start and end apart: 0 -> 2, of which waited for: 0 -> 2; matrix products, arithmetic and copies ran while one was open for 0% -> 0% of each run, Pallas kernels for 0% -> 3%
where the time goes in v2:
time: 142 us; the launch traced here: 141 us
  blocking collectives  92.8 us (65%)
  waiting for transfers between devices  18.2 us (13%)
  starting transfers between devices  14.5 us (10%)
  Pallas kernels  13.8 us (10%)
    all_to_all x2, blocking collectives, exchange(): parts = lax.all_to_all(parts, axes, split_axis=0, concat_axis=0, tiled=True)  92.8 us
    all_to_all x1, waiting for transfers between devices, exchange(): parts = lax.all_to_all(parts, axes, split_axis=0, concat_axis=0, tiled=True)  14.6 us
    pallas_call x7, Pallas kernels, call(): pl.pallas_call(kernel, out_shape=out_shape, in_specs=specs, scratch_shape...  13.8 us
    all_to_all x1, starting transfers between devices, exchange(): parts = lax.all_to_all(parts, axes, split_axis=0, concat_axis=0, tiled=True)  9 us
    all_to_all x1, starting transfers between devices, shards(): lax.all_to_all(gains, ('dp', 'core'), split_axis=0, concat_axis=0, tiled=...  5.5 us
    all_to_all x1, waiting for transfers between devices, shards(): lax.all_to_all(gains, ('dp', 'core'), split_axis=0, concat_axis=0, tiled=...  3.53 us
  transfers between devices with their start and end apart: 2, of which 2 were waited for; matrix products, arithmetic and copies ran while one was open for 0% of the time, Pallas kernels for 3%

profile of v2, /device:TPU:1, one launch (start us, length us, event | category | flops | bytes accessed | tf_op | source)
XLA Modules:
  0.0 141.2 jit_solution(13757461060217252221)
XLA Ops:
  0.6 2.7 %shard_map.203 = bf16[2304,128]{1,0:T(8,128)(2,1)S(1)} custom-call(f32[1,72]{1,0:T(1,128)} %bitcast.68, f32[1,72]{1,0:T(1,128)} %bitcast.70, bf16[576,128]{1,0:T(8,128)(2,1)} %bitcast.61, bf16[576,128]{1,0:T(8,128)(2,1)} %bitcast.63, bf16[576,128]{1,0:T(8,128)(2,1)} %bitcast.65, bf16[576,128]{1,0:T(8,128)(2,1)} %bitcast.76, bf16[576,128]{1,0:T(8,128)(2,1)} %bitcast.77, ...), custom_call_target="tpu_custom_call" | custom-call | tf_op jit(solution)/shard_map/pallas_call | solution.py:258
  3.3 54.1 %all_to_all.20 = bf16[128,9,2,128]{3,2,1,0:T(2,128)(2,1)S(1)} all-to-all(bf16[128,9,2,128]{3,2,1,0:T(2,128)(2,1)S(1)} %bitcast.57), channel_id=1, replica_groups=mesh['dp'=4,'z'=16,'y'=4,'core'=2] {'z','y','core'}, dimensions={0} | all-to-all | bytes 1179648 | tf_op jit(solution)/shard_map/all_to_all | solution.py:274
  57.4 3.0 %shard_map.204 = (bf16[768,128]{1,0:T(8,128)(2,1)}, bf16[2304,128]{1,0:T(8,128)(2,1)S(1)}) custom-call(bf16[2304,128]{1,0:T(8,128)(2,1)S(1)} %bitcast.56, s32[1,128]{1,0:T(1,128)} %ids_ref.1, f32[1,72]{1,0:T(1,128)} %bitcast.72, f32[1,72]{1,0:T(1,128)} %bitcast.74), custom_call_target="tpu_custom_call" | custom-call | tf_op jit(solution)/shard_map/pallas_call | solution.py:258
  60.4 9.0 %all-to-all-start.1 = ((bf16[128,3,2,128]{3,2,1,0:T(2,128)(2,1)}), bf16[128,3,2,128]{3,2,1,0:T(2,128)(2,1)S(1)}, u32[]{:S(2)}, u32[]{:S(2)}) async-start(bf16[128,3,2,128]{3,2,1,0:T(2,128)(2,1)} %bitcast.20), calls=%async_computation.1 | async-start | bytes 393216 | tf_op jit(solution)/shard_map/all_to_all | solution.py:274
  69.4 0.0 copy-start.5
  69.4 0.0 copy-start.6
  69.4 0.0 copy-start.7
  69.4 0.6 copy-done.5
  70.0 0.0 copy-done.6
  70.0 0.0 copy-done.7
  70.1 0.0 copy-start
  70.1 0.0 copy-start.1
  70.1 0.0 copy-start.2
  70.1 2.6 %shard_map.205 = (bf16[2048,128]{1,0:T(8,128)(2,1)S(1)}, f32[2,72,128]{2,1,0:T(8,128)S(1)}) custom-call(bf16[2304,128]{1,0:T(8,128)(2,1)S(1)} %get-tuple-element.28.arrays_ref, s32[1,128]{1,0:T(1,128)S(1)} %copy-done.5, f32[1,72]{1,0:T(1,128)S(1)} %bitcast.73, f32[1,72]{1,0:T(1,128)S(1)} %bitcast.75), custom_call_target="tpu_custom_call" | custom-call | flops 4000000000 | tf_op jit(solution)/shard_map/pallas_call | solution.py:258
  72.7 14.6 %all-to-all-done.1 = bf16[128,3,2,128]{3,2,1,0:T(2,128)(2,1)S(1)} async-done(((bf16[128,3,2,128]{3,2,1,0:T(2,128)(2,1)}), bf16[128,3,2,128]{3,2,1,0:T(2,128)(2,1)S(1)}, u32[]{:S(2)}, u32[]{:S(2)}) %all-to-all-start.1) | async-done | bytes 196640 | tf_op jit(solution)/shard_map/all_to_all | solution.py:274
  87.3 0.0 copy-start.3
  87.3 0.0 copy-start.4
  87.3 0.0 copy-done
  87.3 0.0 copy-done.1
  87.3 0.0 copy-done.2
  87.3 0.6 copy-done.3
  88.0 0.0 copy-done.4
  88.0 3.1 %shard_map.206 = (bf16[2048,128]{1,0:T(8,128)(2,1)S(1)}, bf16[576,128]{1,0:T(8,128)(2,1)}, bf16[576,128]{1,0:T(8,128)(2,1)}, bf16[576,128]{1,0:T(8,128)(2,1)}, bf16[576,128]{1,0:T(8,128)(2,1)}) custom-call(bf16[768,128]{1,0:T(8,128)(2,1)S(1)} %bitcast.60, bf16[2048,128]{1,0:T(8,128)(2,1)S(1)} %get-tuple-element.29.message, ...), custom_call_target="tpu_custom_call" | custom-call | tf_op jit(solution)/shard_map/pallas_call | solution.py:258
  91.1 38.7 %all_to_all.21 = bf16[128,8,2,128]{3,2,1,0:T(2,128)(2,1)S(1)} all-to-all(bf16[128,8,2,128]{3,2,1,0:T(2,128)(2,1)S(1)} %bitcast.67), channel_id=1, replica_groups=mesh['dp'=4,'z'=16,'y'=4,'core'=2] {'z','y','core'}, dimensions={0} | all-to-all | bytes 1048576 | tf_op jit(solution)/shard_map/all_to_all | solution.py:274
  129.8 0.8 shard_map.208
  130.6 5.5 %all-to-all-start.3 = ((f32[8,2,128]{2,1,0:T(2,128)}), f32[8,2,128]{2,1,0:T(2,128)S(1)}, u32[]{:S(2)}, u32[]{:S(2)}) async-start(f32[8,2,128]{2,1,0:T(2,128)} %shard_map.208), calls=%async_computation.3 | async-start | bytes 16384 | tf_op jit(solution)/shard_map/all_to_all | solution.py:344
  136.1 1.1 shard_map.207
  137.2 3.5 %all-to-all-done.3.in_ref = f32[8,2,128]{2,1,0:T(2,128)S(1)} async-done(((f32[8,2,128]{2,1,0:T(2,128)}), f32[8,2,128]{2,1,0:T(2,128)S(1)}, u32[]{:S(2)}, u32[]{:S(2)}) %all-to-all-start.3) | async-done | bytes 8224 | tf_op jit(solution)/shard_map/all_to_all | solution.py:344
  140.7 0.5 shard_map.209
Async XLA Ops:
  60.4 27.0 %all-to-all-start.1 = ((bf16[128,3,2,128]{3,2,1,0:T(2,128)(2,1)}), bf16[128,3,2,128]{3,2,1,0:T(2,128)(2,1)S(1)}, u32[]{:S(2)}, u32[]{:S(2)}) async-start(bf16[128,3,2,128]{3,2,1,0:T(2,128)(2,1)} %bitcast.20), calls=%async_computation.1 | async-start | bytes 393216 | tf_op jit(solution)/shard_map/all_to_all | solution.py:274
  69.4 0.7 copy-start.5
  69.4 0.7 copy-start.6
  69.4 0.7 copy-start.7
  70.1 17.3 %copy-start = (bf16[1,1,128,576]{2,3,1,0:T(8,128)(2,1)S(1)}, bf16[1,1,128,576]{2,3,1,0:T(8,128)(2,1)}, u32[]{:S(2)}) copy-start(bf16[1,1,128,576]{2,3,1,0:T(8,128)(2,1)} %param.12) | copy-start | bytes 442372
  70.1 17.3 %copy-start.1 = (bf16[1,1,128,576]{2,3,1,0:T(8,128)(2,1)S(1)}, bf16[1,1,128,576]{2,3,1,0:T(8,128)(2,1)}, u32[]{:S(2)}) copy-start(bf16[1,1,128,576]{2,3,1,0:T(8,128)(2,1)} %param.13) | copy-start | bytes 442372
  70.1 17.3 %copy-start.2 = (bf16[1,1,128,576]{2,3,1,0:T(8,128)(2,1)S(1)}, bf16[1,1,128,576]{2,3,1,0:T(8,128)(2,1)}, u32[]{:S(2)}) copy-start(bf16[1,1,128,576]{2,3,1,0:T(8,128)(2,1)} %param.14) | copy-start | bytes 442372
  87.3 0.7 copy-start.3
  87.3 0.7 copy-start.4
  130.6 10.1 %all-to-all-start.3 = ((f32[8,2,128]{2,1,0:T(2,128)}), f32[8,2,128]{2,1,0:T(2,128)S(1)}, u32[]{:S(2)}, u32[]{:S(2)}) async-start(f32[8,2,128]{2,1,0:T(2,128)} %shard_map.208), calls=%async_computation.3 | async-start | bytes 16384 | tf_op jit(solution)/shard_map/all_to_all | solution.py:344

commit v3 on v2

v3 whole, which is shorter than its diff:
```python
import jax
import jax.numpy as jnp
from jax import lax
from jax.experimental import pallas as pl
from jax.experimental.pallas import tpu as pltpu
from jax.sharding import Mesh
from jax.sharding import PartitionSpec as P

HEADS = 8
HEAD_DIM = 72
INNER = 576
TOKENS = 128
SCALE = HEAD_DIM ** (-0.5)
EPS = 1e-06
BF = jnp.bfloat16
F32 = jnp.float32
MIB = 1024 * 1024


def dot(left, right, left_dim, right_dim):
    return lax.dot_general(
        left, right, (((left_dim,), (right_dim,)), ((), ())), preferred_element_type=F32
    )


def pack(features, tiles, out_ref):
    size = 16 * tiles
    row = lax.broadcasted_iota(jnp.int32, (size, size), 0)
    col = lax.broadcasted_iota(jnp.int32, (size, size), 1)
    order = (row == (col & 15) * tiles + (col >> 4)).astype(F32).astype(BF)
    stacked = []
    for tile in range(tiles):
        turned = features[128 * tile : 128 * tile + 128, :].T
        stacked.append(
            jnp.concatenate([turned[16 * b : 16 * b + 16, :] for b in range(8)], axis=1)
        )
    mixed = dot(order, jnp.concatenate(stacked, axis=0), 1, 0).astype(BF)
    for b in range(8):
        out_ref[size * b : size * b + size, :] = mixed[:, 128 * b : 128 * b + 128]


def unpack(in_ref, tiles, wanted=None):
    wanted = wanted or tiles
    size = 16 * tiles
    row = lax.broadcasted_iota(jnp.int32, (16 * wanted, size), 0)
    col = lax.broadcasted_iota(jnp.int32, (16 * wanted, size), 1)
    order = (col == (row & 15) * tiles + (row >> 4)).astype(F32).astype(BF)
    blocks = jnp.concatenate(
        [in_ref[size * b : size * b + size, :] for b in range(8)], axis=1
    )
    mixed = dot(order, blocks, 1, 0).astype(BF)
    turned = []
    for tile in range(wanted):
        rows = mixed[16 * tile : 16 * tile + 16, :]
        turned.append(
            jnp.concatenate([rows[:, 128 * b : 128 * b + 128] for b in range(8)], axis=0).T
        )
    return jnp.concatenate(turned, axis=0)


def column(gain_ref):
    row = lax.broadcasted_iota(jnp.int32, (HEAD_DIM, HEAD_DIM), 0)
    col = lax.broadcasted_iota(jnp.int32, (HEAD_DIM, HEAD_DIM), 1)
    spread = jnp.where(row == col, gain_ref[...], 0.0)
    return jnp.sum(spread, axis=1, keepdims=True)


def normed(values, gain):
    floats = values.astype(F32).reshape(HEADS, HEAD_DIM, TOKENS)
    inverse = lax.rsqrt(jnp.mean(floats * floats, axis=1, keepdims=True) + EPS)
    unit = floats * inverse
    return unit, inverse, (unit * gain[None]).astype(BF)


def normed_back(cotangent, unit, inverse, gain):
    scaled = cotangent * gain[None]
    along = jnp.mean(scaled * unit, axis=1, keepdims=True)
    return (inverse * (scaled - unit * along)).reshape(INNER, TOKENS).astype(BF)


def gain_terms(cotangent, unit):
    return jnp.sum(jnp.sum(cotangent * unit, axis=0), axis=1, keepdims=True)


def probabilities(query, key_in, same):
    weights = jnp.exp(dot(key_in, query, 0, 0) * SCALE)
    if same is not None:
        weights = weights * same
    return weights * (1.0 / jnp.sum(weights, axis=0, keepdims=True))


def scores_back(probs, value, cotangent):
    grad_probs = dot(value, cotangent, 0, 0)
    along = jnp.sum(probs * grad_probs, axis=0, keepdims=True)
    return (probs * (grad_probs - along) * SCALE).astype(BF)


def head(values, index):
    return values[HEAD_DIM * index : HEAD_DIM * (index + 1), :]


def by_head(parts):
    return jnp.stack([part.astype(BF).astype(F32) for part in parts])


def load(sources, buffers, sems):
    copies = [
        pltpu.make_async_copy(source, buffer, sems.at[i])
        for i, (source, buffer) in enumerate(zip(sources, buffers))
    ]
    for copy in copies:
        copy.start()
    return copies


def send_kernel(*refs):
    sources, (out_ref, *buffers, sems) = refs[:9], refs[9:]
    copies = load(sources, buffers, sems)
    gain_q, gain_k, sq, sk, sv, tq, tk, og, tv_in = buffers
    for copy in copies[:4]:
        copy.wait()
    _, _, query = normed(sq[...], column(gain_q))
    _, _, key_in = normed(sk[...], column(gain_k))
    for copy in copies[4:]:
        copy.wait()
    value = sv[...]
    mixed = []
    for h in range(HEADS):
        probs = probabilities(query[h], key_in[h], None).astype(BF)
        mixed.append(dot(head(value, h), probs, 1, 0))
    spatial = jnp.concatenate(mixed, axis=0).astype(BF)
    total = (tv_in[...].astype(F32) + spatial.astype(F32)).astype(BF)
    pack(jnp.concatenate([tq[...], tk[...], og[...], total], axis=0), 18, out_ref)


def same_video(ids):
    ids = jnp.broadcast_to(ids.astype(F32), (TOKENS, TOKENS))
    return (ids == ids.T).astype(F32)


def temporal_kernel(in_ref, ids_hbm, gain_q_hbm, gain_k_hbm, out_ref, gains_ref, ids, gain_q, gain_k, sems):
    copies = load((ids_hbm, gain_q_hbm, gain_k_hbm), (ids, gain_q, gain_k), sems)
    arrays = unpack(in_ref, 18)
    tq, tk, og, tv = (arrays[INNER * i : INNER * (i + 1), :] for i in range(4))
    for copy in copies:
        copy.wait()
    column_q, column_k = column(gain_q), column(gain_k)
    unit_q, inverse_q, query = normed(tq, column_q)
    unit_k, inverse_k, key_in = normed(tk, column_k)
    same = same_video(ids[...])
    mixed, grads_q, grads_k, grads_v = [], [], [], []
    for h in range(HEADS):
        probs = probabilities(query[h], key_in[h], same)
        rounded = probs.astype(BF)
        value, cotangent = head(tv, h), head(og, h)
        mixed.append(dot(value, rounded, 1, 0))
        grads_v.append(dot(cotangent, rounded, 1, 1))
        scores = scores_back(probs, value, cotangent)
        grads_q.append(dot(key_in[h], scores, 1, 0))
        grads_k.append(dot(query[h], scores, 1, 1))
    out = jnp.concatenate(mixed, axis=0).astype(BF)
    grad_v = jnp.concatenate(grads_v, axis=0).astype(BF)
    grads_q, grads_k = by_head(grads_q), by_head(grads_k)
    gains_ref[...] = gain_terms(grads_q, unit_q)
    grad_q = normed_back(grads_q, unit_q, inverse_q, column_q)
    grad_k = normed_back(grads_k, unit_k, inverse_k, column_k)
    pack(jnp.concatenate([grad_v, out, grad_q, grad_k], axis=0), 18, out_ref)


def spatial_again_kernel(sq, sk, gain_q, gain_k, unit_q, unit_k, inverse_q, inverse_k, query, key_in, probs):
    unit_q[...], inverse_q[...], query[...] = normed(sq[...], column(gain_q))
    unit_k[...], inverse_k[...], key_in[...] = normed(sk[...], column(gain_k))
    for h in range(HEADS):
        probs[h] = probabilities(query[h], key_in[h], None)


def spatial_gain_kernel(in_ref, sv, unit_q, key_in, probs, temporal, grads_q, scores, out_ref):
    given = unpack(in_ref, 18, 5)
    for h in range(HEADS):
        scores[h] = scores_back(probs[h], head(sv, h), head(given, h))
        grads_q[h] = dot(key_in[h], scores[h], 1, 0).astype(BF)
    total = gain_terms(grads_q[...].astype(F32), unit_q[...])
    both = jnp.concatenate(
        [jnp.broadcast_to(t, (HEAD_DIM, 128)) for t in (total, temporal[...])], axis=0
    )
    both = jnp.concatenate([both, jnp.zeros((112, 128), F32)], axis=0)
    first, second = both[:128, :].T[:1, :], both[128:, :].T[:1, :]
    rows = jnp.concatenate([first, second], axis=0)
    out_ref[...] = jnp.broadcast_to(rows[None], out_ref.shape)


def spatial_rest_kernel(
    in_ref, unit_q, unit_k, inverse_q, inverse_k, query, probs, grads_q, scores, gain_q, gain_k,
    out, grad_tq, grad_tk, grad_tv, grad_sq, grad_sk, grad_sv
):
    arrays = unpack(in_ref, 18)
    grad_tv[...], out[...], grad_tq[...], grad_tk[...] = (
        arrays[INNER * i : INNER * (i + 1), :] for i in range(4)
    )
    grads_k, grads_v = [], []
    for h in range(HEADS):
        grads_k.append(dot(query[h], scores[h], 1, 1))
        grads_v.append(dot(head(arrays, h), probs[h].astype(BF), 1, 1))
    grad_sv[...] = jnp.concatenate(grads_v, axis=0).astype(BF)
    grad_sq[...] = normed_back(
        grads_q[...].astype(F32), unit_q[...], inverse_q[...], column(gain_q)
    )
    grad_sk[...] = normed_back(by_head(grads_k), unit_k[...], inverse_k[...], column(gain_k))


def gain_middle_kernel(in_ref, out_ref):
    out_ref[...] = jnp.broadcast_to(jnp.sum(in_ref[...], axis=0, keepdims=True), out_ref.shape)


def gain_last_kernel(in_ref, sq_gain, sk_gain, tq_gain, tk_gain, grad_sq, grad_sk, grad_tq, grad_tk):
    total = jnp.sum(in_ref[...], axis=0)
    spatial = total[:1, :HEAD_DIM]
    temporal = jnp.concatenate([total[:1, HEAD_DIM:], total[1:, : 2 * HEAD_DIM - 128]], axis=1)
    grad_sq[...] = spatial
    grad_sk[...] = spatial * (sq_gain[...] / sk_gain[...])
    grad_tq[...] = temporal
    grad_tk[...] = temporal * (tq_gain[...] / tk_gain[...])


def shape(*extent, dtype=BF):
    return jax.ShapeDtypeStruct(extent, dtype)


def call(kernel, out_shape, *args, in_hbm=0, scratch=(), work=0, vmem=32):
    specs = [pl.BlockSpec(memory_space=pltpu.VMEM)] * (len(args) - in_hbm)
    specs += [pl.BlockSpec(memory_space=pltpu.HBM)] * in_hbm
    split = len(args) - in_hbm
    args = args[:split] + tuple(
        pltpu.with_memory_space_constraint(a, pltpu.HBM) for a in args[split:]
    )
    cost = pl.CostEstimate(flops=work, bytes_accessed=0, transcendentals=0) if work else None
    return pl.pallas_call(
        kernel,
        out_shape=out_shape,
        in_specs=specs,
        scratch_shapes=scratch,
        compiler_params=pltpu.CompilerParams(vmem_limit_bytes=vmem * MIB),
        cost_estimate=cost,
    )(*args)


def buffers(*arrays):
    return [pltpu.VMEM(a.shape, a.dtype) for a in arrays] + [pltpu.SemaphoreType.DMA((len(arrays),))]


def exchange(message, axes, tiles):
    parts = message.reshape(TOKENS, tiles // 2, 2, 128)
    parts = lax.all_to_all(parts, axes, split_axis=0, concat_axis=0, tiled=True)
    return parts.reshape(TOKENS * tiles, 128)


def shards(
    spatial_query,
    spatial_key,
    spatial_value,
    temporal_query,
    temporal_key,
    temporal_value_in,
    out_grad,
    video_ids,
    spatial_query_gain,
    spatial_key_gain,
    temporal_query_gain,
    temporal_key_gain,
):
    sq, sk, sv, tq, tk, tv_in, og = (
        a.reshape(TOKENS, INNER).T
        for a in (
            spatial_query,
            spatial_key,
            spatial_value,
            temporal_query,
            temporal_key,
            temporal_value_in,
            out_grad,
        )
    )
    sq_gain, sk_gain, tq_gain, tk_gain = (
        g.reshape(1, HEAD_DIM)
        for g in (spatial_query_gain, spatial_key_gain, temporal_query_gain, temporal_key_gain)
    )
    seq = ("z", "y", "core")
    array = shape(INNER, TOKENS)
    args = (sq_gain, sk_gain, sq, sk, sv, tq, tk, og, tv_in)
    sent = call(send_kernel, shape(2304, 128), *args, in_hbm=9, scratch=buffers(*args))
    arrived = exchange(sent, seq, 18)
    args = (video_ids, tq_gain, tk_gain)
    sent, temporal = call(
        temporal_kernel,
        (shape(2304, 128), shape(HEAD_DIM, 1, dtype=F32)),
        arrived,
        *args,
        in_hbm=3,
        scratch=buffers(*args),
    )
    arrived = exchange(sent, seq, 18)
    unit, inverse = shape(HEADS, HEAD_DIM, TOKENS, dtype=F32), shape(HEADS, 1, TOKENS, dtype=F32)
    normal = shape(HEADS, HEAD_DIM, TOKENS)
    unit_q, unit_k, inverse_q, inverse_k, query, key_in, probs = call(
        spatial_again_kernel,
        (unit, unit, inverse, inverse, normal, normal, shape(HEADS, 128, 128, dtype=F32)),
        sq,
        sk,
        sq_gain,
        sk_gain,
        work=2_000_000_000,
    )
    grads_q, scores, gains = call(
        spatial_gain_kernel,
        (normal, shape(HEADS, 128, 128), shape(16, 2, 128, dtype=F32)),
        arrived,
        sv,
        unit_q,
        key_in,
        probs,
        temporal,
    )
    gains = lax.all_to_all(gains, "z", split_axis=0, concat_axis=0, tiled=True)
    out, grad_tq, grad_tk, grad_tv, grad_sq, grad_sk, grad_sv = call(
        spatial_rest_kernel,
        (array,) * 7,
        arrived,
        unit_q,
        unit_k,
        inverse_q,
        inverse_k,
        query,
        probs,
        grads_q,
        scores,
        sq_gain,
        sk_gain,
        work=3_000_000_000,
    )
    gains = call(gain_middle_kernel, shape(32, 2, 128, dtype=F32), gains)
    gains = lax.all_to_all(gains, ("core", "y", "dp"), split_axis=0, concat_axis=0, tiled=True)
    gains = call(
        gain_last_kernel,
        (shape(1, HEAD_DIM, dtype=F32),) * 4,
        gains,
        sq_gain,
        sk_gain,
        tq_gain,
        tk_gain,
    )
    results = (out, grad_sq, grad_sk, grad_sv, grad_tq, grad_tk, grad_tv)
    return tuple(a.T.reshape(1, 1, TOKENS, INNER) for a in results) + tuple(
        g.reshape(HEAD_DIM) for g in gains
    )


def solution(mesh):
    fine = Mesh(mesh.devices.reshape(4, 16, 4, 2), ("dp", "z", "y", "core"))
    tokens = P("dp", ("z", "y", "core"), None, None)
    return jax.shard_map(
        shards,
        mesh=fine,
        in_specs=(tokens,) * 7 + (P("dp", None),) + (P(),) * 4,
        out_specs=(tokens,) * 7 + (P(),) * 4,
        check_vma=False,
    )
```

time: 142 us -> 140 us (0.986)
  blocking collectives: 92.8 us -> 71.4 us
  waiting for transfers between devices: 18.2 us -> 38.4 us
  starting transfers between devices: 14.5 us -> 16.3 us
    all_to_all x2 -> x1, blocking collectives: 92.8 us -> 54.1 us  [exchange(): parts = lax.all_to_all(parts, axes, split_axis=0, concat_axis=0, tiled=True)]
    all_to_all x1, waiting for transfers between devices: 14.6 us -> 33.2 us  [exchange(): parts = lax.all_to_all(parts, axes, split_axis=0, concat_axis=0, tiled=True)]
    all_to_all x0 -> x1, blocking collectives: none -> 17.3 us  [shards(): gains = lax.all_to_all(gains, 'z', split_axis=0, concat_axis=0, tiled=True)]
    all_to_all x1, starting transfers between devices: 5.5 us -> 7.21 us  [shards(): lax.all_to_all(gains, ('core', 'y', 'dp'), split_axis=0, concat_axis=0, t...]
    all_to_all x1, waiting for transfers between devices: 3.53 us -> 5.21 us  [shards(): lax.all_to_all(gains, ('core', 'y', 'dp'), split_axis=0, concat_axis=0, t...]
  transfers between devices with their start and end apart: 2 -> 2, of which waited for: 2 -> 2; matrix products, arithmetic and copies ran while one was open for 0% -> 0% of each run, Pallas kernels for 3% -> 2%
where the time goes in v3:
time: 140 us
  blocking collectives  71.4 us (51%)
  waiting for transfers between devices  38.4 us (27%)
  starting transfers between devices  16.3 us (12%)
  Pallas kernels  13 us (9%)
    all_to_all x1, blocking collectives, exchange(): parts = lax.all_to_all(parts, axes, split_axis=0, concat_axis=0, tiled=True)  54.1 us
    all_to_all x1, waiting for transfers between devices, exchange(): parts = lax.all_to_all(parts, axes, split_axis=0, concat_axis=0, tiled=True)  33.2 us
    all_to_all x1, blocking collectives, shards(): gains = lax.all_to_all(gains, 'z', split_axis=0, concat_axis=0, tiled=True)  17.3 us
    pallas_call x7, Pallas kernels, call(): pl.pallas_call(kernel, out_shape=out_shape, in_specs=specs, scratch_shape...  13 us
    all_to_all x1, starting transfers between devices, exchange(): parts = lax.all_to_all(parts, axes, split_axis=0, concat_axis=0, tiled=True)  9.13 us
    all_to_all x1, starting transfers between devices, shards(): lax.all_to_all(gains, ('core', 'y', 'dp'), split_axis=0, concat_axis=0, t...  7.21 us
    all_to_all x1, waiting for transfers between devices, shards(): lax.all_to_all(gains, ('core', 'y', 'dp'), split_axis=0, concat_axis=0, t...  5.21 us
  transfers between devices with their start and end apart: 2, of which 2 were waited for; matrix products, arithmetic and copies ran while one was open for 0% of the time, Pallas kernels for 2%

profile of v3, /device:TPU:1, one launch (start us, length us, event | category | flops | bytes accessed | tf_op | source)
XLA Modules:
  0.0 139.9 jit_solution(16229074713150035839)
XLA Ops:
  0.6 2.7 %shard_map.203 = bf16[2304,128]{1,0:T(8,128)(2,1)S(1)} custom-call(f32[1,72]{1,0:T(1,128)} %bitcast.64, f32[1,72]{1,0:T(1,128)} %bitcast.68, bf16[576,128]{1,0:T(8,128)(2,1)} %bitcast.60, bf16[576,128]{1,0:T(8,128)(2,1)} %bitcast.62, bf16[576,128]{1,0:T(8,128)(2,1)} %bitcast.58, bf16[576,128]{1,0:T(8,128)(2,1)} %bitcast.76, bf16[576,128]{1,0:T(8,128)(2,1)} %bitcast.77, ...), custom_call_target="tpu_custom_call" | custom-call | tf_op jit(solution)/shard_map/pallas_call | solution.py:237
  3.3 54.1 %all_to_all.20 = bf16[128,9,2,128]{3,2,1,0:T(2,128)(2,1)S(1)} all-to-all(bf16[128,9,2,128]{3,2,1,0:T(2,128)(2,1)S(1)} %bitcast.57), channel_id=1, replica_groups=mesh['dp'=4,'z'=16,'y'=4,'core'=2] {'z','y','core'}, dimensions={0} | all-to-all | bytes 1179648 | tf_op jit(solution)/shard_map/all_to_all | solution.py:253
  57.4 5.7 %shard_map.204 = (bf16[2304,128]{1,0:T(8,128)(2,1)}, f32[72,1]{1,0:T(8,128)S(1)}) custom-call(bf16[2304,128]{1,0:T(8,128)(2,1)S(1)} %bitcast.56, s32[1,128]{1,0:T(1,128)} %ids_hbm.1, f32[1,72]{1,0:T(1,128)} %bitcast.72, f32[1,72]{1,0:T(1,128)} %bitcast.74), custom_call_target="tpu_custom_call" | custom-call | tf_op jit(solution)/shard_map/pallas_call | solution.py:237
  63.1 0.0 copy-start.1
  63.1 0.0 copy-start.2
  63.1 0.0 copy-start.3
  63.1 0.0 copy-start.4
  63.1 9.1 %all-to-all-start.1 = ((bf16[128,9,2,128]{3,2,1,0:T(2,128)(2,1)}), bf16[128,9,2,128]{3,2,1,0:T(2,128)(2,1)S(1)}, u32[]{:S(2)}, u32[]{:S(2)}) async-start(bf16[128,9,2,128]{3,2,1,0:T(2,128)(2,1)} %bitcast.20), calls=%async_computation.1 | async-start | bytes 1179648 | tf_op jit(solution)/shard_map/all_to_all | solution.py:253
  72.3 0.0 copy-done.1
  72.3 0.0 copy-done.2
  72.3 0.0 copy-done.3
  72.3 0.0 copy-done.4
  72.3 0.0 copy-start
  72.3 0.5 shard_map.205
  72.8 33.2 %all-to-all-done.1 = bf16[128,9,2,128]{3,2,1,0:T(2,128)(2,1)S(1)} async-done(((bf16[128,9,2,128]{3,2,1,0:T(2,128)(2,1)}), bf16[128,9,2,128]{3,2,1,0:T(2,128)(2,1)S(1)}, u32[]{:S(2)}, u32[]{:S(2)}) %all-to-all-start.1) | async-done | bytes 589856 | tf_op jit(solution)/shard_map/all_to_all | solution.py:253
  106.0 0.0 copy-done
  106.0 1.2 shard_map.206
  107.2 17.3 %all_to_all.21.in_ref = f32[16,2,128]{2,1,0:T(2,128)S(1)} all-to-all(f32[16,2,128]{2,1,0:T(2,128)S(1)} %get-tuple-element.52), channel_id=1, replica_groups=mesh['dp'=4,'z'=16,'y'=4,'core'=2] {'z'}, dimensions={0} | all-to-all | bytes 32768 | tf_op jit(solution)/shard_map/all_to_all | solution.py:323
  124.5 0.6 shard_map.208
  125.1 7.2 %all-to-all-start.3 = ((f32[32,2,128]{2,1,0:T(2,128)}), f32[32,2,128]{2,1,0:T(2,128)S(1)}, u32[]{:S(2)}, u32[]{:S(2)}) async-start(f32[32,2,128]{2,1,0:T(2,128)} %shard_map.208), calls=%async_computation.3 | async-start | bytes 65536 | tf_op jit(solution)/shard_map/all_to_all | solution.py:341
  132.3 0.0 copy-start.5
  132.3 0.0 copy-start.6
  132.4 1.8 %shard_map.207 = (bf16[576,128]{1,0:T(8,128)(2,1)}, bf16[576,128]{1,0:T(8,128)(2,1)}, bf16[576,128]{1,0:T(8,128)(2,1)}, bf16[576,128]{1,0:T(8,128)(2,1)}, bf16[5...) custom-call(bf16[2304,128]{1,0:T(8,128)(2,1)S(1)} %bitcast.55, ...), custom_call_target="tpu_custom_call" | custom-call | flops 3000000000 | tf_op jit(solution)/shard_map/pallas_call | solution.py:237
  134.1 5.2 %all-to-all-done.3.in_ref = f32[32,2,128]{2,1,0:T(2,128)S(1)} async-done(((f32[32,2,128]{2,1,0:T(2,128)}), f32[32,2,128]{2,1,0:T(2,128)S(1)}, u32[]{:S(2)}, u32[]{:S(2)}) %all-to-all-start.3) | async-done | bytes 32800 | tf_op jit(solution)/shard_map/all_to_all | solution.py:341
  139.3 0.0 copy-done.5
  139.3 0.0 copy-done.6
  139.3 0.6 shard_map.209
Async XLA Ops:
  63.1 9.2 %copy-start.1 = (bf16[1,1,128,576]{2,3,1,0:T(8,128)(2,1)S(1)}, bf16[1,1,128,576]{2,3,1,0:T(8,128)(2,1)}, u32[]{:S(2)}) copy-start(bf16[1,1,128,576]{2,3,1,0:T(8,128)(2,1)} %param.12) | copy-start | bytes 442372
  63.1 9.2 %copy-start.2 = (bf16[1,1,128,576]{2,3,1,0:T(8,128)(2,1)S(1)}, bf16[1,1,128,576]{2,3,1,0:T(8,128)(2,1)}, u32[]{:S(2)}) copy-start(bf16[1,1,128,576]{2,3,1,0:T(8,128)(2,1)} %param.13) | copy-start | bytes 442372
  63.1 9.2 %copy-start.3 = (f32[72]{0:T(128)S(1)}, f32[72]{0:T(128)}, u32[]{:S(2)}) copy-start(f32[72]{0:T(128)} %param.20) | copy-start | bytes 868
  63.1 9.2 %copy-start.4 = (f32[72]{0:T(128)S(1)}, f32[72]{0:T(128)}, u32[]{:S(2)}) copy-start(f32[72]{0:T(128)} %param.21) | copy-start | bytes 868
  63.1 42.8 %all-to-all-start.1 = ((bf16[128,9,2,128]{3,2,1,0:T(2,128)(2,1)}), bf16[128,9,2,128]{3,2,1,0:T(2,128)(2,1)S(1)}, u32[]{:S(2)}, u32[]{:S(2)}) async-start(bf16[128,9,2,128]{3,2,1,0:T(2,128)(2,1)} %bitcast.20), calls=%async_computation.1 | async-start | bytes 1179648 | tf_op jit(solution)/shard_map/all_to_all | solution.py:253
  72.3 33.7 %copy-start = (bf16[1,1,128,576]{2,3,1,0:T(8,128)(2,1)S(1)}, bf16[1,1,128,576]{2,3,1,0:T(8,128)(2,1)}, u32[]{:S(2)}) copy-start(bf16[1,1,128,576]{2,3,1,0:T(8,128)(2,1)} %param.14) | copy-start | bytes 442372
  125.1 14.2 %all-to-all-start.3 = ((f32[32,2,128]{2,1,0:T(2,128)}), f32[32,2,128]{2,1,0:T(2,128)S(1)}, u32[]{:S(2)}, u32[]{:S(2)}) async-start(f32[32,2,128]{2,1,0:T(2,128)} %shard_map.208), calls=%async_computation.3 | async-start | bytes 65536 | tf_op jit(solution)/shard_map/all_to_all | solution.py:341
  132.3 7.0 %copy-start.5 = (f32[72]{0:T(128)S(1)}, f32[72]{0:T(128)}, u32[]{:S(2)}) copy-start(f32[72]{0:T(128)} %param.22) | copy-start | bytes 868
  132.3 7.0 %copy-start.6 = (f32[72]{0:T(128)S(1)}, f32[72]{0:T(128)}, u32[]{:S(2)}) copy-start(f32[72]{0:T(128)} %param.23) | copy-start | bytes 868

commit v4 on v3

--- a/solution.py
+++ b/solution.py
@@ -12,6 +12,7 @@
 TOKENS = 128
 SCALE = HEAD_DIM ** (-0.5)
 EPS = 1e-06
+EARLY = 192
 BF = jnp.bfloat16
 F32 = jnp.float32
 MIB = 1024 * 1024
@@ -39,8 +40,7 @@
         out_ref[size * b : size * b + size, :] = mixed[:, 128 * b : 128 * b + 128]
 
 
-def unpack(in_ref, tiles, wanted=None):
-    wanted = wanted or tiles
+def token_tiles(in_ref, tiles, wanted):
     size = 16 * tiles
     row = lax.broadcasted_iota(jnp.int32, (16 * wanted, size), 0)
     col = lax.broadcasted_iota(jnp.int32, (16 * wanted, size), 1)
@@ -49,13 +49,16 @@
         [in_ref[size * b : size * b + size, :] for b in range(8)], axis=1
     )
     mixed = dot(order, blocks, 1, 0).astype(BF)
-    turned = []
-    for tile in range(wanted):
-        rows = mixed[16 * tile : 16 * tile + 16, :]
-        turned.append(
-            jnp.concatenate([rows[:, 128 * b : 128 * b + 128] for b in range(8)], axis=0).T
+    return [
+        jnp.concatenate(
+            [mixed[16 * tile : 16 * tile + 16, 128 * b : 128 * b + 128] for b in range(8)], axis=0
         )
-    return jnp.concatenate(turned, axis=0)
+        for tile in range(wanted)
+    ]
+
+
+def unpack(in_ref, tiles, wanted=None):
+    return jnp.concatenate([t.T for t in token_tiles(in_ref, tiles, wanted or tiles)], axis=0)
 
 
 def column(gain_ref):
@@ -114,20 +117,20 @@
 
 
 def send_kernel(*refs):
-    sources, (out_ref, *buffers, sems) = refs[:9], refs[9:]
+    sources, (out_ref, unit_q, unit_k, inverse_q, inverse_k, query, key_in, probs) = refs[:9], refs[9:17]
+    buffers, sems = refs[17:-1], refs[-1]
     copies = load(sources, buffers, sems)
     gain_q, gain_k, sq, sk, sv, tq, tk, og, tv_in = buffers
     for copy in copies[:4]:
         copy.wait()
-    _, _, query = normed(sq[...], column(gain_q))
-    _, _, key_in = normed(sk[...], column(gain_k))
+    unit_q[...], inverse_q[...], query[...] = normed(sq[...], column(gain_q))
+    unit_k[...], inverse_k[...], key_in[...] = normed(sk[...], column(gain_k))
     for copy in copies[4:]:
         copy.wait()
-    value = sv[...]
     mixed = []
     for h in range(HEADS):
-        probs = probabilities(query[h], key_in[h], None).astype(BF)
-        mixed.append(dot(head(value, h), probs, 1, 0))
+        probs[h] = probabilities(query[h], key_in[h], None)
+        mixed.append(dot(head(sv, h), probs[h].astype(BF), 1, 0))
     spatial = jnp.concatenate(mixed, axis=0).astype(BF)
     total = (tv_in[...].astype(F32) + spatial.astype(F32)).astype(BF)
     pack(jnp.concatenate([tq[...], tk[...], og[...], total], axis=0), 18, out_ref)
@@ -138,7 +141,9 @@
     return (ids == ids.T).astype(F32)
 
 
-def temporal_kernel(in_ref, ids_hbm, gain_q_hbm, gain_k_hbm, out_ref, gains_ref, ids, gain_q, gain_k, sems):
+def temporal_kernel(
+    in_ref, ids_hbm, gain_q_hbm, gain_k_hbm, out_ref, later_ref, gains_ref, ids, gain_q, gain_k, sems
+):
     copies = load((ids_hbm, gain_q_hbm, gain_k_hbm), (ids, gain_q, gain_k), sems)
     arrays = unpack(in_ref, 18)
     tq, tk, og, tv = (arrays[INNER * i : INNER * (i + 1), :] for i in range(4))
@@ -164,18 +169,12 @@
     gains_ref[...] = gain_terms(grads_q, unit_q)
     grad_q = normed_back(grads_q, unit_q, inverse_q, column_q)
     grad_k = normed_back(grads_k, unit_k, inverse_k, column_k)
-    pack(jnp.concatenate([grad_v, out, grad_q, grad_k], axis=0), 18, out_ref)
-
-
-def spatial_again_kernel(sq, sk, gain_q, gain_k, unit_q, unit_k, inverse_q, inverse_k, query, key_in, probs):
-    unit_q[...], inverse_q[...], query[...] = normed(sq[...], column(gain_q))
-    unit_k[...], inverse_k[...], key_in[...] = normed(sk[...], column(gain_k))
-    for h in range(HEADS):
-        probs[h] = probabilities(query[h], key_in[h], None)
+    later_ref[...] = jnp.concatenate([out[EARLY:, :], grad_q, grad_k], axis=0)
+    pack(jnp.concatenate([grad_v, out[:EARLY, :]], axis=0), 6, out_ref)
 
 
 def spatial_gain_kernel(in_ref, sv, unit_q, key_in, probs, temporal, grads_q, scores, out_ref):
-    given = unpack(in_ref, 18, 5)
+    given = unpack(in_ref, 6, 5)
     for h in range(HEADS):
         scores[h] = scores_back(probs[h], head(sv, h), head(given, h))
         grads_q[h] = dot(key_in[h], scores[h], 1, 0).astype(BF)
@@ -184,19 +183,16 @@
         [jnp.broadcast_to(t, (HEAD_DIM, 128)) for t in (total, temporal[...])], axis=0
     )
     both = jnp.concatenate([both, jnp.zeros((112, 128), F32)], axis=0)
-    first, second = both[:128, :].T[:1, :], both[128:, :].T[:1, :]
-    rows = jnp.concatenate([first, second], axis=0)
+    rows = jnp.concatenate([both[:128, :].T[:1, :], both[128:, :].T[:1, :]], axis=0)
     out_ref[...] = jnp.broadcast_to(rows[None], out_ref.shape)
 
 
 def spatial_rest_kernel(
-    in_ref, unit_q, unit_k, inverse_q, inverse_k, query, probs, grads_q, scores, gain_q, gain_k,
-    out, grad_tq, grad_tk, grad_tv, grad_sq, grad_sk, grad_sv
+    in_ref, later, unit_q, unit_k, inverse_q, inverse_k, query, probs, grads_q, scores, gain_q, gain_k,
+    message, out_early, grad_tv, grad_sq, grad_sk, grad_sv
 ):
-    arrays = unpack(in_ref, 18)
-    grad_tv[...], out[...], grad_tq[...], grad_tk[...] = (
-        arrays[INNER * i : INNER * (i + 1), :] for i in range(4)
-    )
+    arrays = unpack(in_ref, 6)
+    grad_tv[...], out_early[...] = arrays[:INNER, :], arrays[INNER:, :]
     grads_k, grads_v = [], []
     for h in range(HEADS):
         grads_k.append(dot(query[h], scores[h], 1, 1))
@@ -206,20 +202,38 @@
         grads_q[...].astype(F32), unit_q[...], inverse_q[...], column(gain_q)
     )
     grad_sk[...] = normed_back(by_head(grads_k), unit_k[...], inverse_k[...], column(gain_k))
-
-
-def gain_middle_kernel(in_ref, out_ref):
-    out_ref[...] = jnp.broadcast_to(jnp.sum(in_ref[...], axis=0, keepdims=True), out_ref.shape)
-
-
-def gain_last_kernel(in_ref, sq_gain, sk_gain, tq_gain, tk_gain, grad_sq, grad_sk, grad_tq, grad_tk):
-    total = jnp.sum(in_ref[...], axis=0)
-    spatial = total[:1, :HEAD_DIM]
-    temporal = jnp.concatenate([total[:1, HEAD_DIM:], total[1:, : 2 * HEAD_DIM - 128]], axis=1)
-    grad_sq[...] = spatial
-    grad_sk[...] = spatial * (sq_gain[...] / sk_gain[...])
-    grad_tq[...] = temporal
-    grad_tk[...] = temporal * (tq_gain[...] / tk_gain[...])
+    pack(jnp.concatenate([later[...], jnp.zeros((256, TOKENS), BF)], axis=0), 14, message)
+
+
+def fill_kernel(gains, message, out_ref):
+    total = jnp.sum(gains[...], axis=0)
+    high = total.astype(BF).astype(F32)
+    part = jnp.where(lax.axis_index("core") == 0, high, total - high)
+    row = lax.broadcasted_iota(jnp.int32, (224, 128), 0)
+    place = row - 14 * ((row * 4682) >> 16)
+    block = jnp.where(place == 12, part[:1, :], part[1:, :])
+    for b in range(8):
+        rows = message[224 * b : 224 * b + 224, :].astype(F32)
+        out_ref[224 * b : 224 * b + 224, :] = jnp.where(place >= 12, block, rows).astype(BF)
+
+
+def last_kernel(
+    in_ref, out_early, sq_gain, sk_gain, tq_gain, tk_gain,
+    out, grad_tq, grad_tk, grad_sq_gain, grad_sk_gain, grad_tq_gain, grad_tk_gain
+):
+    tiles = token_tiles(in_ref, 14, 14)
+    first, second = (jnp.sum(t.astype(F32), axis=0, keepdims=True) for t in tiles[12:])
+    spatial = first[:, :HEAD_DIM]
+    temporal = jnp.concatenate([first[:, HEAD_DIM:], second[:, : 2 * HEAD_DIM - 128]], axis=1)
+    grad_sq_gain[...] = spatial
+    grad_sk_gain[...] = spatial * (sq_gain[...] / sk_gain[...])
+    grad_tq_gain[...] = temporal
+    grad_tk_gain[...] = temporal * (tq_gain[...] / tk_gain[...])
+    arrays = jnp.concatenate([t.T for t in tiles[:12]], axis=0)
+    rest = INNER - EARLY
+    out[...] = jnp.concatenate([out_early[...], arrays[:rest, :]], axis=0)
+    grad_tq[...] = arrays[rest : rest + INNER, :]
+    grad_tk[...] = arrays[rest + INNER :, :]
 
 
 def shape(*extent, dtype=BF):
@@ -287,32 +301,29 @@
     seq = ("z", "y", "core")
     array = shape(INNER, TOKENS)
     args = (sq_gain, sk_gain, sq, sk, sv, tq, tk, og, tv_in)
-    sent = call(send_kernel, shape(2304, 128), *args, in_hbm=9, scratch=buffers(*args))
+    unit, inverse = shape(HEADS, HEAD_DIM, TOKENS, dtype=F32), shape(HEADS, 1, TOKENS, dtype=F32)
+    normal, square = shape(HEADS, HEAD_DIM, TOKENS), shape(HEADS, 128, 128)
+    sent, unit_q, unit_k, inverse_q, inverse_k, query, key_in, probs = call(
+        send_kernel,
+        (shape(2304, 128), unit, unit, inverse, inverse, normal, normal, shape(HEADS, 128, 128, dtype=F32)),
+        *args,
+        in_hbm=9,
+        scratch=buffers(*args),
+    )
     arrived = exchange(sent, seq, 18)
     args = (video_ids, tq_gain, tk_gain)
-    sent, temporal = call(
+    sent, later, temporal = call(
         temporal_kernel,
-        (shape(2304, 128), shape(HEAD_DIM, 1, dtype=F32)),
+        (shape(768, 128), shape(1536, 128), shape(HEAD_DIM, 1, dtype=F32)),
         arrived,
         *args,
         in_hbm=3,
         scratch=buffers(*args),
     )
-    arrived = exchange(sent, seq, 18)
-    unit, inverse = shape(HEADS, HEAD_DIM, TOKENS, dtype=F32), shape(HEADS, 1, TOKENS, dtype=F32)
-    normal = shape(HEADS, HEAD_DIM, TOKENS)
-    unit_q, unit_k, inverse_q, inverse_k, query, key_in, probs = call(
-        spatial_again_kernel,
-        (unit, unit, inverse, inverse, normal, normal, shape(HEADS, 128, 128, dtype=F32)),
-        sq,
-        sk,
-        sq_gain,
-        sk_gain,
-        work=2_000_000_000,
-    )
+    arrived = exchange(sent, seq, 6)
     grads_q, scores, gains = call(
         spatial_gain_kernel,
-        (normal, shape(HEADS, 128, 128), shape(16, 2, 128, dtype=F32)),
+        (normal, square, shape(8, 2, 128, dtype=F32)),
         arrived,
         sv,
         unit_q,
@@ -320,11 +331,12 @@
         probs,
         temporal,
     )
-    gains = lax.all_to_all(gains, "z", split_axis=0, concat_axis=0, tiled=True)
-    out, grad_tq, grad_tk, grad_tv, grad_sq, grad_sk, grad_sv = call(
+    gains = lax.all_to_all(gains, ("dp", "core"), split_axis=0, concat_axis=0, tiled=True)
+    message, out_early, grad_tv, grad_sq, grad_sk, grad_sv = call(
         spatial_rest_kernel,
-        (array,) * 7,
+        (shape(1792, 128), shape(EARLY, TOKENS)) + (array,) * 4,
         arrived,
+        later,
         unit_q,
         unit_k,
         inverse_q,
@@ -337,12 +349,14 @@
         sk_gain,
         work=3_000_000_000,
     )
-    gains = call(gain_middle_kernel, shape(32, 2, 128, dtype=F32), gains)
-    gains = lax.all_to_all(gains, ("core", "y", "dp"), split_axis=0, concat_axis=0, tiled=True)
-    gains = call(
-        gain_last_kernel,
-        (shape(1, HEAD_DIM, dtype=F32),) * 4,
-        gains,
+    sent = call(fill_kernel, shape(1792, 128), gains, message)
+    arrived = exchange(sent, seq, 14)
+    gain = shape(1, HEAD_DIM, dtype=F32)
+    out, grad_tq, grad_tk, *gains = call(
+        last_kernel,
+        (array,) * 3 + (gain,) * 4,
+        arrived,
+        out_early,
         sq_gain,
         sk_gain,
         tq_gain,

time: 140 us -> 140 us (level); the launches traced: 140 us -> 138 us
  blocking collectives: 71.4 us -> 117 us
  waiting for transfers between devices: 38.4 us -> 2.42 us
  starting transfers between devices: 16.3 us -> 4.65 us
  Pallas kernels: 13 us -> 11.6 us
    all_to_all x1 -> x3, blocking collectives: 54.1 us -> 117 us  [exchange(): parts = lax.all_to_all(parts, axes, split_axis=0, concat_axis=0, tiled=True)]
    all_to_all x2 -> x1, waiting for transfers between devices: 38.4 us -> 2.42 us  [shards(): lax.all_to_all(gains, ('dp', 'core'), split_axis=0, concat_axis=0, tiled=...]
    all_to_all x1 -> x0, blocking collectives: 17.3 us -> none  [shards(): gains = lax.all_to_all(gains, 'z', split_axis=0, concat_axis=0, tiled=True)]
    all_to_all x2 -> x1, starting transfers between devices: 16.3 us -> 4.65 us  [shards(): lax.all_to_all(gains, ('dp', 'core'), split_axis=0, concat_axis=0, tiled=...]
    pallas_call x7 -> x6, Pallas kernels: 13 us -> 11.6 us  [call(): pl.pallas_call(kernel, out_shape=out_shape, in_specs=specs, scratch_shape...]
  transfers between devices with their start and end apart: 2 -> 1, of which waited for: 2 -> 1; matrix products, arithmetic and copies ran while one was open for 0% -> 0% of each run, Pallas kernels for 2% -> 1%
where the time goes in v4:
time: 140 us; the launch traced here: 138 us
  blocking collectives  117 us (84%)
  Pallas kernels  11.6 us (8%)
  starting transfers between devices  4.65 us (3%)
  waiting for transfers between devices  2.42 us (2%)
    all_to_all x3, blocking collectives, exchange(): parts = lax.all_to_all(parts, axes, split_axis=0, concat_axis=0, tiled=True)  117 us
    pallas_call x6, Pallas kernels, call(): pl.pallas_call(kernel, out_shape=out_shape, in_specs=specs, scratch_shape...  11.6 us
    all_to_all x1, starting transfers between devices, shards(): lax.all_to_all(gains, ('dp', 'core'), split_axis=0, concat_axis=0, tiled=...  4.65 us
  transfers between devices with their start and end apart: 1, of which 1 were waited for; matrix products, arithmetic and copies ran while one was open for 0% of the time, Pallas kernels for 1%

profile of v4, /device:TPU:1, one launch (start us, length us, event | category | flops | bytes accessed | tf_op | source)
XLA Modules:
  0.0 137.9 jit_solution(8113634241709923728)
XLA Ops:
  0.6 2.7 %shard_map.203 = (bf16[2304,128]{1,0:T(8,128)(2,1)S(1)}, f32[8,72,128]{2,1,0:T(8,128)S(1)}, f32[8,72,128]{2,1,0:T(8,128)S(1)}, f32[8,1,128]{2,1,0:T(1,128)S(1)},...) custom-call(f32[1,72]{1,0:T(1,128)} %bitcast.65, ...), custom_call_target="tpu_custom_call" | custom-call | tf_op jit(solution)/shard_map/pallas_call | solution.py:251
  3.3 54.1 %all_to_all.20 = bf16[128,9,2,128]{3,2,1,0:T(2,128)(2,1)S(1)} all-to-all(bf16[128,9,2,128]{3,2,1,0:T(2,128)(2,1)S(1)} %bitcast.63), channel_id=1, replica_groups=mesh['dp'=4,'z'=16,'y'=4,'core'=2] {'z','y','core'}, dimensions={0} | all-to-all | bytes 1179648 | tf_op jit(solution)/shard_map/all_to_all | solution.py:267
  57.4 4.4 %shard_map.204 = (bf16[768,128]{1,0:T(8,128)(2,1)S(1)}, bf16[1536,128]{1,0:T(8,128)(2,1)S(1)}, f32[72,1]{1,0:T(8,128)S(1)}) custom-call(bf16[2304,128]{1,0:T(8,128)(2,1)S(1)} %bitcast.56, s32[1,128]{1,0:T(1,128)} %ids_hbm.1, f32[1,72]{1,0:T(1,128)} %bitcast.71, f32[1,72]{1,0:T(1,128)} %bitcast.73), custom_call_target="tpu_custom_call" | custom-call | tf_op jit(solution)/shard_map/pallas_call | solution.py:251
  61.8 0.0 copy-start
  61.8 27.0 %all_to_all.21 = bf16[128,3,2,128]{3,2,1,0:T(2,128)(2,1)S(1)} all-to-all(bf16[128,3,2,128]{3,2,1,0:T(2,128)(2,1)S(1)} %bitcast.64), channel_id=1, replica_groups=mesh['dp'=4,'z'=16,'y'=4,'core'=2] {'z','y','core'}, dimensions={0} | all-to-all | bytes 393216 | tf_op jit(solution)/shard_map/all_to_all | solution.py:267
  88.8 0.0 copy-done
  88.8 1.7 %shard_map.205 = (bf16[8,72,128]{2,1,0:T(8,128)(2,1)S(1)}, bf16[8,128,128]{2,1,0:T(8,128)(2,1)S(1)}, f32[8,2,128]{2,1,0:T(2,128)}) custom-call(bf16[768,128]{1,0:T(8,128)(2,1)S(1)} %bitcast.59, bf16[576,128]{1,0:T(8,128)(2,1)S(1)} %bitcast.62, f32[8,72,128]{2,1,0:T(8,128)S(1)} %get-tuple-element.40.unit_q, bf16[8,72,128]{2,1,0:T(8,128)(2,1)S(1)} %get-tuple-element.41.key_in, ...), custom_call_target="tpu_custom_call" | custom-call | tf_op jit(solution)/shard_map/pallas_call | solution.py:251
  90.5 4.7 %all-to-all-start.2 = ((f32[8,2,128]{2,1,0:T(2,128)}), f32[8,2,128]{2,1,0:T(2,128)S(1)}, u32[]{:S(2)}, u32[]{:S(2)}) async-start(f32[8,2,128]{2,1,0:T(2,128)} %get-tuple-element.44), calls=%async_computation.2 | async-start | bytes 16384 | tf_op jit(solution)/shard_map/all_to_all | solution.py:334
  95.2 0.0 copy-start.1
  95.2 0.0 copy-start.2
  95.2 0.7 copy-done.1
  95.8 0.0 copy-done.2
  95.9 1.5 %shard_map.206 = (bf16[1792,128]{1,0:T(8,128)(2,1)S(1)}, bf16[192,128]{1,0:T(8,128)(2,1)S(1)}, bf16[576,128]{1,0:T(8,128)(2,1)}, bf16[576,128]{1,0:T(8,128)(2,1)...) custom-call(bf16[768,128]{1,0:T(8,128)(2,1)S(1)} %bitcast.60, bf16[1536,128]{1,0:T(8,128)(2,1)S(1)} %get-tuple-element.45.later, ...), custom_call_target="tpu_custom_call" | custom-call | flops 3000000000 | tf_op jit(solution)/shard_map/pallas_call | solution.py:251
  97.4 2.4 %all-to-all-done.2.gains = f32[8,2,128]{2,1,0:T(2,128)S(1)} async-done(((f32[8,2,128]{2,1,0:T(2,128)}), f32[8,2,128]{2,1,0:T(2,128)S(1)}, u32[]{:S(2)}, u32[]{:S(2)}) %all-to-all-start.2) | async-done | bytes 8224 | tf_op jit(solution)/shard_map/all_to_all | solution.py:334
  99.8 0.1 shard_map.207
  99.9 36.2 %all_to_all.22 = bf16[128,7,2,128]{3,2,1,0:T(2,128)(2,1)S(1)} all-to-all(bf16[128,7,2,128]{3,2,1,0:T(2,128)(2,1)S(1)} %bitcast.57), channel_id=1, replica_groups=mesh['dp'=4,'z'=16,'y'=4,'core'=2] {'z','y','core'}, dimensions={0} | all-to-all | bytes 917504 | tf_op jit(solution)/shard_map/all_to_all | solution.py:267
  136.2 0.0 copy-start.3
  136.2 0.0 copy-start.4
  136.2 0.7 copy-done.3
  136.8 0.0 copy-done.4
  136.8 1.1 shard_map.208
Async XLA Ops:
  61.8 27.0 %copy-start = (bf16[1,1,128,576]{2,3,1,0:T(8,128)(2,1)S(1)}, bf16[1,1,128,576]{2,3,1,0:T(8,128)(2,1)}, u32[]{:S(2)}) copy-start(bf16[1,1,128,576]{2,3,1,0:T(8,128)(2,1)} %param.14) | copy-start | bytes 442372
  90.5 9.3 %all-to-all-start.2 = ((f32[8,2,128]{2,1,0:T(2,128)}), f32[8,2,128]{2,1,0:T(2,128)S(1)}, u32[]{:S(2)}, u32[]{:S(2)}) async-start(f32[8,2,128]{2,1,0:T(2,128)} %get-tuple-element.44), calls=%async_computation.2 | async-start | bytes 16384 | tf_op jit(solution)/shard_map/all_to_all | solution.py:334
  95.2 0.7 copy-start.1
  95.2 0.7 copy-start.2
  136.2 0.7 copy-start.3
  136.2 0.7 copy-start.4

commit v5 on v4

--- a/solution.py
+++ b/solution.py
@@ -86,20 +86,24 @@
 
 
 def probabilities(query, key_in, same):
-    weights = jnp.exp(dot(key_in, query, 0, 0) * SCALE)
+    products = [dot(key_in[h], query[h], 0, 0) for h in range(HEADS)]
+    weights = [jnp.exp(product * SCALE) for product in products]
     if same is not None:
-        weights = weights * same
-    return weights * (1.0 / jnp.sum(weights, axis=0, keepdims=True))
-
-
-def scores_back(probs, value, cotangent):
-    grad_probs = dot(value, cotangent, 0, 0)
-    along = jnp.sum(probs * grad_probs, axis=0, keepdims=True)
-    return (probs * (grad_probs - along) * SCALE).astype(BF)
-
-
-def head(values, index):
-    return values[HEAD_DIM * index : HEAD_DIM * (index + 1), :]
+        weights = [weight * same for weight in weights]
+    return [weight * (1.0 / jnp.sum(weight, axis=0, keepdims=True)) for weight in weights]
+
+
+def scores_back(probs, grad_probs):
+    along = [jnp.sum(p * g, axis=0, keepdims=True) for p, g in zip(probs, grad_probs)]
+    return [(p * (g - a) * SCALE).astype(BF) for p, g, a in zip(probs, grad_probs, along)]
+
+
+def heads(values):
+    return [values[HEAD_DIM * h : HEAD_DIM * (h + 1), :] for h in range(HEADS)]
+
+
+def dots(left, right, left_dim, right_dim):
+    return [dot(left[h], right[h], left_dim, right_dim) for h in range(HEADS)]
 
 
 def by_head(parts):
@@ -127,10 +131,10 @@
     unit_k[...], inverse_k[...], key_in[...] = normed(sk[...], column(gain_k))
     for copy in copies[4:]:
         copy.wait()
-    mixed = []
+    found = probabilities(query, key_in, None)
     for h in range(HEADS):
-        probs[h] = probabilities(query[h], key_in[h], None)
-        mixed.append(dot(head(sv, h), probs[h].astype(BF), 1, 0))
+        probs[h] = found[h]
+    mixed = dots(heads(sv), [p.astype(BF) for p in found], 1, 0)
     spatial = jnp.concatenate(mixed, axis=0).astype(BF)
     total = (tv_in[...].astype(F32) + spatial.astype(F32)).astype(BF)
     pack(jnp.concatenate([tq[...], tk[...], og[...], total], axis=0), 18, out_ref)
@@ -153,19 +157,15 @@
     unit_q, inverse_q, query = normed(tq, column_q)
     unit_k, inverse_k, key_in = normed(tk, column_k)
     same = same_video(ids[...])
-    mixed, grads_q, grads_k, grads_v = [], [], [], []
-    for h in range(HEADS):
-        probs = probabilities(query[h], key_in[h], same)
-        rounded = probs.astype(BF)
-        value, cotangent = head(tv, h), head(og, h)
-        mixed.append(dot(value, rounded, 1, 0))
-        grads_v.append(dot(cotangent, rounded, 1, 1))
-        scores = scores_back(probs, value, cotangent)
-        grads_q.append(dot(key_in[h], scores, 1, 0))
-        grads_k.append(dot(query[h], scores, 1, 1))
-    out = jnp.concatenate(mixed, axis=0).astype(BF)
-    grad_v = jnp.concatenate(grads_v, axis=0).astype(BF)
-    grads_q, grads_k = by_head(grads_q), by_head(grads_k)
+    values, cotangents = heads(tv), heads(og)
+    probs = probabilities(query, key_in, same)
+    grad_probs = dots(values, cotangents, 0, 0)
+    rounded = [p.astype(BF) for p in probs]
+    out = jnp.concatenate(dots(values, rounded, 1, 0), axis=0).astype(BF)
+    grad_v = jnp.concatenate(dots(cotangents, rounded, 1, 1), axis=0).astype(BF)
+    scores = scores_back(probs, grad_probs)
+    grads_q = by_head(dots(key_in, scores, 1, 0))
+    grads_k = by_head(dots(query, scores, 1, 1))
     gains_ref[...] = gain_terms(grads_q, unit_q)
     grad_q = normed_back(grads_q, unit_q, inverse_q, column_q)
     grad_k = normed_back(grads_k, unit_k, inverse_k, column_k)
@@ -175,10 +175,12 @@
 
 def spatial_gain_kernel(in_ref, sv, unit_q, key_in, probs, temporal, grads_q, scores, out_ref):
     given = unpack(in_ref, 6, 5)
+    found = scores_back([probs[h] for h in range(HEADS)], dots(heads(sv), heads(given), 0, 0))
+    products = [p.astype(BF) for p in dots(key_in, found, 1, 0)]
     for h in range(HEADS):
-        scores[h] = scores_back(probs[h], head(sv, h), head(given, h))
-        grads_q[h] = dot(key_in[h], scores[h], 1, 0).astype(BF)
-    total = gain_terms(grads_q[...].astype(F32), unit_q[...])
+        scores[h] = found[h]
+        grads_q[h] = products[h]
+    total = gain_terms(by_head(products), unit_q[...])
     both = jnp.concatenate(
         [jnp.broadcast_to(t, (HEAD_DIM, 128)) for t in (total, temporal[...])], axis=0
     )
@@ -188,15 +190,14 @@
 
 
 def spatial_rest_kernel(
-    in_ref, later, unit_q, unit_k, inverse_q, inverse_k, query, probs, grads_q, scores, gain_q, gain_k,
-    message, out_early, grad_tv, grad_sq, grad_sk, grad_sv
+    in_ref, later, unit_q, unit_k, inverse_q, inverse_k, query, probs, grads_q, scores, gain_q, gain_k, gain_tq, gain_tk,
+    ratios, message, out_early, grad_tv, grad_sq, grad_sk, grad_sv
 ):
+    ratios[...] = jnp.concatenate([gain_q[...] / gain_k[...], gain_tq[...] / gain_tk[...]], axis=0)
     arrays = unpack(in_ref, 6)
     grad_tv[...], out_early[...] = arrays[:INNER, :], arrays[INNER:, :]
-    grads_k, grads_v = [], []
-    for h in range(HEADS):
-        grads_k.append(dot(query[h], scores[h], 1, 1))
-        grads_v.append(dot(head(arrays, h), probs[h].astype(BF), 1, 1))
+    grads_k = dots(query, scores, 1, 1)
+    grads_v = dots(heads(arrays), [probs[h].astype(BF) for h in range(HEADS)], 1, 1)
     grad_sv[...] = jnp.concatenate(grads_v, axis=0).astype(BF)
     grad_sq[...] = normed_back(
         grads_q[...].astype(F32), unit_q[...], inverse_q[...], column(gain_q)
@@ -218,7 +219,7 @@
 
 
 def last_kernel(
-    in_ref, out_early, sq_gain, sk_gain, tq_gain, tk_gain,
+    in_ref, out_early, ratios,
     out, grad_tq, grad_tk, grad_sq_gain, grad_sk_gain, grad_tq_gain, grad_tk_gain
 ):
     tiles = token_tiles(in_ref, 14, 14)
@@ -226,9 +227,9 @@
     spatial = first[:, :HEAD_DIM]
     temporal = jnp.concatenate([first[:, HEAD_DIM:], second[:, : 2 * HEAD_DIM - 128]], axis=1)
     grad_sq_gain[...] = spatial
-    grad_sk_gain[...] = spatial * (sq_gain[...] / sk_gain[...])
+    grad_sk_gain[...] = spatial * ratios[:1, :]
     grad_tq_gain[...] = temporal
-    grad_tk_gain[...] = temporal * (tq_gain[...] / tk_gain[...])
+    grad_tk_gain[...] = temporal * ratios[1:, :]
     arrays = jnp.concatenate([t.T for t in tiles[:12]], axis=0)
     rest = INNER - EARLY
     out[...] = jnp.concatenate([out_early[...], arrays[:rest, :]], axis=0)
@@ -332,9 +333,9 @@
         temporal,
     )
     gains = lax.all_to_all(gains, ("dp", "core"), split_axis=0, concat_axis=0, tiled=True)
-    message, out_early, grad_tv, grad_sq, grad_sk, grad_sv = call(
+    ratios, message, out_early, grad_tv, grad_sq, grad_sk, grad_sv = call(
         spatial_rest_kernel,
-        (shape(1792, 128), shape(EARLY, TOKENS)) + (array,) * 4,
+        (shape(2, HEAD_DIM, dtype=F32), shape(1792, 128), shape(EARLY, TOKENS)) + (array,) * 4,
         arrived,
         later,
         unit_q,
@@ -347,6 +348,8 @@
         scores,
         sq_gain,
         sk_gain,
+        tq_gain,
+        tk_gain,
         work=3_000_000_000,
     )
     sent = call(fill_kernel, shape(1792, 128), gains, message)
@@ -357,10 +360,7 @@
         (array,) * 3 + (gain,) * 4,
         arrived,
         out_early,
-        sq_gain,
-        sk_gain,
-        tq_gain,
-        tk_gain,
+        ratios,
     )
     results = (out, grad_sq, grad_sk, grad_sv, grad_tq, grad_tk, grad_tv)
     return tuple(a.T.reshape(1, 1, TOKENS, INNER) for a in results) + tuple(

time: 140 us -> 136 us (0.971)
  Pallas kernels: 11.6 us -> 8.61 us
    pallas_call x6, Pallas kernels: 11.6 us -> 8.61 us  [call(): pl.pallas_call(kernel, out_shape=out_shape, in_specs=specs, scratch_shape...]
where the time goes in v5:
time: 136 us; the launch traced here: 134 us
  blocking collectives  117 us (86%)
  Pallas kernels  8.61 us (6%)
  starting transfers between devices  4.65 us (3%)
  waiting for transfers between devices  2.4 us (2%)
    all_to_all x3, blocking collectives, exchange(): parts = lax.all_to_all(parts, axes, split_axis=0, concat_axis=0, tiled=True)  117 us
    pallas_call x6, Pallas kernels, call(): pl.pallas_call(kernel, out_shape=out_shape, in_specs=specs, scratch_shape...  8.61 us
    all_to_all x1, starting transfers between devices, shards(): lax.all_to_all(gains, ('dp', 'core'), split_axis=0, concat_axis=0, tiled=...  4.65 us
  transfers between devices with their start and end apart: 1, of which 1 were waited for; matrix products, arithmetic and copies ran while one was open for 0% of the time, Pallas kernels for 1%

profile of v5, /device:TPU:1, one launch (start us, length us, event | category | flops | bytes accessed | tf_op | source)
XLA Modules:
  0.0 134.3 jit_solution(4688308335281676050)
XLA Ops:
  0.6 2.4 %shard_map.203 = (bf16[2304,128]{1,0:T(8,128)(2,1)S(1)}, f32[8,72,128]{2,1,0:T(8,128)S(1)}, f32[8,72,128]{2,1,0:T(8,128)S(1)}, f32[8,1,128]{2,1,0:T(1,128)S(1)},...) custom-call(f32[1,72]{1,0:T(1,128)} %bitcast.65, ...), custom_call_target="tpu_custom_call" | custom-call | tf_op jit(solution)/shard_map/pallas_call | solution.py:252
  3.0 54.1 %all_to_all.20 = bf16[128,9,2,128]{3,2,1,0:T(2,128)(2,1)S(1)} all-to-all(bf16[128,9,2,128]{3,2,1,0:T(2,128)(2,1)S(1)} %bitcast.63), channel_id=1, replica_groups=mesh['dp'=4,'z'=16,'y'=4,'core'=2] {'z','y','core'}, dimensions={0} | all-to-all | bytes 1179648 | tf_op jit(solution)/shard_map/all_to_all | solution.py:268
  57.1 2.1 %shard_map.204 = (bf16[768,128]{1,0:T(8,128)(2,1)S(1)}, bf16[1536,128]{1,0:T(8,128)(2,1)S(1)}, f32[72,1]{1,0:T(8,128)S(1)}) custom-call(bf16[2304,128]{1,0:T(8,128)(2,1)S(1)} %bitcast.56, s32[1,128]{1,0:T(1,128)} %ids_hbm.1, f32[1,72]{1,0:T(1,128)} %bitcast.69, f32[1,72]{1,0:T(1,128)} %bitcast.71), custom_call_target="tpu_custom_call" | custom-call | tf_op jit(solution)/shard_map/pallas_call | solution.py:252
  59.2 0.0 copy-start
  59.2 27.0 %all_to_all.21 = bf16[128,3,2,128]{3,2,1,0:T(2,128)(2,1)S(1)} all-to-all(bf16[128,3,2,128]{3,2,1,0:T(2,128)(2,1)S(1)} %bitcast.64), channel_id=1, replica_groups=mesh['dp'=4,'z'=16,'y'=4,'core'=2] {'z','y','core'}, dimensions={0} | all-to-all | bytes 393216 | tf_op jit(solution)/shard_map/all_to_all | solution.py:268
  86.1 0.0 copy-done
  86.1 0.0 copy-start.4
  86.1 1.4 %shard_map.205 = (bf16[8,72,128]{2,1,0:T(8,128)(2,1)S(1)}, bf16[8,128,128]{2,1,0:T(8,128)(2,1)S(1)}, f32[8,2,128]{2,1,0:T(2,128)}) custom-call(bf16[768,128]{1,0:T(8,128)(2,1)S(1)} %bitcast.59, bf16[576,128]{1,0:T(8,128)(2,1)S(1)} %bitcast.62, f32[8,72,128]{2,1,0:T(8,128)S(1)} %get-tuple-element.41.unit_q, bf16[8,72,128]{2,1,0:T(8,128)(2,1)S(1)} %get-tuple-element.42.key_in, ...), custom_call_target="tpu_custom_call" | custom-call | tf_op jit(solution)/shard_map/pallas_call | solution.py:252
  87.6 4.7 %all-to-all-start.2 = ((f32[8,2,128]{2,1,0:T(2,128)}), f32[8,2,128]{2,1,0:T(2,128)S(1)}, u32[]{:S(2)}, u32[]{:S(2)}) async-start(f32[8,2,128]{2,1,0:T(2,128)} %get-tuple-element.45), calls=%async_computation.2 | async-start | bytes 16384 | tf_op jit(solution)/shard_map/all_to_all | solution.py:335
  92.2 0.0 copy-start.1
  92.2 0.0 copy-start.2
  92.2 0.0 copy-start.3
  92.2 0.0 copy-done.4
  92.2 0.6 copy-done.1
  92.9 0.0 copy-done.2
  92.9 0.0 copy-done.3
  92.9 1.5 %shard_map.206 = (f32[2,72]{1,0:T(2,128)S(1)}, bf16[1792,128]{1,0:T(8,128)(2,1)S(1)}, bf16[192,128]{1,0:T(8,128)(2,1)S(1)}, bf16[576,128]{1,0:T(8,128)(2,1)}, bf...) custom-call(bf16[768,128]{1,0:T(8,128)(2,1)S(1)} %bitcast.60, ...), custom_call_target="tpu_custom_call" | custom-call | flops 3000000000 | tf_op jit(solution)/shard_map/pallas_call | solution.py:252
  94.4 2.4 %all-to-all-done.2.gains = f32[8,2,128]{2,1,0:T(2,128)S(1)} async-done(((f32[8,2,128]{2,1,0:T(2,128)}), f32[8,2,128]{2,1,0:T(2,128)S(1)}, u32[]{:S(2)}, u32[]{:S(2)}) %all-to-all-start.2) | async-done | bytes 8224 | tf_op jit(solution)/shard_map/all_to_all | solution.py:335
  96.8 0.1 shard_map.207
  96.9 36.2 %all_to_all.22 = bf16[128,7,2,128]{3,2,1,0:T(2,128)(2,1)S(1)} all-to-all(bf16[128,7,2,128]{3,2,1,0:T(2,128)(2,1)S(1)} %bitcast.57), channel_id=1, replica_groups=mesh['dp'=4,'z'=16,'y'=4,'core'=2] {'z','y','core'}, dimensions={0} | all-to-all | bytes 917504 | tf_op jit(solution)/shard_map/all_to_all | solution.py:268
  133.2 1.1 shard_map.208
Async XLA Ops:
  59.2 27.0 %copy-start = (bf16[1,1,128,576]{2,3,1,0:T(8,128)(2,1)S(1)}, bf16[1,1,128,576]{2,3,1,0:T(8,128)(2,1)}, u32[]{:S(2)}) copy-start(bf16[1,1,128,576]{2,3,1,0:T(8,128)(2,1)} %param.14) | copy-start | bytes 442372
  86.1 6.1 %copy-start.4 = (f32[72]{0:T(128)S(1)}, f32[72]{0:T(128)}, u32[]{:S(2)}) copy-start(f32[72]{0:T(128)} %param.23) | copy-start | bytes 868
  87.6 9.3 %all-to-all-start.2 = ((f32[8,2,128]{2,1,0:T(2,128)}), f32[8,2,128]{2,1,0:T(2,128)S(1)}, u32[]{:S(2)}, u32[]{:S(2)}) async-start(f32[8,2,128]{2,1,0:T(2,128)} %get-tuple-element.45), calls=%async_computation.2 | async-start | bytes 16384 | tf_op jit(solution)/shard_map/all_to_all | solution.py:335
  92.2 0.7 copy-start.1
  92.2 0.7 copy-start.2
  92.2 0.7 copy-start.3

commit v6 on v5

--- a/solution.py
+++ b/solution.py
@@ -10,9 +10,10 @@
 HEAD_DIM = 72
 INNER = 576
 TOKENS = 128
+TILES = 18
+ROWS = TILES * TOKENS
 SCALE = HEAD_DIM ** (-0.5)
 EPS = 1e-06
-EARLY = 192
 BF = jnp.bfloat16
 F32 = jnp.float32
 MIB = 1024 * 1024
@@ -24,41 +25,17 @@
     )
 
 
-def pack(features, tiles, out_ref):
-    size = 16 * tiles
-    row = lax.broadcasted_iota(jnp.int32, (size, size), 0)
-    col = lax.broadcasted_iota(jnp.int32, (size, size), 1)
-    order = (row == (col & 15) * tiles + (col >> 4)).astype(F32).astype(BF)
-    stacked = []
-    for tile in range(tiles):
+def pack(features, wide, out_ref):
+    for tile in range(TILES):
         turned = features[128 * tile : 128 * tile + 128, :].T
-        stacked.append(
-            jnp.concatenate([turned[16 * b : 16 * b + 16, :] for b in range(8)], axis=1)
-        )
-    mixed = dot(order, jnp.concatenate(stacked, axis=0), 1, 0).astype(BF)
-    for b in range(8):
-        out_ref[size * b : size * b + size, :] = mixed[:, 128 * b : 128 * b + 128]
-
-
-def token_tiles(in_ref, tiles, wanted):
-    size = 16 * tiles
-    row = lax.broadcasted_iota(jnp.int32, (16 * wanted, size), 0)
-    col = lax.broadcasted_iota(jnp.int32, (16 * wanted, size), 1)
-    order = (col == (row & 15) * tiles + (row >> 4)).astype(F32).astype(BF)
-    blocks = jnp.concatenate(
-        [in_ref[size * b : size * b + size, :] for b in range(8)], axis=1
-    )
-    mixed = dot(order, blocks, 1, 0).astype(BF)
-    return [
-        jnp.concatenate(
-            [mixed[16 * tile : 16 * tile + 16, 128 * b : 128 * b + 128] for b in range(8)], axis=0
-        )
-        for tile in range(wanted)
-    ]
-
-
-def unpack(in_ref, tiles, wanted=None):
-    return jnp.concatenate([t.T for t in token_tiles(in_ref, tiles, wanted or tiles)], axis=0)
+        wide[pl.ds(tile, TOKENS, stride=TILES), :] = turned.astype(F32)
+    out_ref[...] = wide[...].astype(BF)
+
+
+def unpack(in_ref, wide, wanted=None):
+    wide[...] = in_ref[...].astype(F32)
+    tiles = [wide[pl.ds(tile, TOKENS, stride=TILES), :] for tile in range(wanted or TILES)]
+    return jnp.concatenate([tile.astype(BF).T for tile in tiles], axis=0)
 
 
 def column(gain_ref):
@@ -122,7 +99,7 @@
 
 def send_kernel(*refs):
     sources, (out_ref, unit_q, unit_k, inverse_q, inverse_k, query, key_in, probs) = refs[:9], refs[9:17]
-    buffers, sems = refs[17:-1], refs[-1]
+    wide, buffers, sems = refs[17], refs[18:-1], refs[-1]
     copies = load(sources, buffers, sems)
     gain_q, gain_k, sq, sk, sv, tq, tk, og, tv_in = buffers
     for copy in copies[:4]:
@@ -137,7 +114,7 @@
     mixed = dots(heads(sv), [p.astype(BF) for p in found], 1, 0)
     spatial = jnp.concatenate(mixed, axis=0).astype(BF)
     total = (tv_in[...].astype(F32) + spatial.astype(F32)).astype(BF)
-    pack(jnp.concatenate([tq[...], tk[...], og[...], total], axis=0), 18, out_ref)
+    pack(jnp.concatenate([tq[...], tk[...], og[...], total], axis=0), wide, out_ref)
 
 
 def same_video(ids):
@@ -146,10 +123,10 @@
 
 
 def temporal_kernel(
-    in_ref, ids_hbm, gain_q_hbm, gain_k_hbm, out_ref, later_ref, gains_ref, ids, gain_q, gain_k, sems
+    in_ref, ids_hbm, gain_q_hbm, gain_k_hbm, out_ref, gains_ref, wide, ids, gain_q, gain_k, sems
 ):
     copies = load((ids_hbm, gain_q_hbm, gain_k_hbm), (ids, gain_q, gain_k), sems)
-    arrays = unpack(in_ref, 18)
+    arrays = unpack(in_ref, wide)
     tq, tk, og, tv = (arrays[INNER * i : INNER * (i + 1), :] for i in range(4))
     for copy in copies:
         copy.wait()
@@ -169,12 +146,11 @@
     gains_ref[...] = gain_terms(grads_q, unit_q)
     grad_q = normed_back(grads_q, unit_q, inverse_q, column_q)
     grad_k = normed_back(grads_k, unit_k, inverse_k, column_k)
-    later_ref[...] = jnp.concatenate([out[EARLY:, :], grad_q, grad_k], axis=0)
-    pack(jnp.concatenate([grad_v, out[:EARLY, :]], axis=0), 6, out_ref)
-
-
-def spatial_gain_kernel(in_ref, sv, unit_q, key_in, probs, temporal, grads_q, scores, out_ref):
-    given = unpack(in_ref, 6, 5)
+    pack(jnp.concatenate([grad_v, out, grad_q, grad_k], axis=0), wide, out_ref)
+
+
+def spatial_gain_kernel(in_ref, sv, unit_q, key_in, probs, temporal, grads_q, scores, out_ref, wide):
+    given = unpack(in_ref, wide, 5)
     found = scores_back([probs[h] for h in range(HEADS)], dots(heads(sv), heads(given), 0, 0))
     products = [p.astype(BF) for p in dots(key_in, found, 1, 0)]
     for h in range(HEADS):
@@ -190,12 +166,14 @@
 
 
 def spatial_rest_kernel(
-    in_ref, later, unit_q, unit_k, inverse_q, inverse_k, query, probs, grads_q, scores, gain_q, gain_k, gain_tq, gain_tk,
-    ratios, message, out_early, grad_tv, grad_sq, grad_sk, grad_sv
+    in_ref, unit_q, unit_k, inverse_q, inverse_k, query, probs, grads_q, scores, gain_q, gain_k, gain_tq, gain_tk,
+    ratios, out, grad_tq, grad_tk, grad_tv, grad_sq, grad_sk, grad_sv, wide
 ):
     ratios[...] = jnp.concatenate([gain_q[...] / gain_k[...], gain_tq[...] / gain_tk[...]], axis=0)
-    arrays = unpack(in_ref, 6)
-    grad_tv[...], out_early[...] = arrays[:INNER, :], arrays[INNER:, :]
+    arrays = unpack(in_ref, wide)
+    grad_tv[...], out[...], grad_tq[...], grad_tk[...] = (
+        arrays[INNER * i : INNER * (i + 1), :] for i in range(4)
+    )
     grads_k = dots(query, scores, 1, 1)
     grads_v = dots(heads(arrays), [probs[h].astype(BF) for h in range(HEADS)], 1, 1)
     grad_sv[...] = jnp.concatenate(grads_v, axis=0).astype(BF)
@@ -203,38 +181,20 @@
         grads_q[...].astype(F32), unit_q[...], inverse_q[...], column(gain_q)
     )
     grad_sk[...] = normed_back(by_head(grads_k), unit_k[...], inverse_k[...], column(gain_k))
-    pack(jnp.concatenate([later[...], jnp.zeros((256, TOKENS), BF)], axis=0), 14, message)
-
-
-def fill_kernel(gains, message, out_ref):
-    total = jnp.sum(gains[...], axis=0)
-    high = total.astype(BF).astype(F32)
-    part = jnp.where(lax.axis_index("core") == 0, high, total - high)
-    row = lax.broadcasted_iota(jnp.int32, (224, 128), 0)
-    place = row - 14 * ((row * 4682) >> 16)
-    block = jnp.where(place == 12, part[:1, :], part[1:, :])
-    for b in range(8):
-        rows = message[224 * b : 224 * b + 224, :].astype(F32)
-        out_ref[224 * b : 224 * b + 224, :] = jnp.where(place >= 12, block, rows).astype(BF)
-
-
-def last_kernel(
-    in_ref, out_early, ratios,
-    out, grad_tq, grad_tk, grad_sq_gain, grad_sk_gain, grad_tq_gain, grad_tk_gain
-):
-    tiles = token_tiles(in_ref, 14, 14)
-    first, second = (jnp.sum(t.astype(F32), axis=0, keepdims=True) for t in tiles[12:])
-    spatial = first[:, :HEAD_DIM]
-    temporal = jnp.concatenate([first[:, HEAD_DIM:], second[:, : 2 * HEAD_DIM - 128]], axis=1)
-    grad_sq_gain[...] = spatial
-    grad_sk_gain[...] = spatial * ratios[:1, :]
-    grad_tq_gain[...] = temporal
-    grad_tk_gain[...] = temporal * ratios[1:, :]
-    arrays = jnp.concatenate([t.T for t in tiles[:12]], axis=0)
-    rest = INNER - EARLY
-    out[...] = jnp.concatenate([out_early[...], arrays[:rest, :]], axis=0)
-    grad_tq[...] = arrays[rest : rest + INNER, :]
-    grad_tk[...] = arrays[rest + INNER :, :]
+
+
+def gain_middle_kernel(in_ref, ratios, out_ref):
+    out_ref[...] = jnp.broadcast_to(jnp.sum(in_ref[...], axis=0, keepdims=True), out_ref.shape)
+
+
+def gain_last_kernel(in_ref, ratios, grad_sq, grad_sk, grad_tq, grad_tk):
+    total = jnp.sum(in_ref[...], axis=0)
+    spatial = total[:1, :HEAD_DIM]
+    temporal = jnp.concatenate([total[:1, HEAD_DIM:], total[1:, : 2 * HEAD_DIM - 128]], axis=1)
+    grad_sq[...] = spatial
+    grad_sk[...] = spatial * ratios[:1, :]
+    grad_tq[...] = temporal
+    grad_tk[...] = temporal * ratios[1:, :]
 
 
 def shape(*extent, dtype=BF):
@@ -263,10 +223,13 @@
     return [pltpu.VMEM(a.shape, a.dtype) for a in arrays] + [pltpu.SemaphoreType.DMA((len(arrays),))]
 
 
-def exchange(message, axes, tiles):
-    parts = message.reshape(TOKENS, tiles // 2, 2, 128)
-    parts = lax.all_to_all(parts, axes, split_axis=0, concat_axis=0, tiled=True)
-    return parts.reshape(TOKENS * tiles, 128)
+WIDE = [pltpu.VMEM((ROWS, 128), F32)]
+
+
+def exchange(message):
+    parts = message.reshape(TOKENS, TILES // 2, 2, 128)
+    parts = lax.all_to_all(parts, ("z", "y", "core"), split_axis=0, concat_axis=0, tiled=True)
+    return parts.reshape(ROWS, 128)
 
 
 def shards(
@@ -299,45 +262,44 @@
         g.reshape(1, HEAD_DIM)
         for g in (spatial_query_gain, spatial_key_gain, temporal_query_gain, temporal_key_gain)
     )
-    seq = ("z", "y", "core")
     array = shape(INNER, TOKENS)
     args = (sq_gain, sk_gain, sq, sk, sv, tq, tk, og, tv_in)
     unit, inverse = shape(HEADS, HEAD_DIM, TOKENS, dtype=F32), shape(HEADS, 1, TOKENS, dtype=F32)
     normal, square = shape(HEADS, HEAD_DIM, TOKENS), shape(HEADS, 128, 128)
     sent, unit_q, unit_k, inverse_q, inverse_k, query, key_in, probs = call(
         send_kernel,
-        (shape(2304, 128), unit, unit, inverse, inverse, normal, normal, shape(HEADS, 128, 128, dtype=F32)),
+        (shape(ROWS, 128), unit, unit, inverse, inverse, normal, normal, shape(HEADS, 128, 128, dtype=F32)),
         *args,
         in_hbm=9,
-        scratch=buffers(*args),
-    )
-    arrived = exchange(sent, seq, 18)
+        scratch=WIDE + buffers(*args),
+    )
+    arrived = exchange(sent)
     args = (video_ids, tq_gain, tk_gain)
-    sent, later, temporal = call(
+    sent, temporal = call(
         temporal_kernel,
-        (shape(768, 128), shape(1536, 128), shape(HEAD_DIM, 1, dtype=F32)),
+        (shape(ROWS, 128), shape(HEAD_DIM, 1, dtype=F32)),
         arrived,
         *args,
         in_hbm=3,
-        scratch=buffers(*args),
-    )
-    arrived = exchange(sent, seq, 6)
+        scratch=WIDE + buffers(*args),
+    )
+    arrived = exchange(sent)
     grads_q, scores, gains = call(
         spatial_gain_kernel,
-        (normal, square, shape(8, 2, 128, dtype=F32)),
+        (normal, square, shape(16, 2, 128, dtype=F32)),
         arrived,
         sv,
         unit_q,
         key_in,
         probs,
         temporal,
-    )
-    gains = lax.all_to_all(gains, ("dp", "core"), split_axis=0, concat_axis=0, tiled=True)
-    ratios, message, out_early, grad_tv, grad_sq, grad_sk, grad_sv = call(
+        scratch=WIDE,
+    )
+    gains = lax.all_to_all(gains, "z", split_axis=0, concat_axis=0, tiled=True)
+    ratios, out, grad_tq, grad_tk, grad_tv, grad_sq, grad_sk, grad_sv = call(
         spatial_rest_kernel,
-        (shape(2, HEAD_DIM, dtype=F32), shape(1792, 128), shape(EARLY, TOKENS)) + (array,) * 4,
+        (shape(2, HEAD_DIM, dtype=F32),) + (array,) * 7,
         arrived,
-        later,
         unit_q,
         unit_k,
         inverse_q,
@@ -350,18 +312,12 @@
         sk_gain,
         tq_gain,
         tk_gain,
+        scratch=WIDE,
         work=3_000_000_000,
     )
-    sent = call(fill_kernel, shape(1792, 128), gains, message)
-    arrived = exchange(sent, seq, 14)
-    gain = shape(1, HEAD_DIM, dtype=F32)
-    out, grad_tq, grad_tk, *gains = call(
-        last_kernel,
-        (array,) * 3 + (gain,) * 4,
-        arrived,
-        out_early,
-        ratios,
-    )
+    gains = call(gain_middle_kernel, shape(32, 2, 128, dtype=F32), gains, ratios)
+    gains = lax.all_to_all(gains, ("core", "y", "dp"), split_axis=0, concat_axis=0, tiled=True)
+    gains = call(gain_last_kernel, (shape(1, HEAD_DIM, dtype=F32),) * 4, gains, ratios)
     results = (out, grad_sq, grad_sk, grad_sv, grad_tq, grad_tk, grad_tv)
     return tuple(a.T.reshape(1, 1, TOKENS, INNER) for a in results) + tuple(
         g.reshape(HEAD_DIM) for g in gains

time: 136 us -> 135 us (level); the launches traced: 134 us -> 135 us
  waiting for transfers between devices: 2.4 us -> 9.22 us
  blocking collectives: 117 us -> 111 us
  starting transfers between devices: 4.65 us -> 6.12 us
    all_to_all x1, waiting for transfers between devices: 2.4 us -> 9.22 us  [shards(): gains = lax.all_to_all(gains, 'z', split_axis=0, concat_axis=0, tiled=True)]
    all_to_all x3, blocking collectives: 117 us -> 111 us  [the longest x2 96.7 us: exchange(): lax.all_to_all(parts, ('z', 'y', 'core'), split_axis=0, concat_axis=0, ti...]
    all_to_all x1, starting transfers between devices: 4.65 us -> 6.12 us  [shards(): gains = lax.all_to_all(gains, 'z', split_axis=0, concat_axis=0, tiled=True)]
where the time goes in v6:
time: 135 us
  blocking collectives  111 us (82%)
  waiting for transfers between devices  9.22 us (7%)
  Pallas kernels  7.51 us (6%)
  starting transfers between devices  6.12 us (5%)
    all_to_all x2, blocking collectives, exchange(): lax.all_to_all(parts, ('z', 'y', 'core'), split_axis=0, concat_axis=0, ti...  96.7 us
    all_to_all x1, blocking collectives, shards(): lax.all_to_all(gains, ('core', 'y', 'dp'), split_axis=0, concat_axis=0, t...  14.3 us
    all_to_all x1, waiting for transfers between devices, shards(): gains = lax.all_to_all(gains, 'z', split_axis=0, concat_axis=0, tiled=True)  9.22 us
    pallas_call x6, Pallas kernels, call(): pl.pallas_call(kernel, out_shape=out_shape, in_specs=specs, scratch_shape...  7.51 us
    all_to_all x1, starting transfers between devices, shards(): gains = lax.all_to_all(gains, 'z', split_axis=0, concat_axis=0, tiled=True)  6.12 us
  transfers between devices with their start and end apart: 1, of which 1 were waited for; matrix products, arithmetic and copies ran while one was open for 0% of the time, Pallas kernels for 1%

profile of v6, /device:TPU:1, one launch (start us, length us, event | category | flops | bytes accessed | tf_op | source)
XLA Modules:
  0.0 135.2 jit_solution(15933273461752384997)
XLA Ops:
  0.6 2.0 %shard_map.203 = (bf16[2304,128]{1,0:T(8,128)(2,1)S(1)}, f32[8,72,128]{2,1,0:T(8,128)S(1)}, f32[8,72,128]{2,1,0:T(8,128)S(1)}, f32[8,1,128]{2,1,0:T(1,128)S(1)},...) custom-call(f32[1,72]{1,0:T(1,128)} %bitcast.61, ...), custom_call_target="tpu_custom_call" | custom-call | tf_op jit(solution)/shard_map/pallas_call | solution.py:212
  2.7 54.1 %all_to_all.20 = bf16[128,9,2,128]{3,2,1,0:T(2,128)(2,1)S(1)} all-to-all(bf16[128,9,2,128]{3,2,1,0:T(2,128)(2,1)S(1)} %bitcast.59), channel_id=1, replica_groups=mesh['dp'=4,'z'=16,'y'=4,'core'=2] {'z','y','core'}, dimensions={0} | all-to-all | bytes 1179648 | tf_op jit(solution)/shard_map/all_to_all | solution.py:231
  56.7 2.1 %shard_map.204 = (bf16[2304,128]{1,0:T(8,128)(2,1)S(1)}, f32[72,1]{1,0:T(8,128)S(1)}) custom-call(bf16[2304,128]{1,0:T(8,128)(2,1)S(1)} %bitcast.56, s32[1,128]{1,0:T(1,128)} %ids_hbm.1, f32[1,72]{1,0:T(1,128)} %bitcast.65, f32[1,72]{1,0:T(1,128)} %bitcast.67), custom_call_target="tpu_custom_call" | custom-call | tf_op jit(solution)/shard_map/pallas_call | solution.py:212
  58.8 0.0 copy-start
  58.8 42.6 %all_to_all.21 = bf16[128,9,2,128]{3,2,1,0:T(2,128)(2,1)S(1)} all-to-all(bf16[128,9,2,128]{3,2,1,0:T(2,128)(2,1)S(1)} %bitcast.60), channel_id=1, replica_groups=mesh['dp'=4,'z'=16,'y'=4,'core'=2] {'z','y','core'}, dimensions={0} | all-to-all | bytes 1179648 | tf_op jit(solution)/shard_map/all_to_all | solution.py:231
  101.4 0.0 copy-done
  101.4 0.0 copy-start.4
  101.4 1.3 shard_map.205
  102.7 6.1 %all-to-all-start.2 = ((f32[16,2,128]{2,1,0:T(2,128)}), f32[16,2,128]{2,1,0:T(2,128)S(1)}, u32[]{:S(2)}, u32[]{:S(2)}) async-start(f32[16,2,128]{2,1,0:T(2,128)} %get-tuple-element.55), calls=%async_computation.2 | async-start | bytes 32768 | tf_op jit(solution)/shard_map/all_to_all | solution.py:298
  108.9 0.0 copy-start.1
  108.9 0.0 copy-start.2
  108.9 0.0 copy-start.3
  108.9 0.0 copy-done.4
  108.9 0.6 copy-done.1
  109.5 0.0 copy-done.2
  109.5 0.0 copy-done.3
  109.6 1.5 %shard_map.206 = (f32[2,72]{1,0:T(2,128)S(1)}, bf16[576,128]{1,0:T(8,128)(2,1)}, bf16[576,128]{1,0:T(8,128)(2,1)}, bf16[576,128]{1,0:T(8,128)(2,1)}, bf16[576,12...) custom-call(bf16[2304,128]{1,0:T(8,128)(2,1)S(1)} %bitcast.55, ...), custom_call_target="tpu_custom_call" | custom-call | flops 3000000000 | tf_op jit(solution)/shard_map/pallas_call | solution.py:212
  111.0 9.2 %all-to-all-done.2.in_ref = f32[16,2,128]{2,1,0:T(2,128)S(1)} async-done(((f32[16,2,128]{2,1,0:T(2,128)}), f32[16,2,128]{2,1,0:T(2,128)S(1)}, u32[]{:S(2)}, u32[]{:S(2)}) %all-to-all-start.2) | async-done | bytes 16416 | tf_op jit(solution)/shard_map/all_to_all | solution.py:298
  120.3 14.3 %all_to_all.22.in_ref = f32[32,2,128]{2,1,0:T(2,128)S(1)} all-to-all(f32[32,2,128]{2,1,0:T(2,128)S(1)} %shard_map.207), channel_id=1, replica_groups=mesh['dp'=4,'z'=16,'y'=4,'core'=2] {'core','y','dp'}, dimensions={0} | all-to-all | bytes 65536 | tf_op jit(solution)/shard_map/all_to_all | solution.py:319
  134.5 0.6 shard_map.208
  (1 shorter events, 0.0 us)
Async XLA Ops:
  58.8 42.6 %copy-start = (bf16[1,1,128,576]{2,3,1,0:T(8,128)(2,1)S(1)}, bf16[1,1,128,576]{2,3,1,0:T(8,128)(2,1)}, u32[]{:S(2)}) copy-start(bf16[1,1,128,576]{2,3,1,0:T(8,128)(2,1)} %param.14) | copy-start | bytes 442372
  101.4 7.5 %copy-start.4 = (f32[72]{0:T(128)S(1)}, f32[72]{0:T(128)}, u32[]{:S(2)}) copy-start(f32[72]{0:T(128)} %param.23) | copy-start | bytes 868
  102.7 17.5 %all-to-all-start.2 = ((f32[16,2,128]{2,1,0:T(2,128)}), f32[16,2,128]{2,1,0:T(2,128)S(1)}, u32[]{:S(2)}, u32[]{:S(2)}) async-start(f32[16,2,128]{2,1,0:T(2,128)} %get-tuple-element.55), calls=%async_computation.2 | async-start | bytes 32768 | tf_op jit(solution)/shard_map/all_to_all | solution.py:298
  108.9 0.7 copy-start.1
  108.9 0.7 copy-start.2
  108.9 0.7 copy-start.3

commit v7 on v6

--- a/solution.py
+++ b/solution.py
@@ -59,7 +59,7 @@
 
 
 def gain_terms(cotangent, unit):
-    return jnp.sum(jnp.sum(cotangent * unit, axis=0), axis=1, keepdims=True)
+    return jnp.sum(cotangent * unit, axis=0)
 
 
 def probabilities(query, key_in, same):
@@ -98,17 +98,22 @@
 
 
 def send_kernel(*refs):
-    sources, (out_ref, unit_q, unit_k, inverse_q, inverse_k, query, key_in, probs) = refs[:9], refs[9:17]
-    wide, buffers, sems = refs[17], refs[18:-1], refs[-1]
+    sources, refs = refs[:12], refs[12:]
+    out_ref, unit_q, unit_k, inverse_q, inverse_k, query, key_in, probs, gains, ratios, same = refs[:11]
+    wide, buffers, sems = refs[11], refs[12:-1], refs[-1]
     copies = load(sources, buffers, sems)
-    gain_q, gain_k, sq, sk, sv, tq, tk, og, tv_in = buffers
-    for copy in copies[:4]:
+    *rows, ids, sq, sk, sv, tq, tk, og, tv_in = buffers
+    for copy in copies[:7]:
         copy.wait()
-    unit_q[...], inverse_q[...], query[...] = normed(sq[...], column(gain_q))
-    unit_k[...], inverse_k[...], key_in[...] = normed(sk[...], column(gain_k))
-    for copy in copies[4:]:
+    for i in range(4):
+        gains[i] = jnp.broadcast_to(column(rows[i]), (HEAD_DIM, TOKENS))
+    ratios[...] = jnp.concatenate([rows[0][...] / rows[1][...], rows[2][...] / rows[3][...]], axis=0)
+    same[...] = same_video(ids[...])
+    unit_q[...], inverse_q[...], query[...] = normed(sq[...], gains[0])
+    unit_k[...], inverse_k[...], key_in[...] = normed(sk[...], gains[1])
+    found = probabilities(query, key_in, None)
+    for copy in copies[7:]:
         copy.wait()
-    found = probabilities(query, key_in, None)
     for h in range(HEADS):
         probs[h] = found[h]
     mixed = dots(heads(sv), [p.astype(BF) for p in found], 1, 0)
@@ -122,20 +127,13 @@
     return (ids == ids.T).astype(F32)
 
 
-def temporal_kernel(
-    in_ref, ids_hbm, gain_q_hbm, gain_k_hbm, out_ref, gains_ref, wide, ids, gain_q, gain_k, sems
-):
-    copies = load((ids_hbm, gain_q_hbm, gain_k_hbm), (ids, gain_q, gain_k), sems)
+def temporal_kernel(in_ref, gains, same, out_ref, terms_ref, wide):
     arrays = unpack(in_ref, wide)
     tq, tk, og, tv = (arrays[INNER * i : INNER * (i + 1), :] for i in range(4))
-    for copy in copies:
-        copy.wait()
-    column_q, column_k = column(gain_q), column(gain_k)
-    unit_q, inverse_q, query = normed(tq, column_q)
-    unit_k, inverse_k, key_in = normed(tk, column_k)
-    same = same_video(ids[...])
+    unit_q, inverse_q, query = normed(tq, gains[2])
+    unit_k, inverse_k, key_in = normed(tk, gains[3])
     values, cotangents = heads(tv), heads(og)
-    probs = probabilities(query, key_in, same)
+    probs = probabilities(query, key_in, same[...])
     grad_probs = dots(values, cotangents, 0, 0)
     rounded = [p.astype(BF) for p in probs]
     out = jnp.concatenate(dots(values, rounded, 1, 0), axis=0).astype(BF)
@@ -143,9 +141,9 @@
     scores = scores_back(probs, grad_probs)
     grads_q = by_head(dots(key_in, scores, 1, 0))
     grads_k = by_head(dots(query, scores, 1, 1))
-    gains_ref[...] = gain_terms(grads_q, unit_q)
-    grad_q = normed_back(grads_q, unit_q, inverse_q, column_q)
-    grad_k = normed_back(grads_k, unit_k, inverse_k, column_k)
+    terms_ref[...] = gain_terms(grads_q, unit_q)
+    grad_q = normed_back(grads_q, unit_q, inverse_q, gains[2])
+    grad_k = normed_back(grads_k, unit_k, inverse_k, gains[3])
     pack(jnp.concatenate([grad_v, out, grad_q, grad_k], axis=0), wide, out_ref)
 
 
@@ -157,19 +155,17 @@
         scores[h] = found[h]
         grads_q[h] = products[h]
     total = gain_terms(by_head(products), unit_q[...])
-    both = jnp.concatenate(
-        [jnp.broadcast_to(t, (HEAD_DIM, 128)) for t in (total, temporal[...])], axis=0
-    )
-    both = jnp.concatenate([both, jnp.zeros((112, 128), F32)], axis=0)
-    rows = jnp.concatenate([both[:128, :].T[:1, :], both[128:, :].T[:1, :]], axis=0)
+    both = jnp.concatenate([total, temporal[...], jnp.zeros((112, 128), F32)], axis=0)
+    rows = jnp.concatenate(
+        [jnp.sum(part.T, axis=0, keepdims=True) for part in (both[:128, :], both[128:, :])], axis=0
+    )
     out_ref[...] = jnp.broadcast_to(rows[None], out_ref.shape)
 
 
 def spatial_rest_kernel(
-    in_ref, unit_q, unit_k, inverse_q, inverse_k, query, probs, grads_q, scores, gain_q, gain_k, gain_tq, gain_tk,
-    ratios, out, grad_tq, grad_tk, grad_tv, grad_sq, grad_sk, grad_sv, wide
+    in_ref, unit_q, unit_k, inverse_q, inverse_k, query, probs, grads_q, scores, gains,
+    out, grad_tq, grad_tk, grad_tv, grad_sq, grad_sk, grad_sv, wide
 ):
-    ratios[...] = jnp.concatenate([gain_q[...] / gain_k[...], gain_tq[...] / gain_tk[...]], axis=0)
     arrays = unpack(in_ref, wide)
     grad_tv[...], out[...], grad_tq[...], grad_tk[...] = (
         arrays[INNER * i : INNER * (i + 1), :] for i in range(4)
@@ -178,12 +174,12 @@
     grads_v = dots(heads(arrays), [probs[h].astype(BF) for h in range(HEADS)], 1, 1)
     grad_sv[...] = jnp.concatenate(grads_v, axis=0).astype(BF)
     grad_sq[...] = normed_back(
-        grads_q[...].astype(F32), unit_q[...], inverse_q[...], column(gain_q)
-    )
-    grad_sk[...] = normed_back(by_head(grads_k), unit_k[...], inverse_k[...], column(gain_k))
-
-
-def gain_middle_kernel(in_ref, ratios, out_ref):
+        grads_q[...].astype(F32), unit_q[...], inverse_q[...], gains[0]
+    )
+    grad_sk[...] = normed_back(by_head(grads_k), unit_k[...], inverse_k[...], gains[1])
+
+
+def gain_middle_kernel(in_ref, out_ref):
     out_ref[...] = jnp.broadcast_to(jnp.sum(in_ref[...], axis=0, keepdims=True), out_ref.shape)
 
 
@@ -263,25 +259,36 @@
         for g in (spatial_query_gain, spatial_key_gain, temporal_query_gain, temporal_key_gain)
     )
     array = shape(INNER, TOKENS)
-    args = (sq_gain, sk_gain, sq, sk, sv, tq, tk, og, tv_in)
+    args = (sq_gain, sk_gain, tq_gain, tk_gain, video_ids, sq, sk, sv, tq, tk, og, tv_in)
     unit, inverse = shape(HEADS, HEAD_DIM, TOKENS, dtype=F32), shape(HEADS, 1, TOKENS, dtype=F32)
     normal, square = shape(HEADS, HEAD_DIM, TOKENS), shape(HEADS, 128, 128)
-    sent, unit_q, unit_k, inverse_q, inverse_k, query, key_in, probs = call(
+    sent, unit_q, unit_k, inverse_q, inverse_k, query, key_in, probs, gain_columns, ratios, same = call(
         send_kernel,
-        (shape(ROWS, 128), unit, unit, inverse, inverse, normal, normal, shape(HEADS, 128, 128, dtype=F32)),
+        (
+            shape(ROWS, 128),
+            unit,
+            unit,
+            inverse,
+            inverse,
+            normal,
+            normal,
+            shape(HEADS, 128, 128, dtype=F32),
+            shape(4, HEAD_DIM, TOKENS, dtype=F32),
+            shape(2, HEAD_DIM, dtype=F32),
+            shape(TOKENS, TOKENS, dtype=F32),
+        ),
         *args,
-        in_hbm=9,
+        in_hbm=12,
         scratch=WIDE + buffers(*args),
     )
     arrived = exchange(sent)
-    args = (video_ids, tq_gain, tk_gain)
     sent, temporal = call(
         temporal_kernel,
-        (shape(ROWS, 128), shape(HEAD_DIM, 1, dtype=F32)),
+        (shape(ROWS, 128), shape(HEAD_DIM, TOKENS, dtype=F32)),
         arrived,
-        *args,
-        in_hbm=3,
-        scratch=WIDE + buffers(*args),
+        gain_columns,
+        same,
+        scratch=WIDE,
     )
     arrived = exchange(sent)
     grads_q, scores, gains = call(
@@ -296,9 +303,9 @@
         scratch=WIDE,
     )
     gains = lax.all_to_all(gains, "z", split_axis=0, concat_axis=0, tiled=True)
-    ratios, out, grad_tq, grad_tk, grad_tv, grad_sq, grad_sk, grad_sv = call(
+    out, grad_tq, grad_tk, grad_tv, grad_sq, grad_sk, grad_sv = call(
         spatial_rest_kernel,
-        (shape(2, HEAD_DIM, dtype=F32),) + (array,) * 7,
+        (array,) * 7,
         arrived,
         unit_q,
         unit_k,
@@ -308,14 +315,11 @@
         probs,
         grads_q,
         scores,
-        sq_gain,
-        sk_gain,
-        tq_gain,
-        tk_gain,
+        gain_columns,
         scratch=WIDE,
         work=3_000_000_000,
     )
-    gains = call(gain_middle_kernel, shape(32, 2, 128, dtype=F32), gains, ratios)
+    gains = call(gain_middle_kernel, shape(32, 2, 128, dtype=F32), gains)
     gains = lax.all_to_all(gains, ("core", "y", "dp"), split_axis=0, concat_axis=0, tiled=True)
     gains = call(gain_last_kernel, (shape(1, HEAD_DIM, dtype=F32),) * 4, gains, ratios)
     results = (out, grad_sq, grad_sk, grad_sv, grad_tq, grad_tk, grad_tv)

time: 135 us -> 134 us (level)
  waiting for transfers between devices: 9.22 us -> 5.58 us
  blocking collectives: 111 us -> 114 us
    all_to_all x1, waiting for transfers between devices: 9.22 us -> 5.58 us  [shards(): lax.all_to_all(gains, ('core', 'y', 'dp'), split_axis=0, concat_axis=0, t...]
    all_to_all x1, blocking collectives: 14.3 us -> 17.3 us  [shards(): gains = lax.all_to_all(gains, 'z', split_axis=0, concat_axis=0, tiled=True)]
where the time goes in v7:
time: 134 us
  blocking collectives  114 us (85%)
  starting transfers between devices  7.21 us (5%)
  Pallas kernels  6.56 us (5%)
  waiting for transfers between devices  5.58 us (4%)
    all_to_all x2, blocking collectives, exchange(): lax.all_to_all(parts, ('z', 'y', 'core'), split_axis=0, concat_axis=0, ti...  96.7 us
    all_to_all x1, blocking collectives, shards(): gains = lax.all_to_all(gains, 'z', split_axis=0, concat_axis=0, tiled=True)  17.3 us
    all_to_all x1, starting transfers between devices, shards(): lax.all_to_all(gains, ('core', 'y', 'dp'), split_axis=0, concat_axis=0, t...  7.21 us
    pallas_call x6, Pallas kernels, call(): pl.pallas_call(kernel, out_shape=out_shape, in_specs=specs, scratch_shape...  6.56 us
    all_to_all x1, waiting for transfers between devices, shards(): lax.all_to_all(gains, ('core', 'y', 'dp'), split_axis=0, concat_axis=0, t...  5.58 us
  transfers between devices with their start and end apart: 1, of which 1 were waited for; matrix products, arithmetic and copies ran while one was open for 0% of the time, Pallas kernels for 1%

profile of v7, /device:TPU:1, one launch (start us, length us, event | category | flops | bytes accessed | tf_op | source)
XLA Modules:
  0.0 134.1 jit_solution(17886104204765983221)
XLA Ops:
  0.6 2.0 %shard_map.203 = (bf16[2304,128]{1,0:T(8,128)(2,1)S(1)}, f32[8,72,128]{2,1,0:T(8,128)S(1)}, f32[8,72,128]{2,1,0:T(8,128)S(1)}, f32[8,1,128]{2,1,0:T(1,128)S(1)},...) custom-call(f32[1,72]{1,0:T(1,128)} %bitcast.67, ...), custom_call_target="tpu_custom_call" | custom-call | tf_op jit(solution)/shard_map/pallas_call | solution.py:208
  2.6 54.1 %all_to_all.20 = bf16[128,9,2,128]{3,2,1,0:T(2,128)(2,1)S(1)} all-to-all(bf16[128,9,2,128]{3,2,1,0:T(2,128)(2,1)S(1)} %bitcast.59), channel_id=1, replica_groups=mesh['dp'=4,'z'=16,'y'=4,'core'=2] {'z','y','core'}, dimensions={0} | all-to-all | bytes 1179648 | tf_op jit(solution)/shard_map/all_to_all | solution.py:227
  56.7 1.3 shard_map.204
  58.0 0.0 copy-start
  58.0 42.6 %all_to_all.21 = bf16[128,9,2,128]{3,2,1,0:T(2,128)(2,1)S(1)} all-to-all(bf16[128,9,2,128]{3,2,1,0:T(2,128)(2,1)S(1)} %bitcast.60), channel_id=1, replica_groups=mesh['dp'=4,'z'=16,'y'=4,'core'=2] {'z','y','core'}, dimensions={0} | all-to-all | bytes 1179648 | tf_op jit(solution)/shard_map/all_to_all | solution.py:227
  100.6 0.0 copy-done
  100.6 0.6 shard_map.205
  101.3 17.3 %all_to_all.22.in_ref = f32[16,2,128]{2,1,0:T(2,128)S(1)} all-to-all(f32[16,2,128]{2,1,0:T(2,128)S(1)} %get-tuple-element.59), channel_id=1, replica_groups=mesh['dp'=4,'z'=16,'y'=4,'core'=2] {'z'}, dimensions={0} | all-to-all | bytes 32768 | tf_op jit(solution)/shard_map/all_to_all | solution.py:305
  118.6 0.6 shard_map.207
  119.2 7.2 %all-to-all-start.3 = ((f32[32,2,128]{2,1,0:T(2,128)}), f32[32,2,128]{2,1,0:T(2,128)S(1)}, u32[]{:S(2)}, u32[]{:S(2)}) async-start(f32[32,2,128]{2,1,0:T(2,128)} %shard_map.207), calls=%async_computation.3 | async-start | bytes 65536 | tf_op jit(solution)/shard_map/all_to_all | solution.py:323
  126.5 1.4 %shard_map.206 = (bf16[576,128]{1,0:T(8,128)(2,1)}, bf16[576,128]{1,0:T(8,128)(2,1)}, bf16[576,128]{1,0:T(8,128)(2,1)}, bf16[576,128]{1,0:T(8,128)(2,1)}, bf16[5...) custom-call(bf16[2304,128]{1,0:T(8,128)(2,1)S(1)} %bitcast.55, ...), custom_call_target="tpu_custom_call" | custom-call | flops 3000000000 | tf_op jit(solution)/shard_map/pallas_call | solution.py:208
  127.9 5.6 %all-to-all-done.3.in_ref = f32[32,2,128]{2,1,0:T(2,128)S(1)} async-done(((f32[32,2,128]{2,1,0:T(2,128)}), f32[32,2,128]{2,1,0:T(2,128)S(1)}, u32[]{:S(2)}, u32[]{:S(2)}) %all-to-all-start.3) | async-done | bytes 32800 | tf_op jit(solution)/shard_map/all_to_all | solution.py:323
  133.4 0.6 shard_map.208
Async XLA Ops:
  58.0 42.6 %copy-start = (bf16[1,1,128,576]{2,3,1,0:T(8,128)(2,1)S(1)}, bf16[1,1,128,576]{2,3,1,0:T(8,128)(2,1)}, u32[]{:S(2)}) copy-start(bf16[1,1,128,576]{2,3,1,0:T(8,128)(2,1)} %param.14) | copy-start | bytes 442372
  119.2 14.2 %all-to-all-start.3 = ((f32[32,2,128]{2,1,0:T(2,128)}), f32[32,2,128]{2,1,0:T(2,128)S(1)}, u32[]{:S(2)}, u32[]{:S(2)}) async-start(f32[32,2,128]{2,1,0:T(2,128)} %shard_map.207), calls=%async_computation.3 | async-start | bytes 65536 | tf_op jit(solution)/shard_map/all_to_all | solution.py:323

commit v8 on v7

--- a/solution.py
+++ b/solution.py
@@ -29,11 +29,11 @@
     for tile in range(TILES):
         turned = features[128 * tile : 128 * tile + 128, :].T
         wide[pl.ds(tile, TOKENS, stride=TILES), :] = turned.astype(F32)
-    out_ref[...] = wide[...].astype(BF)
+    out_ref[...] = wide[:ROWS, :].astype(BF)
 
 
 def unpack(in_ref, wide, wanted=None):
-    wide[...] = in_ref[...].astype(F32)
+    wide[:ROWS, :] = in_ref[...].astype(F32)
     tiles = [wide[pl.ds(tile, TOKENS, stride=TILES), :] for tile in range(wanted or TILES)]
     return jnp.concatenate([tile.astype(BF).T for tile in tiles], axis=0)
 
@@ -103,12 +103,14 @@
     wide, buffers, sems = refs[11], refs[12:-1], refs[-1]
     copies = load(sources, buffers, sems)
     *rows, ids, sq, sk, sv, tq, tk, og, tv_in = buffers
-    for copy in copies[:7]:
+    for copy in copies[:5]:
         copy.wait()
     for i in range(4):
         gains[i] = jnp.broadcast_to(column(rows[i]), (HEAD_DIM, TOKENS))
     ratios[...] = jnp.concatenate([rows[0][...] / rows[1][...], rows[2][...] / rows[3][...]], axis=0)
     same[...] = same_video(ids[...])
+    for copy in copies[5:7]:
+        copy.wait()
     unit_q[...], inverse_q[...], query[...] = normed(sq[...], gains[0])
     unit_k[...], inverse_k[...], key_in[...] = normed(sk[...], gains[1])
     found = probabilities(query, key_in, None)
@@ -219,7 +221,7 @@
     return [pltpu.VMEM(a.shape, a.dtype) for a in arrays] + [pltpu.SemaphoreType.DMA((len(arrays),))]
 
 
-WIDE = [pltpu.VMEM((ROWS, 128), F32)]
+WIDE = [pltpu.VMEM((ROWS + 24, 128), F32)]
 
 
 def exchange(message):
@@ -320,7 +322,7 @@
         work=3_000_000_000,
     )
     gains = call(gain_middle_kernel, shape(32, 2, 128, dtype=F32), gains)
-    gains = lax.all_to_all(gains, ("core", "y", "dp"), split_axis=0, concat_axis=0, tiled=True)
+    gains = lax.all_to_all(gains, ("dp", "core", "y"), split_axis=0, concat_axis=0, tiled=True)
     gains = call(gain_last_kernel, (shape(1, HEAD_DIM, dtype=F32),) * 4, gains, ratios)
     results = (out, grad_sq, grad_sk, grad_sv, grad_tq, grad_tk, grad_tv)
     return tuple(a.T.reshape(1, 1, TOKENS, INNER) for a in results) + tuple(

time: 134 us -> 135 us (level)
  no operation moved by 1% of the time
where the time goes in v8:
time: 135 us; the launch traced here: 134 us
  blocking collectives  114 us (84%)
  starting transfers between devices  7.2 us (5%)
  Pallas kernels  6.51 us (5%)
  waiting for transfers between devices  5.82 us (4%)
    all_to_all x2, blocking collectives, exchange(): lax.all_to_all(parts, ('z', 'y', 'core'), split_axis=0, concat_axis=0, ti...  96.7 us
    all_to_all x1, blocking collectives, shards(): gains = lax.all_to_all(gains, 'z', split_axis=0, concat_axis=0, tiled=True)  17.3 us
    all_to_all x1, starting transfers between devices, shards(): lax.all_to_all(gains, ('dp', 'core', 'y'), split_axis=0, concat_axis=0, t...  7.2 us
    pallas_call x6, Pallas kernels, call(): pl.pallas_call(kernel, out_shape=out_shape, in_specs=specs, scratch_shape...  6.51 us
    all_to_all x1, waiting for transfers between devices, shards(): lax.all_to_all(gains, ('dp', 'core', 'y'), split_axis=0, concat_axis=0, t...  5.82 us
  transfers between devices with their start and end apart: 1, of which 1 were waited for; matrix products, arithmetic and copies ran while one was open for 0% of the time, Pallas kernels for 1%

profile of v8, /device:TPU:1, one launch (start us, length us, event | category | flops | bytes accessed | tf_op | source)
XLA Modules:
  0.0 134.2 jit_solution(4857431686425094762)
XLA Ops:
  0.6 1.9 %shard_map.203 = (bf16[2304,128]{1,0:T(8,128)(2,1)S(1)}, f32[8,72,128]{2,1,0:T(8,128)S(1)}, f32[8,72,128]{2,1,0:T(8,128)S(1)}, f32[8,1,128]{2,1,0:T(1,128)S(1)},...) custom-call(f32[1,72]{1,0:T(1,128)} %bitcast.67, ...), custom_call_target="tpu_custom_call" | custom-call | tf_op jit(solution)/shard_map/pallas_call | solution.py:210
  2.6 54.1 %all_to_all.20 = bf16[128,9,2,128]{3,2,1,0:T(2,128)(2,1)S(1)} all-to-all(bf16[128,9,2,128]{3,2,1,0:T(2,128)(2,1)S(1)} %bitcast.59), channel_id=1, replica_groups=mesh['dp'=4,'z'=16,'y'=4,'core'=2] {'z','y','core'}, dimensions={0} | all-to-all | bytes 1179648 | tf_op jit(solution)/shard_map/all_to_all | solution.py:229
  56.7 1.3 shard_map.204
  58.0 0.0 copy-start
  58.0 42.6 %all_to_all.21 = bf16[128,9,2,128]{3,2,1,0:T(2,128)(2,1)S(1)} all-to-all(bf16[128,9,2,128]{3,2,1,0:T(2,128)(2,1)S(1)} %bitcast.60), channel_id=1, replica_groups=mesh['dp'=4,'z'=16,'y'=4,'core'=2] {'z','y','core'}, dimensions={0} | all-to-all | bytes 1179648 | tf_op jit(solution)/shard_map/all_to_all | solution.py:229
  100.6 0.0 copy-done
  100.6 0.6 shard_map.205
  101.3 17.3 %all_to_all.22.in_ref = f32[16,2,128]{2,1,0:T(2,128)S(1)} all-to-all(f32[16,2,128]{2,1,0:T(2,128)S(1)} %get-tuple-element.59), channel_id=1, replica_groups=mesh['dp'=4,'z'=16,'y'=4,'core'=2] {'z'}, dimensions={0} | all-to-all | bytes 32768 | tf_op jit(solution)/shard_map/all_to_all | solution.py:307
  118.6 0.6 shard_map.207
  119.2 7.2 %all-to-all-start.3 = ((f32[32,2,128]{2,1,0:T(2,128)}), f32[32,2,128]{2,1,0:T(2,128)S(1)}, u32[]{:S(2)}, u32[]{:S(2)}) async-start(f32[32,2,128]{2,1,0:T(2,128)} %shard_map.207), calls=%async_computation.3 | async-start | bytes 65536 | tf_op jit(solution)/shard_map/all_to_all | solution.py:325
  126.4 1.4 %shard_map.206 = (bf16[576,128]{1,0:T(8,128)(2,1)}, bf16[576,128]{1,0:T(8,128)(2,1)}, bf16[576,128]{1,0:T(8,128)(2,1)}, bf16[576,128]{1,0:T(8,128)(2,1)}, bf16[5...) custom-call(bf16[2304,128]{1,0:T(8,128)(2,1)S(1)} %bitcast.55, ...), custom_call_target="tpu_custom_call" | custom-call | flops 3000000000 | tf_op jit(solution)/shard_map/pallas_call | solution.py:210
  127.8 5.8 %all-to-all-done.3.in_ref = f32[32,2,128]{2,1,0:T(2,128)S(1)} async-done(((f32[32,2,128]{2,1,0:T(2,128)}), f32[32,2,128]{2,1,0:T(2,128)S(1)}, u32[]{:S(2)}, u32[]{:S(2)}) %all-to-all-start.3) | async-done | bytes 32800 | tf_op jit(solution)/shard_map/all_to_all | solution.py:325
  133.6 0.6 shard_map.208
Async XLA Ops:
  58.0 42.6 %copy-start = (bf16[1,1,128,576]{2,3,1,0:T(8,128)(2,1)S(1)}, bf16[1,1,128,576]{2,3,1,0:T(8,128)(2,1)}, u32[]{:S(2)}) copy-start(bf16[1,1,128,576]{2,3,1,0:T(8,128)(2,1)} %param.14) | copy-start | bytes 442372
  119.2 14.4 %all-to-all-start.3 = ((f32[32,2,128]{2,1,0:T(2,128)}), f32[32,2,128]{2,1,0:T(2,128)S(1)}, u32[]{:S(2)}, u32[]{:S(2)}) async-start(f32[32,2,128]{2,1,0:T(2,128)} %shard_map.207), calls=%async_computation.3 | async-start | bytes 65536 | tf_op jit(solution)/shard_map/all_to_all | solution.py:325

commit v9 on v8

--- a/solution.py
+++ b/solution.py
@@ -118,7 +118,7 @@
         copy.wait()
     for h in range(HEADS):
         probs[h] = found[h]
-    mixed = dots(heads(sv), [p.astype(BF) for p in found], 1, 0)
+    mixed = dots(heads(sv[...]), [p.astype(BF) for p in found], 1, 0)
     spatial = jnp.concatenate(mixed, axis=0).astype(BF)
     total = (tv_in[...].astype(F32) + spatial.astype(F32)).astype(BF)
     pack(jnp.concatenate([tq[...], tk[...], og[...], total], axis=0), wide, out_ref)
@@ -151,7 +151,7 @@
 
 def spatial_gain_kernel(in_ref, sv, unit_q, key_in, probs, temporal, grads_q, scores, out_ref, wide):
     given = unpack(in_ref, wide, 5)
-    found = scores_back([probs[h] for h in range(HEADS)], dots(heads(sv), heads(given), 0, 0))
+    found = scores_back([probs[h] for h in range(HEADS)], dots(heads(sv[...]), heads(given), 0, 0))
     products = [p.astype(BF) for p in dots(key_in, found, 1, 0)]
     for h in range(HEADS):
         scores[h] = found[h]

time: 135 us -> 135 us (level)
  no operation moved by 1% of the time
where the time goes in v9:
time: 135 us; the launch traced here: 134 us
  blocking collectives  114 us (84%)
  starting transfers between devices  7.2 us (5%)
  Pallas kernels  6.51 us (5%)
  waiting for transfers between devices  5.82 us (4%)
    all_to_all x2, blocking collectives, exchange(): lax.all_to_all(parts, ('z', 'y', 'core'), split_axis=0, concat_axis=0, ti...  96.7 us
    all_to_all x1, blocking collectives, shards(): gains = lax.all_to_all(gains, 'z', split_axis=0, concat_axis=0, tiled=True)  17.3 us
    all_to_all x1, starting transfers between devices, shards(): lax.all_to_all(gains, ('dp', 'core', 'y'), split_axis=0, concat_axis=0, t...  7.2 us
    pallas_call x6, Pallas kernels, call(): pl.pallas_call(kernel, out_shape=out_shape, in_specs=specs, scratch_shape...  6.51 us
    all_to_all x1, waiting for transfers between devices, shards(): lax.all_to_all(gains, ('dp', 'core', 'y'), split_axis=0, concat_axis=0, t...  5.82 us
  transfers between devices with their start and end apart: 1, of which 1 were waited for; matrix products, arithmetic and copies ran while one was open for 0% of the time, Pallas kernels for 1%

profile of v9, /device:TPU:1, one launch (start us, length us, event | category | flops | bytes accessed | tf_op | source)
XLA Modules:
  0.0 134.2 jit_solution(4857431686425094762)
XLA Ops:
  0.6 1.9 %shard_map.203 = (bf16[2304,128]{1,0:T(8,128)(2,1)S(1)}, f32[8,72,128]{2,1,0:T(8,128)S(1)}, f32[8,72,128]{2,1,0:T(8,128)S(1)}, f32[8,1,128]{2,1,0:T(1,128)S(1)},...) custom-call(f32[1,72]{1,0:T(1,128)} %bitcast.67, ...), custom_call_target="tpu_custom_call" | custom-call | tf_op jit(solution)/shard_map/pallas_call | solution.py:210
  2.6 54.1 %all_to_all.20 = bf16[128,9,2,128]{3,2,1,0:T(2,128)(2,1)S(1)} all-to-all(bf16[128,9,2,128]{3,2,1,0:T(2,128)(2,1)S(1)} %bitcast.59), channel_id=1, replica_groups=mesh['dp'=4,'z'=16,'y'=4,'core'=2] {'z','y','core'}, dimensions={0} | all-to-all | bytes 1179648 | tf_op jit(solution)/shard_map/all_to_all | solution.py:229
  56.7 1.3 shard_map.204
  58.0 0.0 copy-start
  58.0 42.6 %all_to_all.21 = bf16[128,9,2,128]{3,2,1,0:T(2,128)(2,1)S(1)} all-to-all(bf16[128,9,2,128]{3,2,1,0:T(2,128)(2,1)S(1)} %bitcast.60), channel_id=1, replica_groups=mesh['dp'=4,'z'=16,'y'=4,'core'=2] {'z','y','core'}, dimensions={0} | all-to-all | bytes 1179648 | tf_op jit(solution)/shard_map/all_to_all | solution.py:229
  100.6 0.0 copy-done
  100.6 0.6 shard_map.205
  101.3 17.3 %all_to_all.22.in_ref = f32[16,2,128]{2,1,0:T(2,128)S(1)} all-to-all(f32[16,2,128]{2,1,0:T(2,128)S(1)} %get-tuple-element.59), channel_id=1, replica_groups=mesh['dp'=4,'z'=16,'y'=4,'core'=2] {'z'}, dimensions={0} | all-to-all | bytes 32768 | tf_op jit(solution)/shard_map/all_to_all | solution.py:307
  118.6 0.6 shard_map.207
  119.2 7.2 %all-to-all-start.3 = ((f32[32,2,128]{2,1,0:T(2,128)}), f32[32,2,128]{2,1,0:T(2,128)S(1)}, u32[]{:S(2)}, u32[]{:S(2)}) async-start(f32[32,2,128]{2,1,0:T(2,128)} %shard_map.207), calls=%async_computation.3 | async-start | bytes 65536 | tf_op jit(solution)/shard_map/all_to_all | solution.py:325
  126.4 1.4 %shard_map.206 = (bf16[576,128]{1,0:T(8,128)(2,1)}, bf16[576,128]{1,0:T(8,128)(2,1)}, bf16[576,128]{1,0:T(8,128)(2,1)}, bf16[576,128]{1,0:T(8,128)(2,1)}, bf16[5...) custom-call(bf16[2304,128]{1,0:T(8,128)(2,1)S(1)} %bitcast.55, ...), custom_call_target="tpu_custom_call" | custom-call | flops 3000000000 | tf_op jit(solution)/shard_map/pallas_call | solution.py:210
  127.8 5.8 %all-to-all-done.3.in_ref = f32[32,2,128]{2,1,0:T(2,128)S(1)} async-done(((f32[32,2,128]{2,1,0:T(2,128)}), f32[32,2,128]{2,1,0:T(2,128)S(1)}, u32[]{:S(2)}, u32[]{:S(2)}) %all-to-all-start.3) | async-done | bytes 32800 | tf_op jit(solution)/shard_map/all_to_all | solution.py:325
  133.6 0.6 shard_map.208
Async XLA Ops:
  58.0 42.6 %copy-start = (bf16[1,1,128,576]{2,3,1,0:T(8,128)(2,1)S(1)}, bf16[1,1,128,576]{2,3,1,0:T(8,128)(2,1)}, u32[]{:S(2)}) copy-start(bf16[1,1,128,576]{2,3,1,0:T(8,128)(2,1)} %param.14) | copy-start | bytes 442372
  119.2 14.4 %all-to-all-start.3 = ((f32[32,2,128]{2,1,0:T(2,128)}), f32[32,2,128]{2,1,0:T(2,128)S(1)}, u32[]{:S(2)}, u32[]{:S(2)}) async-start(f32[32,2,128]{2,1,0:T(2,128)} %shard_map.207), calls=%async_computation.3 | async-start | bytes 65536 | tf_op jit(solution)/shard_map/all_to_all | solution.py:325

commit v10 on v9

--- a/solution.py
+++ b/solution.py
@@ -164,21 +164,30 @@
     out_ref[...] = jnp.broadcast_to(rows[None], out_ref.shape)
 
 
-def spatial_rest_kernel(
-    in_ref, unit_q, unit_k, inverse_q, inverse_k, query, probs, grads_q, scores, gains,
-    out, grad_tq, grad_tk, grad_tv, grad_sq, grad_sk, grad_sv, wide
-):
+def spatial_rest_kernel(*refs):
+    in_ref, unit_q, unit_k, inverse_q, inverse_k, query, probs, grads_q, scores, gains, sums, ratios = refs[:12]
+    targets, wide, results, sems = refs[12:23], refs[23], refs[24:35], refs[35]
+    copies = [pltpu.make_async_copy(r, t, sems.at[i]) for i, (r, t) in enumerate(zip(results, targets))]
+    out, grad_tq, grad_tk, grad_tv, grad_sq, grad_sk, grad_sv, *gain_grads = results
+    gain_last_kernel(sums, ratios, *gain_grads)
     arrays = unpack(in_ref, wide)
     grad_tv[...], out[...], grad_tq[...], grad_tk[...] = (
         arrays[INNER * i : INNER * (i + 1), :] for i in range(4)
     )
+    for copy in copies[:4] + copies[7:]:
+        copy.start()
     grads_k = dots(query, scores, 1, 1)
     grads_v = dots(heads(arrays), [probs[h].astype(BF) for h in range(HEADS)], 1, 1)
     grad_sv[...] = jnp.concatenate(grads_v, axis=0).astype(BF)
+    copies[6].start()
     grad_sq[...] = normed_back(
         grads_q[...].astype(F32), unit_q[...], inverse_q[...], gains[0]
     )
+    copies[4].start()
     grad_sk[...] = normed_back(by_head(grads_k), unit_k[...], inverse_k[...], gains[1])
+    copies[5].start()
+    for copy in copies:
+        copy.wait()
 
 
 def gain_middle_kernel(in_ref, out_ref):
@@ -199,7 +208,7 @@
     return jax.ShapeDtypeStruct(extent, dtype)
 
 
-def call(kernel, out_shape, *args, in_hbm=0, scratch=(), work=0, vmem=32):
+def call(kernel, out_shape, *args, in_hbm=0, scratch=(), work=0, vmem=32, out_hbm=False):
     specs = [pl.BlockSpec(memory_space=pltpu.VMEM)] * (len(args) - in_hbm)
     specs += [pl.BlockSpec(memory_space=pltpu.HBM)] * in_hbm
     split = len(args) - in_hbm
@@ -207,9 +216,11 @@
         pltpu.with_memory_space_constraint(a, pltpu.HBM) for a in args[split:]
     )
     cost = pl.CostEstimate(flops=work, bytes_accessed=0, transcendentals=0) if work else None
+    out_space = pltpu.HBM if out_hbm else pltpu.VMEM
     return pl.pallas_call(
         kernel,
         out_shape=out_shape,
+        out_specs=jax.tree.map(lambda _: pl.BlockSpec(memory_space=out_space), out_shape),
         in_specs=specs,
         scratch_shapes=scratch,
         compiler_params=pltpu.CompilerParams(vmem_limit_bytes=vmem * MIB),
@@ -305,9 +316,12 @@
         scratch=WIDE,
     )
     gains = lax.all_to_all(gains, "z", split_axis=0, concat_axis=0, tiled=True)
-    out, grad_tq, grad_tk, grad_tv, grad_sq, grad_sk, grad_sv = call(
+    gains = call(gain_middle_kernel, shape(32, 2, 128, dtype=F32), gains)
+    gains = lax.all_to_all(gains, ("dp", "core", "y"), split_axis=0, concat_axis=0, tiled=True)
+    rest = (array,) * 7 + (shape(1, HEAD_DIM, dtype=F32),) * 4
+    out, grad_tq, grad_tk, grad_tv, grad_sq, grad_sk, grad_sv, *gains = call(
         spatial_rest_kernel,
-        (array,) * 7,
+        rest,
         arrived,
         unit_q,
         unit_k,
@@ -318,12 +332,11 @@
         grads_q,
         scores,
         gain_columns,
-        scratch=WIDE,
-        work=3_000_000_000,
-    )
-    gains = call(gain_middle_kernel, shape(32, 2, 128, dtype=F32), gains)
-    gains = lax.all_to_all(gains, ("dp", "core", "y"), split_axis=0, concat_axis=0, tiled=True)
-    gains = call(gain_last_kernel, (shape(1, HEAD_DIM, dtype=F32),) * 4, gains, ratios)
+        gains,
+        ratios,
+        scratch=WIDE + [pltpu.VMEM(r.shape, r.dtype) for r in rest] + [pltpu.SemaphoreType.DMA((11,))],
+        out_hbm=True,
+    )
     results = (out, grad_sq, grad_sk, grad_sv, grad_tq, grad_tk, grad_tv)
     return tuple(a.T.reshape(1, 1, TOKENS, INNER) for a in results) + tuple(
         g.reshape(HEAD_DIM) for g in gains

time: 135 us -> 135 us (level)
  blocking collectives: 114 us -> 128 us
  starting transfers between devices: 7.2 us -> 0 us
  waiting for transfers between devices: 5.82 us -> 0 us
    all_to_all x0 -> x1, blocking collectives: none -> 14.2 us  [shards(): lax.all_to_all(gains, ('dp', 'core', 'y'), split_axis=0, concat_axis=0, t...]
    all_to_all x1 -> x0, starting transfers between devices: 7.2 us -> none  [shards(): lax.all_to_all(gains, ('dp', 'core', 'y'), split_axis=0, concat_axis=0, t...]
    all_to_all x1 -> x0, waiting for transfers between devices: 5.82 us -> none  [shards(): lax.all_to_all(gains, ('dp', 'core', 'y'), split_axis=0, concat_axis=0, t...]
    pallas_call x6 -> x5, Pallas kernels: 6.51 us -> 5.45 us  [call(): pl.pallas_call(kernel, out_shape=out_shape, out_specs=jax.tree.map(lambda...]
  transfers between devices with their start and end apart: 1 -> 0, of which waited for: 1 -> 0; matrix products, arithmetic and copies ran while one was open for 0% -> 0% of each run, Pallas kernels for 1% -> 0%
where the time goes in v10:
time: 135 us; the launch traced here: 134 us
  blocking collectives  128 us (95%)
  Pallas kernels  5.45 us (4%)
    all_to_all x2, blocking collectives, exchange(): lax.all_to_all(parts, ('z', 'y', 'core'), split_axis=0, concat_axis=0, ti...  96.7 us
    all_to_all x1, blocking collectives, shards(): gains = lax.all_to_all(gains, 'z', split_axis=0, concat_axis=0, tiled=True)  17.3 us
    all_to_all x1, blocking collectives, shards(): lax.all_to_all(gains, ('dp', 'core', 'y'), split_axis=0, concat_axis=0, t...  14.2 us
    pallas_call x5, Pallas kernels, call(): pl.pallas_call(kernel, out_shape=out_shape, out_specs=jax.tree.map(lambda...  5.45 us

profile of v10, /device:TPU:1, one launch (start us, length us, event | category | flops | bytes accessed | tf_op | source)
XLA Modules:
  0.0 134.4 jit_solution(11605437038043180916)
XLA Ops:
  0.6 1.9 %shard_map.203 = (bf16[2304,128]{1,0:T(8,128)(2,1)S(1)}, f32[8,72,128]{2,1,0:T(8,128)S(1)}, f32[8,72,128]{2,1,0:T(8,128)S(1)}, f32[8,1,128]{2,1,0:T(1,128)S(1)},...) custom-call(f32[1,72]{1,0:T(1,128)} %bitcast.67, ...), custom_call_target="tpu_custom_call" | custom-call | tf_op jit(solution)/shard_map/pallas_call | solution.py:220
  2.6 54.1 %all_to_all.20 = bf16[128,9,2,128]{3,2,1,0:T(2,128)(2,1)S(1)} all-to-all(bf16[128,9,2,128]{3,2,1,0:T(2,128)(2,1)S(1)} %bitcast.59), channel_id=1, replica_groups=mesh['dp'=4,'z'=16,'y'=4,'core'=2] {'z','y','core'}, dimensions={0} | all-to-all | bytes 1179648 | tf_op jit(solution)/shard_map/all_to_all | solution.py:240
  56.7 1.3 shard_map.204
  58.0 0.0 copy-start
  58.0 42.6 %all_to_all.21 = bf16[128,9,2,128]{3,2,1,0:T(2,128)(2,1)S(1)} all-to-all(bf16[128,9,2,128]{3,2,1,0:T(2,128)(2,1)S(1)} %bitcast.60), channel_id=1, replica_groups=mesh['dp'=4,'z'=16,'y'=4,'core'=2] {'z','y','core'}, dimensions={0} | all-to-all | bytes 1179648 | tf_op jit(solution)/shard_map/all_to_all | solution.py:240
  100.6 0.0 copy-done
  100.6 0.6 shard_map.205
  101.3 17.3 %all_to_all.22.in_ref = f32[16,2,128]{2,1,0:T(2,128)S(1)} all-to-all(f32[16,2,128]{2,1,0:T(2,128)S(1)} %get-tuple-element.52), channel_id=1, replica_groups=mesh['dp'=4,'z'=16,'y'=4,'core'=2] {'z'}, dimensions={0} | all-to-all | bytes 32768 | tf_op jit(solution)/shard_map/all_to_all | solution.py:318
  118.6 14.2 %all_to_all.23.refs_10_ = f32[32,2,128]{2,1,0:T(2,128)S(1)} all-to-all(f32[32,2,128]{2,1,0:T(2,128)S(1)} %shard_map.206), channel_id=1, replica_groups=mesh['dp'=4,'z'=16,'y'=4,'core'=2] {'dp','core','y'}, dimensions={0} | all-to-all | bytes 65536 | tf_op jit(solution)/shard_map/all_to_all | solution.py:320
  132.8 1.5 %shard_map.207 = (bf16[576,128]{1,0:T(8,128)(2,1)}, bf16[576,128]{1,0:T(8,128)(2,1)}, bf16[576,128]{1,0:T(8,128)(2,1)}, bf16[576,128]{1,0:T(8,128)(2,1)}, bf16[5...) custom-call(bf16[2304,128]{1,0:T(8,128)(2,1)S(1)} %bitcast.55, ...), custom_call_target="tpu_custom_call" | custom-call | tf_op jit(solution)/shard_map/pallas_call | solution.py:220
  (1 shorter events, 0.0 us)
Async XLA Ops:
  58.0 42.6 %copy-start = (bf16[1,1,128,576]{2,3,1,0:T(8,128)(2,1)S(1)}, bf16[1,1,128,576]{2,3,1,0:T(8,128)(2,1)}, u32[]{:S(2)}) copy-start(bf16[1,1,128,576]{2,3,1,0:T(8,128)(2,1)} %param.14) | copy-start | bytes 442372

commit v11 on v9

--- a/solution.py
+++ b/solution.py
@@ -165,9 +165,10 @@
 
 
 def spatial_rest_kernel(
-    in_ref, unit_q, unit_k, inverse_q, inverse_k, query, probs, grads_q, scores, gains,
-    out, grad_tq, grad_tk, grad_tv, grad_sq, grad_sk, grad_sv, wide
+    in_ref, unit_q, unit_k, inverse_q, inverse_k, query, probs, grads_q, scores, gains, sums, ratios,
+    out, grad_tq, grad_tk, grad_tv, grad_sq, grad_sk, grad_sv, gain_sq, gain_sk, gain_tq, gain_tk, wide
 ):
+    gain_last_kernel(sums, ratios, gain_sq, gain_sk, gain_tq, gain_tk)
     arrays = unpack(in_ref, wide)
     grad_tv[...], out[...], grad_tq[...], grad_tk[...] = (
         arrays[INNER * i : INNER * (i + 1), :] for i in range(4)
@@ -305,9 +306,11 @@
         scratch=WIDE,
     )
     gains = lax.all_to_all(gains, "z", split_axis=0, concat_axis=0, tiled=True)
-    out, grad_tq, grad_tk, grad_tv, grad_sq, grad_sk, grad_sv = call(
+    gains = call(gain_middle_kernel, shape(32, 2, 128, dtype=F32), gains)
+    gains = lax.all_to_all(gains, ("dp", "core", "y"), split_axis=0, concat_axis=0, tiled=True)
+    out, grad_tq, grad_tk, grad_tv, grad_sq, grad_sk, grad_sv, *gains = call(
         spatial_rest_kernel,
-        (array,) * 7,
+        (array,) * 7 + (shape(1, HEAD_DIM, dtype=F32),) * 4,
         arrived,
         unit_q,
         unit_k,
@@ -318,12 +321,10 @@
         grads_q,
         scores,
         gain_columns,
+        gains,
+        ratios,
         scratch=WIDE,
-        work=3_000_000_000,
-    )
-    gains = call(gain_middle_kernel, shape(32, 2, 128, dtype=F32), gains)
-    gains = lax.all_to_all(gains, ("dp", "core", "y"), split_axis=0, concat_axis=0, tiled=True)
-    gains = call(gain_last_kernel, (shape(1, HEAD_DIM, dtype=F32),) * 4, gains, ratios)
+    )
     results = (out, grad_sq, grad_sk, grad_sv, grad_tq, grad_tk, grad_tv)
     return tuple(a.T.reshape(1, 1, TOKENS, INNER) for a in results) + tuple(
         g.reshape(HEAD_DIM) for g in gains

time: 135 us -> 135 us (level)
  blocking collectives: 114 us -> 128 us
  starting transfers between devices: 7.2 us -> 0 us
  waiting for transfers between devices: 5.82 us -> 0 us
    all_to_all x0 -> x1, blocking collectives: none -> 14.2 us  [shards(): lax.all_to_all(gains, ('dp', 'core', 'y'), split_axis=0, concat_axis=0, t...]
    all_to_all x1 -> x0, starting transfers between devices: 7.2 us -> none  [shards(): lax.all_to_all(gains, ('dp', 'core', 'y'), split_axis=0, concat_axis=0, t...]
    all_to_all x1 -> x0, waiting for transfers between devices: 5.82 us -> none  [shards(): lax.all_to_all(gains, ('dp', 'core', 'y'), split_axis=0, concat_axis=0, t...]
    pallas_call x6 -> x5, Pallas kernels: 6.51 us -> 5.32 us  [call(): pl.pallas_call(kernel, out_shape=out_shape, in_specs=specs, scratch_shape...]
  transfers between devices with their start and end apart: 1 -> 0, of which waited for: 1 -> 0; matrix products, arithmetic and copies ran while one was open for 0% -> 0% of each run, Pallas kernels for 1% -> 0%
where the time goes in v11:
time: 135 us; the launch traced here: 134 us
  blocking collectives  128 us (95%)
  Pallas kernels  5.32 us (4%)
    all_to_all x2, blocking collectives, exchange(): lax.all_to_all(parts, ('z', 'y', 'core'), split_axis=0, concat_axis=0, ti...  96.7 us
    all_to_all x1, blocking collectives, shards(): gains = lax.all_to_all(gains, 'z', split_axis=0, concat_axis=0, tiled=True)  17.3 us
    all_to_all x1, blocking collectives, shards(): lax.all_to_all(gains, ('dp', 'core', 'y'), split_axis=0, concat_axis=0, t...  14.2 us
    pallas_call x5, Pallas kernels, call(): pl.pallas_call(kernel, out_shape=out_shape, in_specs=specs, scratch_shape...  5.32 us

profile of v11, /device:TPU:1, one launch (start us, length us, event | category | flops | bytes accessed | tf_op | source)
XLA Modules:
  0.0 134.2 jit_solution(9877550946779127)
XLA Ops:
  0.6 1.9 %shard_map.203 = (bf16[2304,128]{1,0:T(8,128)(2,1)S(1)}, f32[8,72,128]{2,1,0:T(8,128)S(1)}, f32[8,72,128]{2,1,0:T(8,128)S(1)}, f32[8,1,128]{2,1,0:T(1,128)S(1)},...) custom-call(f32[1,72]{1,0:T(1,128)} %bitcast.67, ...), custom_call_target="tpu_custom_call" | custom-call | tf_op jit(solution)/shard_map/pallas_call | solution.py:211
  2.6 54.1 %all_to_all.20 = bf16[128,9,2,128]{3,2,1,0:T(2,128)(2,1)S(1)} all-to-all(bf16[128,9,2,128]{3,2,1,0:T(2,128)(2,1)S(1)} %bitcast.59), channel_id=1, replica_groups=mesh['dp'=4,'z'=16,'y'=4,'core'=2] {'z','y','core'}, dimensions={0} | all-to-all | bytes 1179648 | tf_op jit(solution)/shard_map/all_to_all | solution.py:230
  56.7 1.3 shard_map.204
  58.0 0.0 copy-start
  58.0 42.6 %all_to_all.21 = bf16[128,9,2,128]{3,2,1,0:T(2,128)(2,1)S(1)} all-to-all(bf16[128,9,2,128]{3,2,1,0:T(2,128)(2,1)S(1)} %bitcast.60), channel_id=1, replica_groups=mesh['dp'=4,'z'=16,'y'=4,'core'=2] {'z','y','core'}, dimensions={0} | all-to-all | bytes 1179648 | tf_op jit(solution)/shard_map/all_to_all | solution.py:230
  100.6 0.0 copy-done
  100.6 0.6 shard_map.205
  101.3 17.3 %all_to_all.22.in_ref = f32[16,2,128]{2,1,0:T(2,128)S(1)} all-to-all(f32[16,2,128]{2,1,0:T(2,128)S(1)} %get-tuple-element.52), channel_id=1, replica_groups=mesh['dp'=4,'z'=16,'y'=4,'core'=2] {'z'}, dimensions={0} | all-to-all | bytes 32768 | tf_op jit(solution)/shard_map/all_to_all | solution.py:308
  118.6 14.2 %all_to_all.23.sums = f32[32,2,128]{2,1,0:T(2,128)S(1)} all-to-all(f32[32,2,128]{2,1,0:T(2,128)S(1)} %shard_map.206), channel_id=1, replica_groups=mesh['dp'=4,'z'=16,'y'=4,'core'=2] {'dp','core','y'}, dimensions={0} | all-to-all | bytes 65536 | tf_op jit(solution)/shard_map/all_to_all | solution.py:310
  132.8 1.4 %shard_map.207 = (bf16[576,128]{1,0:T(8,128)(2,1)}, bf16[576,128]{1,0:T(8,128)(2,1)}, bf16[576,128]{1,0:T(8,128)(2,1)}, bf16[576,128]{1,0:T(8,128)(2,1)}, bf16[5...) custom-call(bf16[2304,128]{1,0:T(8,128)(2,1)S(1)} %bitcast.55, ...), custom_call_target="tpu_custom_call" | custom-call | tf_op jit(solution)/shard_map/pallas_call | solution.py:211
  (1 shorter events, 0.0 us)
Async XLA Ops:
  58.0 42.6 %copy-start = (bf16[1,1,128,576]{2,3,1,0:T(8,128)(2,1)S(1)}, bf16[1,1,128,576]{2,3,1,0:T(8,128)(2,1)}, u32[]{:S(2)}) copy-start(bf16[1,1,128,576]{2,3,1,0:T(8,128)(2,1)} %param.14) | copy-start | bytes 442372
